TPU v7x, 32 devices: a whole 2x2x4 slice. The times are simulated.
32 devices in a mesh: sub: 8 (over z, x), blk: 4 (over y, core).
Axes of the slice: x: 2, y: 2, z: 4, core: 2. Of those that a mesh axis runs over, the one named last changes fastest.
Arguments:
- residual: float32 [32, 16384], P(None, ('sub', 'blk')), may hold values from -6 to 6
- fine_inverse: float32 [8, 2560, 2048], P('sub', None, 'blk'), may hold values from -1 to 1.1
- coarse_inverse: float32 [2048, 4, 512], P('sub', 'blk'), may hold values from -0.5 to 0.5, as said below
- wanted_rows: int32 [8, 2, 256], P('sub'), may hold values from 0 to 2047
- wanted_count: int32 [8, 2], P('sub'), may hold values from 32 to 256, as said below
- aggregate: int32 [16384], P(('sub', 'blk')), may hold values from 0 to 255
Outputs:
- preconditioned: float32 [32, 16384], P(None, ('sub', 'blk'))
Inputs may be any that keep to these rules, and one draw needn't show every extreme that they name: M of the steps is symmetric: coarse_inverse[i, b, s * 64 + q] equals coarse_inverse[s * 256 + b * 64 + q, b2, s2 * 64 + q2] where i = s2 * 256 + b2 * 64 + q2. `wanted_count`: counts vary from side to side; in every draw some subdomain other than the first and last takes exactly 256 rows from one side.
All inputs are finite; a program needn't handle non-finite values.
Results may differ from a plain program's by a relative error of at most 0.000052.
Values sent between devices are 32-bit elements; how exact they have to be, the bound alone decides.
No kernel may reach another device: no remote copies, remote signals or barrier semaphores. Data moves between devices by JAX's collectives and lax.ppermute only.
A program may use at most 64 MiB of HBM per device.

v0:
```python
import functools

import jax
import jax.numpy as jnp
from jax import lax
from jax.experimental import pallas as pl
from jax.experimental.pallas import tpu as pltpu
from jax.sharding import PartitionSpec as P

BF16 = jnp.bfloat16
F32 = jnp.float32
NN = (((1,), (0,)), ((), ()))
NT = (((1,), (1,)), ((), ()))
LANES = 128
MIB = 1 << 20


def split3(x):
    hi = x.astype(BF16)
    rest = x - hi.astype(F32)
    mid = rest.astype(BF16)
    low = (rest - mid.astype(F32)).astype(BF16)
    return jnp.concatenate([hi, mid, low], axis=0)


def split2(x):
    hi = x.astype(BF16)
    low = (x - hi.astype(F32)).astype(BF16)
    return hi, low


def dot(a, b, dims=NN):
    return lax.dot_general(a, b, dims, preferred_element_type=F32)


def dot_halves(x, w_hi, w_low):
    rows = x.shape[0]
    x_hi, x_low = split2(x)
    both = dot(jnp.concatenate([x_hi, x_low], axis=0), w_hi)
    return both[:rows] + both[rows:] + dot(x_hi, w_low)


def fold3(acc):
    rows = acc.shape[0] // 3
    return acc[:rows] + acc[rows : 2 * rows] + acc[2 * rows :]


def onehot(condition):
    return condition.astype(F32).astype(BF16)


def block_rows(ref, rows, first, count):
    return jnp.concatenate([ref[pl.ds((first + t) * rows, rows)] for t in range(count)], axis=1)


def block_shard(k):
    return lax.axis_index("blk") ^ k


def facing():
    return (lax.axis_index("sub") ^ lax.axis_index("blk")) & 1


def pack_kernel(
    residual_ref, agg_ref, lists_ref, counts_ref, coarse_ref,
    out_ref, lists_out, coarse_out,
    residual_buf, agg_buf, lists_buf, counts_buf, sems,
):
    sources = (residual_ref, agg_ref, lists_ref, counts_ref, coarse_ref)
    targets = (residual_buf, agg_buf, lists_buf, counts_buf, coarse_out)
    fetches = [pltpu.make_async_copy(a, b, sems.at[k]) for k, (a, b) in enumerate(zip(sources, targets))]
    for fetch in fetches:
        fetch.start()
    rows, cols = residual_buf.shape
    tiles = cols // LANES
    fetches[0].wait()
    for t in range(tiles):
        out_ref[t * rows : (t + 1) * rows] = residual_buf[:, t * LANES : (t + 1) * LANES]
    fetches[1].wait()
    codes = [agg_buf[:, t * LANES : (t + 1) * LANES].astype(F32) for t in range(tiles)]
    codes.append(jnp.zeros((out_ref.shape[0] - rows * tiles - tiles, LANES), F32))
    out_ref[rows * tiles :] = jnp.concatenate(codes, axis=0)
    fetches[2].wait()
    fetches[3].wait()
    slots = lax.broadcasted_iota(jnp.int32, (1, lists_buf.shape[1]), 1)
    for side in range(2):
        used = slots < counts_buf[:, side : side + 1]
        lists_out[side : side + 1] = jnp.where(used, lists_buf[side : side + 1], -1)
    fetches[4].wait()


def coarse_kernel(width, rows, tiles, *refs):
    blocks, coarse_ref, send_ref = refs[:-2], refs[-2], refs[-1]
    shards = len(blocks)
    cols = tiles * LANES
    coarse_len = width * shards
    levels = lax.broadcasted_iota(jnp.int32, (coarse_len, cols), 0)
    rhs = jnp.zeros((3 * rows, coarse_len), F32)
    for ref in blocks:
        codes = [ref[pl.ds(tiles * rows + t, 1)] for t in range(tiles)]
        unknowns = jnp.concatenate(codes, axis=1).astype(jnp.int32)
        rhs = rhs + dot(split3(block_rows(ref, rows, 0, tiles)), onehot(levels == unknowns), NT)
    rhs = fold3(rhs)
    half = rows // 2
    lane = lax.broadcasted_iota(jnp.int32, (half, LANES), 1)
    stride = coarse_ref.shape[0] // coarse_len
    for tile in range(0, stride, 2):
        parts = [coarse_ref[pl.ds(tile + k, coarse_len, stride=stride), :] for k in range(2)]
        value = dot_halves(rhs, *split2(jnp.concatenate(parts, axis=1)))
        for k in range(2):
            part = value[:, k * LANES : (k + 1) * LANES]
            turned = pltpu.roll(part, width, 1)
            left = jnp.where(lane < width, part[:half], turned[half:])
            right = jnp.where(lane < width, turned[:half], part[half:])
            for copy in range(shards):
                send_ref[2 * (tile + k), copy] = left
                send_ref[2 * (tile + k) + 1, copy] = right


def margin_kernel(rows, tiles, *refs):
    blocks, lists_ref, out_ref = refs[:-2], refs[-2], refs[-1]
    cols = tiles * LANES
    wanted = jnp.where(facing() == 1, lists_ref[1:2], lists_ref[0:1])
    local = lax.broadcasted_iota(jnp.int32, (cols, wanted.shape[1]), 0)
    total = jnp.zeros((3 * rows, wanted.shape[1]), F32)
    for k, ref in enumerate(blocks):
        chosen = onehot(local == wanted - block_shard(k) * cols)
        total = total + dot(split3(block_rows(ref, rows, 0, tiles)), chosen)
    out_ref[...] = fold3(total)


def own_kernel(rows, tiles, margin, shards, *refs):
    blocks = refs[:shards]
    agg_ref, fine_ref, out_ref, hi_ref, low_ref, hot_ref, agg_buf, fine_buf, sems = refs[shards:]
    ext = fine_ref.shape[1]
    step = 2 * LANES
    per_block = tiles * LANES // step
    starts = [
        pl.multiple_of(margin + block_shard(k) * (tiles * LANES) + part * step, step)
        for k in range(shards)
        for part in range(per_block)
    ]
    starts += [0, ext - margin]
    sizes = [step] * (len(starts) - 2) + [margin] * 2
    fetch = pltpu.make_async_copy(agg_ref, agg_buf, sems.at[len(starts)])
    fetch.start()
    copies = []
    for k, (start, size) in enumerate(zip(starts, sizes)):
        copies.append(
            pltpu.make_async_copy(
                fine_ref.at[0, pl.ds(start, size)], fine_buf.at[pl.ds(start, size)], sems.at[k]
            )
        )
        copies[k].start()
    fetch.wait()
    levels = lax.broadcasted_iota(jnp.int32, hot_ref.shape, 0)
    hot_ref[...] = onehot(levels == agg_buf[...])
    total = jnp.zeros(out_ref.shape, F32)
    for k, start in enumerate(starts[:-2]):
        block = block_rows(blocks[k // per_block], rows, 2 * (k % per_block), 2)
        copies[k].wait()
        total = total + dot_halves(block, *split2(fine_buf[pl.ds(start, step)]))
    out_ref[...] = total
    for side in range(2):
        start = starts[side - 2]
        copies[side - 2].wait()
        hi_ref[side], low_ref[side] = split2(fine_buf[start : start + margin])


def halo_kernel(mine_ref, other_ref, hi_ref, low_ref, total_ref, out_ref):
    mine, other = mine_ref[...], other_ref[...]
    first = facing() == 1
    total = total_ref[...]
    total = total + dot_halves(jnp.where(first, mine, other), hi_ref[0], low_ref[0])
    total = total + dot_halves(jnp.where(first, other, mine), hi_ref[1], low_ref[1])
    out_ref[...] = total


def tail_kernel(width, got_ref, hot_ref, total_ref, out_ref):
    subs, shards, half, _ = got_ref.shape
    sums = [got_ref[0, shard] for shard in range(shards)]
    for sub in range(1, subs):
        for shard in range(shards):
            sums[shard] = sums[shard] + got_ref[sub, shard]
    lane = lax.broadcasted_iota(jnp.int32, (half, LANES), 1)
    top, bottom = [], []
    for pair in range(shards // 2):
        left, right = sums[2 * pair], sums[2 * pair + 1]
        top.append(jnp.where(lane < width, left, pltpu.roll(right, width, 1)))
        bottom.append(jnp.where(lane < width, pltpu.roll(left, width, 1), right))
    coarse = jnp.concatenate([jnp.concatenate(top, axis=1), jnp.concatenate(bottom, axis=1)], axis=0)
    out_ref[...] = total_ref[...] + fold3(dot(split3(coarse), hot_ref[...]))


def whole(space=pltpu.VMEM):
    return pl.BlockSpec(memory_space=space)


def limit(mib):
    return pltpu.CompilerParams(vmem_limit_bytes=mib * MIB)


def in_hbm(x):
    return pltpu.with_memory_space_constraint(x, pltpu.HBM)


def weight(flops):
    return pl.CostEstimate(flops=flops, bytes_accessed=0, transcendentals=0)


def on_device(residual, fine_inverse, coarse_inverse, wanted_rows, wanted_count, aggregate):
    subs = lax.axis_size("sub")
    shards = lax.axis_size("blk")
    rows, cols = residual.shape
    tiles = cols // LANES
    margin = wanted_rows.shape[2]
    coarse_len = coarse_inverse.shape[0]
    width = coarse_len // shards
    packed_rows = -(-(rows * tiles + tiles) // 8) * 8
    core_swap = [(b, b ^ 1) for b in range(shards)]
    far_swap = [(b, b ^ 2) for b in range(shards)]
    neighbours = []
    for sub in range(subs):
        for b in range(shards):
            other = sub ^ 1 if b % 2 == 0 else (sub + 1 if sub % 2 else sub - 1)
            if 0 <= other < subs:
                neighbours.append((sub * shards + b, other * shards + b))
    codes = aggregate[None]
    lists = wanted_rows[0]
    table = coarse_inverse.reshape(-1, LANES)
    packed_shape = (packed_rows, LANES)

    packed, lists, table = pl.pallas_call(
        pack_kernel,
        out_shape=(
            jax.ShapeDtypeStruct(packed_shape, F32),
            jax.ShapeDtypeStruct(lists.shape, jnp.int32),
            jax.ShapeDtypeStruct(table.shape, F32),
        ),
        in_specs=[whole(pl.ANY)] * 5,
        out_specs=(whole(), whole(), whole()),
        scratch_shapes=[
            pltpu.VMEM(residual.shape, F32),
            pltpu.VMEM(codes.shape, jnp.int32),
            pltpu.VMEM(lists.shape, jnp.int32),
            pltpu.VMEM(wanted_count.shape, jnp.int32),
            pltpu.SemaphoreType.DMA((5,)),
        ],
        compiler_params=limit(4),
        name="pack",
    )(in_hbm(residual), in_hbm(codes), in_hbm(lists), in_hbm(wanted_count), in_hbm(table))
    lists = lax.ppermute(lists, ("sub", "blk"), neighbours)
    over_y = lax.ppermute(packed, "blk", far_swap)
    over_core = lax.ppermute(packed, "blk", core_swap)
    over_both = lax.ppermute(over_y, "blk", core_swap)
    blocks = (packed, over_core, over_y, over_both)

    send = pl.pallas_call(
        functools.partial(coarse_kernel, width, rows, tiles),
        out_shape=jax.ShapeDtypeStruct((subs, shards, rows // 2, LANES), F32),
        in_specs=[whole()] * (shards + 1),
        out_specs=whole(),
        compiler_params=limit(12),
        cost_estimate=weight(8 * 10**9),
        name="coarse",
    )(*blocks, table)
    flat = send.reshape((subs * shards,) + send.shape[2:])
    got = lax.all_to_all(flat, ("sub", "blk"), 0, 0, tiled=True).reshape(send.shape)

    outgoing = pl.pallas_call(
        functools.partial(margin_kernel, rows, tiles),
        out_shape=jax.ShapeDtypeStruct((rows, margin), F32),
        in_specs=[whole()] * (shards + 1),
        out_specs=whole(),
        compiler_params=limit(8),
        cost_estimate=weight(4 * 10**9),
        name="margins",
    )(*blocks, lists)
    halo = lax.ppermute(outgoing, ("sub", "blk"), neighbours)
    other_halo = lax.ppermute(halo, "blk", core_swap)

    owned, w_hi, w_low, hot = pl.pallas_call(
        functools.partial(own_kernel, rows, tiles, margin, shards),
        out_shape=(
            jax.ShapeDtypeStruct((rows, cols), F32),
            jax.ShapeDtypeStruct((2, margin, cols), BF16),
            jax.ShapeDtypeStruct((2, margin, cols), BF16),
            jax.ShapeDtypeStruct((coarse_len, cols), BF16),
        ),
        in_specs=[whole()] * shards + [whole(pl.ANY)] * 2,
        out_specs=(whole(),) * 4,
        scratch_shapes=[
            pltpu.VMEM(codes.shape, jnp.int32),
            pltpu.VMEM(fine_inverse.shape[1:], F32),
            pltpu.SemaphoreType.DMA((shards * tiles // 2 + 3,)),
        ],
        compiler_params=limit(16),
        cost_estimate=weight(40 * 10**9),
        name="owned",
    )(*blocks, in_hbm(codes), in_hbm(fine_inverse))

    fine = pl.pallas_call(
        halo_kernel,
        out_shape=jax.ShapeDtypeStruct((rows, cols), F32),
        in_specs=[whole()] * 5,
        out_specs=whole(),
        compiler_params=limit(12),
        cost_estimate=weight(4 * 10**9),
        name="halos",
    )(halo, other_halo, w_hi, w_low, owned)

    return pl.pallas_call(
        functools.partial(tail_kernel, width),
        out_shape=jax.ShapeDtypeStruct((rows, cols), F32),
        in_specs=[whole()] * 3,
        out_specs=whole(),
        compiler_params=limit(12),
        name="tail",
    )(got, hot, fine)


def solution(mesh):
    in_specs = (
        P(None, ("sub", "blk")),
        P("sub", None, "blk"),
        P("sub", "blk", None),
        P("sub", None, None),
        P("sub", None),
        P(("sub", "blk")),
    )
    out_specs = P(None, ("sub", "blk"))
    return jax.shard_map(
        on_device, mesh=mesh, in_specs=in_specs, out_specs=out_specs, check_vma=False
    )
```

profile of v0, /device:TPU:0, one launch (start us, length us, event | category | flops | bytes accessed | tf_op | source)
XLA Modules:
  0.0 34.1 jit_solution(9061281472414147361)
XLA Ops:
  0.0 1.2 %pack.1 = (f32[136,128]{1,0:T(8,128)S(1)}, s32[2,256]{1,0:T(2,128)S(1)}, f32[1024,128]{1,0:T(8,128)S(1)}) custom-call(f32[32,512]{1,0:T(8,128)} %residual_ref.1, s32[1,512]{1,0:T(1,128)} %bitcast.8, s32[2,256]{1,0:T(2,128)} %bitcast.7, s32[1,2]{1,0:T(1,128)} %counts_ref.1, f32[1024,128]{1,0:T(8,128)} %bitcast.6), custom_call_target="tpu_custom_call" | custom-call | tf_op jit(solution)/shard_map/pack/pallas_call | solution.py:233
  1.2 3.0 %collective-permute-start.1 = (f32[136,128]{1,0:T(8,128)S(1)}, f32[136,128]{1,0:T(8,128)S(1)}, u32[]{:S(2)}, u32[]{:S(2)}) collective-permute-start(f32[136,128]{1,0:T(8,128)S(1)} %get-tuple-element.12.refs_0_), channel_id=1, source_target_pairs={{0,2},{1,3},{2,0},{3,1},{4,6},{5,7},{6,4},{7,5},{8,10},{9,11},{10,... | collective-permute-start | bytes 208904 | tf_op jit(solution)/shard_map/ppermute | solution.py:253
  4.2 0.0 collective-permute-start
  4.2 2.3 %collective-permute-done.1.refs_2_ = f32[136,128]{1,0:T(8,128)S(1)} collective-permute-done((f32[136,128]{1,0:T(8,128)S(1)}, f32[136,128]{1,0:T(8,128)S(1)}, u32[]{:S(2)}, u32[]{:S(2)}) %collective-permute-start.1) | collective-permute-done | bytes 69664 | tf_op jit(solution)/shard_map/ppermute | solution.py:253
  6.5 0.0 collective-permute-start.2
  6.5 3.9 %collective-permute-start.3 = (s32[2,256]{1,0:T(2,128)S(1)}, s32[2,256]{1,0:T(2,128)S(1)}, u32[]{:S(2)}, u32[]{:S(2)}) collective-permute-start(s32[2,256]{1,0:T(2,128)S(1)} %get-tuple-element.15), channel_id=1, source_target_pairs={{0,4},{2,6},{4,0},{5,9},{6,2},{7,11},{8,12},{9,5},{10,14},{11,7},{... | collective-permute-start | bytes 6152 | tf_op jit(solution)/shard_map/ppermute | solution.py:252
  10.4 1.6 %collective-permute-done.3.refs_4_ = s32[2,256]{1,0:T(2,128)S(1)} collective-permute-done((s32[2,256]{1,0:T(2,128)S(1)}, s32[2,256]{1,0:T(2,128)S(1)}, u32[]{:S(2)}, u32[]{:S(2)}) %collective-permute-start.3) | collective-permute-done | bytes 2080 | tf_op jit(solution)/shard_map/ppermute | solution.py:252
  12.0 0.0 collective-permute-done.refs_1_
  12.0 0.0 collective-permute-done.2.refs_3_
  12.0 0.3 margins.1
  12.3 3.9 %collective-permute-start.4 = (f32[32,256]{1,0:T(8,128)S(1)}, f32[32,256]{1,0:T(8,128)S(1)}, u32[]{:S(2)}, u32[]{:S(2)}) collective-permute-start(f32[32,256]{1,0:T(8,128)S(1)} %margins.1), channel_id=1, source_target_pairs={{0,4},{2,6},{4,0},{5,9},{6,2},{7,11},{8,12},{9,5},{10,14},{11,7},{... | collective-permute-start | bytes 98312 | tf_op jit(solution)/shard_map/ppermute | solution.py:279
  16.2 1.5 %coarse.1 = f32[8,4,16,128]{3,2,1,0:T(8,128)} custom-call(f32[136,128]{1,0:T(8,128)S(1)} %get-tuple-element.12.refs_0_, f32[136,128]{1,0:T(8,128)S(1)} %collective-permute-done.refs_1_, f32[136,128]{1,0:T(8,128)S(1)} %collective-permute-done.1.refs_2_, f32[136,128]{1,0:T(8,128)S(1)} %collective-permute-done.2.refs_3_, f32[1024,128]{1,0:T(8,128)S(1)} %get-tuple-element.13.refs_4_), custom_call_target="tpu_custom_call" | custom-call | flops 8000000000 | tf_op jit(solution)/shard_map/coarse/pallas_call | solution.py:258
  17.8 4.9 %all-to-all-start = ((f32[32,16,128]{2,1,0:T(8,128)}), f32[32,16,128]{2,1,0:T(8,128)S(1)}, u32[]{:S(2)}, u32[]{:S(2)}) async-start(f32[32,16,128]{2,1,0:T(8,128)} %bitcast.3), calls=%async_computation | async-start | bytes 524288 | tf_op jit(solution)/shard_map/all_to_all | solution.py:268
  22.7 0.0 collective-permute-done.4.mine_ref
  22.7 0.3 collective-permute-start.5
  23.0 2.7 %owned.1 = (f32[32,512]{1,0:T(8,128)S(1)}, bf16[2,256,512]{2,1,0:T(8,128)(2,1)S(1)}, bf16[2,256,512]{2,1,0:T(8,128)(2,1)S(1)}, bf16[256,512]{1,0:T(8,128)(2,1)S(1)}) custom-call(f32[136,128]{1,0:T(8,128)S(1)} %get-tuple-element.12.refs_0_, f32[136,128]{1,0:T(8,128)S(1)} %collective-permute-done.refs_1_, f32[136,128]{1,0:T(8,128)S(1)} %collective-permute-done.1.refs_2_, ...), custom_call_target="tpu_custom_call" | custom-call | flops 40000000000 | tf_op jit(solution)/shard_map/owned/pallas_call | solution.py:282
  25.7 0.0 collective-permute-done.5.other_ref
  25.7 0.3 halos.1.total_ref
  26.0 7.3 %all-to-all-done = f32[32,16,128]{2,1,0:T(8,128)S(1)} async-done(((f32[32,16,128]{2,1,0:T(8,128)}), f32[32,16,128]{2,1,0:T(8,128)S(1)}, u32[]{:S(2)}, u32[]{:S(2)}) %all-to-all-start) | async-done | bytes 262176 | tf_op jit(solution)/shard_map/all_to_all | solution.py:268
  33.3 0.9 %tail.1 = f32[32,512]{1,0:T(8,128)} custom-call(f32[8,4,16,128]{3,2,1,0:T(8,128)S(1)} %bitcast.5, bf16[256,512]{1,0:T(8,128)(2,1)S(1)} %get-tuple-element.14.hot_ref, f32[32,512]{1,0:T(8,128)S(1)} %halos.1.total_ref), custom_call_target="tpu_custom_call" | custom-call | tf_op jit(solution)/shard_map/tail/pallas_call | solution.py:312
Async XLA Ops:
  1.2 5.3 %collective-permute-start.1 = (f32[136,128]{1,0:T(8,128)S(1)}, f32[136,128]{1,0:T(8,128)S(1)}, u32[]{:S(2)}, u32[]{:S(2)}) collective-permute-start(f32[136,128]{1,0:T(8,128)S(1)} %get-tuple-element.12.refs_0_), channel_id=1, source_target_pairs={{0,2},{1,3},{2,0},{3,1},{4,6},{5,7},{6,4},{7,5},{8,10},{9,11},{10,... | collective-permute-start | bytes 208904 | tf_op jit(solution)/shard_map/ppermute | solution.py:253
  4.2 7.8 %collective-permute-start = (f32[136,128]{1,0:T(8,128)S(1)}, f32[136,128]{1,0:T(8,128)S(1)}, u32[]{:S(2)}, u32[]{:S(2)}) collective-permute-start(f32[136,128]{1,0:T(8,128)S(1)} %get-tuple-element.12.refs_0_), channel_id=1, source_target_pairs={{0,1},{1,0},{2,3},{3,2},{4,5},{5,4},{6,7},{7,6},{8,9},{9,8},{10,11... | collective-permute-start | bytes 208904 | tf_op jit(solution)/shard_map/ppermute | solution.py:254
  6.5 5.5 %collective-permute-start.2 = (f32[136,128]{1,0:T(8,128)S(1)}, f32[136,128]{1,0:T(8,128)S(1)}, u32[]{:S(2)}, u32[]{:S(2)}) collective-permute-start(f32[136,128]{1,0:T(8,128)S(1)} %collective-permute-done.1.refs_2_), channel_id=1, source_target_pairs={{0,1},{1,0},{2,3},{3,2},{4,5},{5,4},{6,7},{7,6},{8,9},{9,8},{10,11... | collective-permute-start | bytes 208904 | tf_op jit(solution)/shard_map/ppermute | solution.py:255
  6.5 5.5 %collective-permute-start.3 = (s32[2,256]{1,0:T(2,128)S(1)}, s32[2,256]{1,0:T(2,128)S(1)}, u32[]{:S(2)}, u32[]{:S(2)}) collective-permute-start(s32[2,256]{1,0:T(2,128)S(1)} %get-tuple-element.15), channel_id=1, source_target_pairs={{0,4},{2,6},{4,0},{5,9},{6,2},{7,11},{8,12},{9,5},{10,14},{11,7},{... | collective-permute-start | bytes 6152 | tf_op jit(solution)/shard_map/ppermute | solution.py:252
  12.3 10.4 %collective-permute-start.4 = (f32[32,256]{1,0:T(8,128)S(1)}, f32[32,256]{1,0:T(8,128)S(1)}, u32[]{:S(2)}, u32[]{:S(2)}) collective-permute-start(f32[32,256]{1,0:T(8,128)S(1)} %margins.1), channel_id=1, source_target_pairs={{0,4},{2,6},{4,0},{5,9},{6,2},{7,11},{8,12},{9,5},{10,14},{11,7},{... | collective-permute-start | bytes 98312 | tf_op jit(solution)/shard_map/ppermute | solution.py:279
  17.8 15.5 %all-to-all-start = ((f32[32,16,128]{2,1,0:T(8,128)}), f32[32,16,128]{2,1,0:T(8,128)S(1)}, u32[]{:S(2)}, u32[]{:S(2)}) async-start(f32[32,16,128]{2,1,0:T(8,128)} %bitcast.3), calls=%async_computation | async-start | bytes 524288 | tf_op jit(solution)/shard_map/all_to_all | solution.py:268
  22.7 3.0 %collective-permute-start.5 = (f32[32,256]{1,0:T(8,128)S(1)}, f32[32,256]{1,0:T(8,128)S(1)}, u32[]{:S(2)}, u32[]{:S(2)}) collective-permute-start(f32[32,256]{1,0:T(8,128)S(1)} %collective-permute-done.4.mine_ref), channel_id=1, source_target_pairs={{0,1},{1,0},{2,3},{3,2},{4,5},{5,4},{6,7},{7,6},{8,9},{9,8},{10,11... | collective-permute-start | bytes 98312 | tf_op jit(solution)/shard_map/ppermute | solution.py:280
where the time goes:
time: 34.4 us; the launch traced here: 34.1 us
  starting transfers between devices  16.1 us (47%)
  waiting for transfers between devices  11.2 us (33%)
  Pallas kernels  6.81 us (20%)
    all_to_all x1, waiting for transfers between devices, on_device(): lax.all_to_all(flat, ('sub', 'blk'), 0, 0, tiled=True).reshape(send.shape)  7.32 us
    all_to_all x1, starting transfers between devices, on_device(): lax.all_to_all(flat, ('sub', 'blk'), 0, 0, tiled=True).reshape(send.shape)  4.92 us
    ppermute x1, starting transfers between devices, on_device(): halo = lax.ppermute(outgoing, ('sub', 'blk'), neighbours)  3.92 us
    ppermute x1, starting transfers between devices, on_device(): lists = lax.ppermute(lists, ('sub', 'blk'), neighbours)  3.89 us
    ppermute x1, starting transfers between devices, on_device(): over_y = lax.ppermute(packed, 'blk', far_swap)  3.03 us
    pallas_call x1, Pallas kernels, on_device(): pl.pallas_call(functools.partial(own_kernel, rows, tiles, margin, shards)...  2.66 us
    ppermute x1, waiting for transfers between devices, on_device(): over_y = lax.ppermute(packed, 'blk', far_swap)  2.29 us
    ppermute x1, waiting for transfers between devices, on_device(): lists = lax.ppermute(lists, ('sub', 'blk'), neighbours)  1.57 us
  transfers between devices with their start and end apart: 7, of which 3 were waited for; matrix products, arithmetic and copies ran while one was open for 0% of the time, Pallas kernels for 13%

commit v1 on v0

--- a/solution.py
+++ b/solution.py
@@ -89,17 +89,18 @@
     fetches[4].wait()
 
 
-def coarse_kernel(width, rows, tiles, *refs):
-    blocks, coarse_ref, send_ref = refs[:-2], refs[-2], refs[-1]
-    shards = len(blocks)
+def coarse_kernel(width, rows, tiles, shards, *refs):
+    blocks, (coarse_ref, send_ref, parts_ref) = refs[:shards], refs[shards:]
     cols = tiles * LANES
     coarse_len = width * shards
     levels = lax.broadcasted_iota(jnp.int32, (coarse_len, cols), 0)
     rhs = jnp.zeros((3 * rows, coarse_len), F32)
-    for ref in blocks:
+    for k, ref in enumerate(blocks):
         codes = [ref[pl.ds(tiles * rows + t, 1)] for t in range(tiles)]
         unknowns = jnp.concatenate(codes, axis=1).astype(jnp.int32)
-        rhs = rhs + dot(split3(block_rows(ref, rows, 0, tiles)), onehot(levels == unknowns), NT)
+        parts = split3(block_rows(ref, rows, 0, tiles))
+        parts_ref[k] = parts
+        rhs = rhs + dot(parts, onehot(levels == unknowns), NT)
     rhs = fold3(rhs)
     half = rows // 2
     lane = lax.broadcasted_iota(jnp.int32, (half, LANES), 1)
@@ -117,21 +118,22 @@
                 send_ref[2 * (tile + k) + 1, copy] = right
 
 
-def margin_kernel(rows, tiles, *refs):
-    blocks, lists_ref, out_ref = refs[:-2], refs[-2], refs[-1]
-    cols = tiles * LANES
+def margin_kernel(parts_ref, lists_ref, out_ref):
+    shards, rows, cols = parts_ref.shape
     wanted = jnp.where(facing() == 1, lists_ref[1:2], lists_ref[0:1])
     local = lax.broadcasted_iota(jnp.int32, (cols, wanted.shape[1]), 0)
-    total = jnp.zeros((3 * rows, wanted.shape[1]), F32)
-    for k, ref in enumerate(blocks):
-        chosen = onehot(local == wanted - block_shard(k) * cols)
-        total = total + dot(split3(block_rows(ref, rows, 0, tiles)), chosen)
+    total = jnp.zeros((rows, wanted.shape[1]), F32)
+    for k in range(shards):
+        total = total + dot(parts_ref[k], onehot(local == wanted - block_shard(k) * cols))
     out_ref[...] = fold3(total)
 
 
-def own_kernel(rows, tiles, margin, shards, *refs):
-    blocks = refs[:shards]
-    agg_ref, fine_ref, out_ref, hi_ref, low_ref, hot_ref, agg_buf, fine_buf, sems = refs[shards:]
+def own_kernel(
+    margin, parts_ref, agg_ref, fine_ref, out_ref, hi_ref, low_ref, hot_ref, agg_buf, fine_buf, sems
+):
+    shards, rows, cols = parts_ref.shape
+    rows = rows // 3
+    tiles = cols // LANES
     ext = fine_ref.shape[1]
     step = 2 * LANES
     per_block = tiles * LANES // step
@@ -157,9 +159,12 @@
     hot_ref[...] = onehot(levels == agg_buf[...])
     total = jnp.zeros(out_ref.shape, F32)
     for k, start in enumerate(starts[:-2]):
-        block = block_rows(blocks[k // per_block], rows, 2 * (k % per_block), 2)
+        part = k % per_block
+        block = parts_ref[k // per_block, :, part * step : (part + 1) * step]
         copies[k].wait()
-        total = total + dot_halves(block, *split2(fine_buf[pl.ds(start, step)]))
+        w_hi, w_low = split2(fine_buf[pl.ds(start, step)])
+        both = dot(block[: 2 * rows], w_hi)
+        total = total + (both[:rows] + both[rows:] + dot(block[:rows], w_low))
     out_ref[...] = total
     for side in range(2):
         start = starts[side - 2]
@@ -167,13 +172,16 @@
         hi_ref[side], low_ref[side] = split2(fine_buf[start : start + margin])
 
 
-def halo_kernel(mine_ref, other_ref, hi_ref, low_ref, total_ref, out_ref):
-    mine, other = mine_ref[...], other_ref[...]
-    first = facing() == 1
-    total = total_ref[...]
-    total = total + dot_halves(jnp.where(first, mine, other), hi_ref[0], low_ref[0])
-    total = total + dot_halves(jnp.where(first, other, mine), hi_ref[1], low_ref[1])
-    out_ref[...] = total
+def mine_kernel(halo_ref, hi_ref, low_ref, total_ref, out_ref, copy_ref):
+    halo = halo_ref[...]
+    copy_ref[...] = halo
+    side = 1 - facing()
+    out_ref[...] = total_ref[...] + dot_halves(halo, hi_ref[side], low_ref[side])
+
+
+def other_kernel(halo_ref, hi_ref, low_ref, total_ref, out_ref):
+    side = facing()
+    out_ref[...] = total_ref[...] + dot_halves(halo_ref[...], hi_ref[side], low_ref[side])
 
 
 def tail_kernel(width, got_ref, hot_ref, total_ref, out_ref):
@@ -219,6 +227,7 @@
     packed_rows = -(-(rows * tiles + tiles) // 8) * 8
     core_swap = [(b, b ^ 1) for b in range(shards)]
     far_swap = [(b, b ^ 2) for b in range(shards)]
+    both_swap = [(b, b ^ 3) for b in range(shards)]
     neighbours = []
     for sub in range(subs):
         for b in range(shards):
@@ -252,14 +261,17 @@
     lists = lax.ppermute(lists, ("sub", "blk"), neighbours)
     over_y = lax.ppermute(packed, "blk", far_swap)
     over_core = lax.ppermute(packed, "blk", core_swap)
-    over_both = lax.ppermute(over_y, "blk", core_swap)
+    over_both = lax.ppermute(packed, "blk", both_swap)
     blocks = (packed, over_core, over_y, over_both)
 
-    send = pl.pallas_call(
-        functools.partial(coarse_kernel, width, rows, tiles),
-        out_shape=jax.ShapeDtypeStruct((subs, shards, rows // 2, LANES), F32),
+    send, parts = pl.pallas_call(
+        functools.partial(coarse_kernel, width, rows, tiles, shards),
+        out_shape=(
+            jax.ShapeDtypeStruct((subs, shards, rows // 2, LANES), F32),
+            jax.ShapeDtypeStruct((shards, 3 * rows, cols), BF16),
+        ),
         in_specs=[whole()] * (shards + 1),
-        out_specs=whole(),
+        out_specs=(whole(), whole()),
         compiler_params=limit(12),
         cost_estimate=weight(8 * 10**9),
         name="coarse",
@@ -268,26 +280,25 @@
     got = lax.all_to_all(flat, ("sub", "blk"), 0, 0, tiled=True).reshape(send.shape)
 
     outgoing = pl.pallas_call(
-        functools.partial(margin_kernel, rows, tiles),
+        margin_kernel,
         out_shape=jax.ShapeDtypeStruct((rows, margin), F32),
-        in_specs=[whole()] * (shards + 1),
+        in_specs=[whole()] * 2,
         out_specs=whole(),
         compiler_params=limit(8),
         cost_estimate=weight(4 * 10**9),
         name="margins",
-    )(*blocks, lists)
+    )(parts, lists)
     halo = lax.ppermute(outgoing, ("sub", "blk"), neighbours)
-    other_halo = lax.ppermute(halo, "blk", core_swap)
 
     owned, w_hi, w_low, hot = pl.pallas_call(
-        functools.partial(own_kernel, rows, tiles, margin, shards),
+        functools.partial(own_kernel, margin),
         out_shape=(
             jax.ShapeDtypeStruct((rows, cols), F32),
             jax.ShapeDtypeStruct((2, margin, cols), BF16),
             jax.ShapeDtypeStruct((2, margin, cols), BF16),
             jax.ShapeDtypeStruct((coarse_len, cols), BF16),
         ),
-        in_specs=[whole()] * shards + [whole(pl.ANY)] * 2,
+        in_specs=[whole(), whole(pl.ANY), whole(pl.ANY)],
         out_specs=(whole(),) * 4,
         scratch_shapes=[
             pltpu.VMEM(codes.shape, jnp.int32),
@@ -297,17 +308,30 @@
         compiler_params=limit(16),
         cost_estimate=weight(40 * 10**9),
         name="owned",
-    )(*blocks, in_hbm(codes), in_hbm(fine_inverse))
-
+    )(parts, in_hbm(codes), in_hbm(fine_inverse))
+
+    fine, mine = pl.pallas_call(
+        mine_kernel,
+        out_shape=(
+            jax.ShapeDtypeStruct((rows, cols), F32),
+            jax.ShapeDtypeStruct(halo.shape, F32),
+        ),
+        in_specs=[whole()] * 4,
+        out_specs=(whole(), whole()),
+        compiler_params=limit(12),
+        cost_estimate=weight(4 * 10**9),
+        name="mine",
+    )(halo, w_hi, w_low, owned)
+    other = lax.ppermute(mine, "blk", core_swap)
     fine = pl.pallas_call(
-        halo_kernel,
+        other_kernel,
         out_shape=jax.ShapeDtypeStruct((rows, cols), F32),
-        in_specs=[whole()] * 5,
+        in_specs=[whole()] * 4,
         out_specs=whole(),
         compiler_params=limit(12),
-        cost_estimate=weight(4 * 10**9),
-        name="halos",
-    )(halo, other_halo, w_hi, w_low, owned)
+        cost_estimate=weight(10**9),
+        name="other",
+    )(other, w_hi, w_low, fine)
 
     return pl.pallas_call(
         functools.partial(tail_kernel, width),

time: 34.4 us -> 27.8 us (0.81)
  waiting for transfers between devices: 11.2 us -> 3.96 us
  starting transfers between devices: 16.1 us -> 16.6 us
    all_to_all x1, waiting for transfers between devices: 7.32 us -> 2.29 us  [on_device(): lax.all_to_all(flat, ('sub', 'blk'), 0, 0, tiled=True).reshape(send.shape)]
    ppermute x1, starting transfers between devices: 3.03 us -> 0.64 us  [on_device(): over_y = lax.ppermute(packed, 'blk', far_swap)]
    ppermute x2, starting transfers between devices: 0.32 us -> 2.49 us  [the longest x1 2.47 us: on_device(): over_both = lax.ppermute(packed, 'blk', both_swap)]
    ppermute x1, waiting for transfers between devices: 2.29 us -> 0.45 us  [on_device(): over_y = lax.ppermute(packed, 'blk', far_swap)]
    ppermute x1, waiting for transfers between devices: 1.57 us -> 0.01 us  [on_device(): lists = lax.ppermute(lists, ('sub', 'blk'), neighbours)]
    ppermute x2, waiting for transfers between devices: 0.01 us -> 1.21 us  [the longest x1 1.2 us: on_device(): other = lax.ppermute(mine, 'blk', core_swap)]
    all_to_all x1, starting transfers between devices: 4.92 us -> 6.1 us  [on_device(): lax.all_to_all(flat, ('sub', 'blk'), 0, 0, tiled=True).reshape(send.shape)]
    pallas_call x4 -> x5, Pallas kernels: 4.78 us -> 4.88 us  [the longest x1 2.67 us: on_device(): pl.pallas_call(functools.partial(own_kernel, margin), out_shape=(jax.Shap...]
  transfers between devices with their start and end apart: 7 -> 7, of which waited for: 3 -> 3; matrix products, arithmetic and copies ran while one was open for 0% -> 0% of each run, Pallas kernels for 13% -> 18%
where the time goes in v1:
time: 27.8 us; the launch traced here: 27.5 us
  starting transfers between devices  16.6 us (60%)
  Pallas kernels  6.91 us (25%)
  waiting for transfers between devices  3.96 us (14%)
    all_to_all x1, starting transfers between devices, on_device(): lax.all_to_all(flat, ('sub', 'blk'), 0, 0, tiled=True).reshape(send.shape)  6.1 us
    ppermute x1, starting transfers between devices, on_device(): halo = lax.ppermute(outgoing, ('sub', 'blk'), neighbours)  3.69 us
    ppermute x1, starting transfers between devices, on_device(): lists = lax.ppermute(lists, ('sub', 'blk'), neighbours)  3.61 us
    pallas_call x1, Pallas kernels, on_device(): pl.pallas_call(functools.partial(own_kernel, margin), out_shape=(jax.Shap...  2.67 us
    ppermute x1, starting transfers between devices, on_device(): over_both = lax.ppermute(packed, 'blk', both_swap)  2.47 us
    all_to_all x1, waiting for transfers between devices, on_device(): lax.all_to_all(flat, ('sub', 'blk'), 0, 0, tiled=True).reshape(send.shape)  2.29 us
    pallas_call x1, Pallas kernels, on_device(): pl.pallas_call(functools.partial(coarse_kernel, width, rows, tiles, shard...  1.53 us
    ppermute x1, waiting for transfers between devices, on_device(): other = lax.ppermute(mine, 'blk', core_swap)  1.2 us
  transfers between devices with their start and end apart: 7, of which 3 were waited for; matrix products, arithmetic and copies ran while one was open for 0% of the time, Pallas kernels for 18%

profile of v1, /device:TPU:0, one launch (start us, length us, event | category | flops | bytes accessed | tf_op | source)
XLA Modules:
  0.0 27.5 jit_solution(5331390275811508046)
XLA Ops:
  0.0 1.2 %pack.1 = (f32[136,128]{1,0:T(8,128)S(1)}, s32[2,256]{1,0:T(2,128)S(1)}, f32[1024,128]{1,0:T(8,128)S(1)}) custom-call(f32[32,512]{1,0:T(8,128)} %residual_ref.1, s32[1,512]{1,0:T(1,128)} %bitcast.8, s32[2,256]{1,0:T(2,128)} %bitcast.7, s32[1,2]{1,0:T(1,128)} %counts_ref.1, f32[1024,128]{1,0:T(8,128)} %bitcast.6), custom_call_target="tpu_custom_call" | custom-call | tf_op jit(solution)/shard_map/pack/pallas_call | solution.py:242
  1.2 2.5 %collective-permute-start.2 = (f32[136,128]{1,0:T(8,128)S(1)}, f32[136,128]{1,0:T(8,128)S(1)}, u32[]{:S(2)}, u32[]{:S(2)}) collective-permute-start(f32[136,128]{1,0:T(8,128)S(1)} %get-tuple-element.16.refs_0_), channel_id=1, source_target_pairs={{0,3},{1,2},{2,1},{3,0},{4,7},{5,6},{6,5},{7,4},{8,11},{9,10},{10,... | collective-permute-start | bytes 208904 | tf_op jit(solution)/shard_map/ppermute | solution.py:264
  3.7 0.6 %collective-permute-start.1 = (f32[136,128]{1,0:T(8,128)S(1)}, f32[136,128]{1,0:T(8,128)S(1)}, u32[]{:S(2)}, u32[]{:S(2)}) collective-permute-start(f32[136,128]{1,0:T(8,128)S(1)} %get-tuple-element.16.refs_0_), channel_id=1, source_target_pairs={{0,2},{1,3},{2,0},{3,1},{4,6},{5,7},{6,4},{7,5},{8,10},{9,11},{10,... | collective-permute-start | bytes 208904 | tf_op jit(solution)/shard_map/ppermute | solution.py:262
  4.3 0.0 collective-permute-start
  4.3 3.6 %collective-permute-start.3 = (s32[2,256]{1,0:T(2,128)S(1)}, s32[2,256]{1,0:T(2,128)S(1)}, u32[]{:S(2)}, u32[]{:S(2)}) collective-permute-start(s32[2,256]{1,0:T(2,128)S(1)} %get-tuple-element.21), channel_id=1, source_target_pairs={{0,4},{2,6},{4,0},{5,9},{6,2},{7,11},{8,12},{9,5},{10,14},{11,7},{... | collective-permute-start | bytes 6152 | tf_op jit(solution)/shard_map/ppermute | solution.py:261
  8.0 0.0 collective-permute-done.2.refs_3_
  8.0 0.5 %collective-permute-done.1.refs_2_ = f32[136,128]{1,0:T(8,128)S(1)} collective-permute-done((f32[136,128]{1,0:T(8,128)S(1)}, f32[136,128]{1,0:T(8,128)S(1)}, u32[]{:S(2)}, u32[]{:S(2)}) %collective-permute-start.1) | collective-permute-done | bytes 69664 | tf_op jit(solution)/shard_map/ppermute | solution.py:262
  8.4 0.0 collective-permute-done.refs_1_
  8.4 1.5 %coarse.1 = (f32[8,4,16,128]{3,2,1,0:T(8,128)}, bf16[4,96,512]{2,1,0:T(8,128)(2,1)S(1)}) custom-call(f32[136,128]{1,0:T(8,128)S(1)} %get-tuple-element.16.refs_0_, f32[136,128]{1,0:T(8,128)S(1)} %collective-permute-done.refs_1_, f32[136,128]{1,0:T(8,128)S(1)} %collective-permute-done.1.refs_2_, f32[136,128]{1,0:T(8,128)S(1)} %collective-permute-done.2.refs_3_, ...), custom_call_target="tpu_custom_call" | custom-call | flops 8000000000 | tf_op jit(solution)/shard_map/coarse/pallas_call | solution.py:267
  9.9 6.1 %all-to-all-start = ((f32[32,16,128]{2,1,0:T(8,128)}), f32[32,16,128]{2,1,0:T(8,128)S(1)}, u32[]{:S(2)}, u32[]{:S(2)}) async-start(f32[32,16,128]{2,1,0:T(8,128)} %bitcast.3), calls=%async_computation | async-start | bytes 524288 | tf_op jit(solution)/shard_map/all_to_all | solution.py:280
  16.1 0.0 collective-permute-done.3.lists_ref
  16.1 0.3 %margins.1 = f32[32,256]{1,0:T(8,128)S(1)} custom-call(bf16[4,96,512]{2,1,0:T(8,128)(2,1)S(1)} %get-tuple-element.19.parts_ref, s32[2,256]{1,0:T(2,128)S(1)} %collective-permute-done.3.lists_ref), custom_call_target="tpu_custom_call" | custom-call | flops 4000000000 | tf_op jit(solution)/shard_map/margins/pallas_call | solution.py:282
  16.4 3.7 %collective-permute-start.4 = (f32[32,256]{1,0:T(8,128)S(1)}, f32[32,256]{1,0:T(8,128)S(1)}, u32[]{:S(2)}, u32[]{:S(2)}) collective-permute-start(f32[32,256]{1,0:T(8,128)S(1)} %margins.1), channel_id=1, source_target_pairs={{0,4},{2,6},{4,0},{5,9},{6,2},{7,11},{8,12},{9,5},{10,14},{11,7},{... | collective-permute-start | bytes 98312 | tf_op jit(solution)/shard_map/ppermute | solution.py:291
  20.1 2.7 %owned.1 = (f32[32,512]{1,0:T(8,128)S(1)}, bf16[2,256,512]{2,1,0:T(8,128)(2,1)S(1)}, bf16[2,256,512]{2,1,0:T(8,128)(2,1)S(1)}, bf16[256,512]{1,0:T(8,128)(2,1)S(1)}) custom-call(bf16[4,96,512]{2,1,0:T(8,128)(2,1)S(1)} %get-tuple-element.19.parts_ref, s32[1,512]{1,0:T(1,128)} %bitcast.9, f32[1,2560,512]{2,1,0:T(8,128)} %fine_ref.1), custom_call_target="tpu_custom_call" | custom-call | flops 40000000000 | tf_op jit(solution)/shard_map/owned/pallas_call | solution.py:293
  22.7 0.0 collective-permute-done.4.halo_ref
  22.8 0.2 mine.1
  22.9 0.0 collective-permute-start.5
  23.0 1.2 %collective-permute-done.5.halo_ref = f32[32,256]{1,0:T(8,128)S(1)} collective-permute-done((f32[32,256]{1,0:T(8,128)S(1)}, f32[32,256]{1,0:T(8,128)S(1)}, u32[]{:S(2)}, u32[]{:S(2)}) %collective-permute-start.5) | collective-permute-done | bytes 32800 | tf_op jit(solution)/shard_map/ppermute | solution.py:325
  24.2 0.2 other.1.total_ref
  24.4 2.3 %all-to-all-done = f32[32,16,128]{2,1,0:T(8,128)S(1)} async-done(((f32[32,16,128]{2,1,0:T(8,128)}), f32[32,16,128]{2,1,0:T(8,128)S(1)}, u32[]{:S(2)}, u32[]{:S(2)}) %all-to-all-start) | async-done | bytes 262176 | tf_op jit(solution)/shard_map/all_to_all | solution.py:280
  26.7 0.9 %tail.1 = f32[32,512]{1,0:T(8,128)} custom-call(f32[8,4,16,128]{3,2,1,0:T(8,128)S(1)} %bitcast.5, bf16[256,512]{1,0:T(8,128)(2,1)S(1)} %get-tuple-element.20.hot_ref, f32[32,512]{1,0:T(8,128)S(1)} %other.1.total_ref), custom_call_target="tpu_custom_call" | custom-call | tf_op jit(solution)/shard_map/tail/pallas_call | solution.py:336
Async XLA Ops:
  1.2 6.8 %collective-permute-start.2 = (f32[136,128]{1,0:T(8,128)S(1)}, f32[136,128]{1,0:T(8,128)S(1)}, u32[]{:S(2)}, u32[]{:S(2)}) collective-permute-start(f32[136,128]{1,0:T(8,128)S(1)} %get-tuple-element.16.refs_0_), channel_id=1, source_target_pairs={{0,3},{1,2},{2,1},{3,0},{4,7},{5,6},{6,5},{7,4},{8,11},{9,10},{10,... | collective-permute-start | bytes 208904 | tf_op jit(solution)/shard_map/ppermute | solution.py:264
  3.7 4.8 %collective-permute-start.1 = (f32[136,128]{1,0:T(8,128)S(1)}, f32[136,128]{1,0:T(8,128)S(1)}, u32[]{:S(2)}, u32[]{:S(2)}) collective-permute-start(f32[136,128]{1,0:T(8,128)S(1)} %get-tuple-element.16.refs_0_), channel_id=1, source_target_pairs={{0,2},{1,3},{2,0},{3,1},{4,6},{5,7},{6,4},{7,5},{8,10},{9,11},{10,... | collective-permute-start | bytes 208904 | tf_op jit(solution)/shard_map/ppermute | solution.py:262
  4.3 4.1 %collective-permute-start = (f32[136,128]{1,0:T(8,128)S(1)}, f32[136,128]{1,0:T(8,128)S(1)}, u32[]{:S(2)}, u32[]{:S(2)}) collective-permute-start(f32[136,128]{1,0:T(8,128)S(1)} %get-tuple-element.16.refs_0_), channel_id=1, source_target_pairs={{0,1},{1,0},{2,3},{3,2},{4,5},{5,4},{6,7},{7,6},{8,9},{9,8},{10,11... | collective-permute-start | bytes 208904 | tf_op jit(solution)/shard_map/ppermute | solution.py:263
  4.3 11.7 %collective-permute-start.3 = (s32[2,256]{1,0:T(2,128)S(1)}, s32[2,256]{1,0:T(2,128)S(1)}, u32[]{:S(2)}, u32[]{:S(2)}) collective-permute-start(s32[2,256]{1,0:T(2,128)S(1)} %get-tuple-element.21), channel_id=1, source_target_pairs={{0,4},{2,6},{4,0},{5,9},{6,2},{7,11},{8,12},{9,5},{10,14},{11,7},{... | collective-permute-start | bytes 6152 | tf_op jit(solution)/shard_map/ppermute | solution.py:261
  9.9 16.7 %all-to-all-start = ((f32[32,16,128]{2,1,0:T(8,128)}), f32[32,16,128]{2,1,0:T(8,128)S(1)}, u32[]{:S(2)}, u32[]{:S(2)}) async-start(f32[32,16,128]{2,1,0:T(8,128)} %bitcast.3), calls=%async_computation | async-start | bytes 524288 | tf_op jit(solution)/shard_map/all_to_all | solution.py:280
  16.4 6.4 %collective-permute-start.4 = (f32[32,256]{1,0:T(8,128)S(1)}, f32[32,256]{1,0:T(8,128)S(1)}, u32[]{:S(2)}, u32[]{:S(2)}) collective-permute-start(f32[32,256]{1,0:T(8,128)S(1)} %margins.1), channel_id=1, source_target_pairs={{0,4},{2,6},{4,0},{5,9},{6,2},{7,11},{8,12},{9,5},{10,14},{11,7},{... | collective-permute-start | bytes 98312 | tf_op jit(solution)/shard_map/ppermute | solution.py:291
  22.9 1.2 %collective-permute-start.5 = (f32[32,256]{1,0:T(8,128)S(1)}, f32[32,256]{1,0:T(8,128)S(1)}, u32[]{:S(2)}, u32[]{:S(2)}) collective-permute-start(f32[32,256]{1,0:T(8,128)S(1)} %get-tuple-element.25), channel_id=1, source_target_pairs={{0,1},{1,0},{2,3},{3,2},{4,5},{5,4},{6,7},{7,6},{8,9},{9,8},{10,11... | collective-permute-start | bytes 98312 | tf_op jit(solution)/shard_map/ppermute | solution.py:325

commit v2 on v1

--- a/solution.py
+++ b/solution.py
@@ -90,8 +90,15 @@
 
 
 def coarse_kernel(width, rows, tiles, shards, *refs):
-    blocks, (coarse_ref, send_ref, parts_ref) = refs[:shards], refs[shards:]
+    blocks = refs[:shards]
+    coarse_ref, fine_ref, send_ref, parts_ref, early_ref, sems = refs[shards:]
     cols = tiles * LANES
+    margin = (fine_ref.shape[1] - shards * cols) // 2
+    fetches = []
+    for k in range(early_ref.shape[0]):
+        rows_at = pl.ds(pl.multiple_of(margin + block_shard(k) * cols, LANES), cols)
+        fetches.append(pltpu.make_async_copy(fine_ref.at[0, rows_at], early_ref.at[k], sems.at[k]))
+        fetches[k].start()
     coarse_len = width * shards
     levels = lax.broadcasted_iota(jnp.int32, (coarse_len, cols), 0)
     rhs = jnp.zeros((3 * rows, coarse_len), F32)
@@ -113,9 +120,11 @@
             turned = pltpu.roll(part, width, 1)
             left = jnp.where(lane < width, part[:half], turned[half:])
             right = jnp.where(lane < width, turned[:half], part[half:])
-            for copy in range(shards):
+            for copy in range(send_ref.shape[1]):
                 send_ref[2 * (tile + k), copy] = left
                 send_ref[2 * (tile + k) + 1, copy] = right
+    for fetch in fetches:
+        fetch.wait()
 
 
 def margin_kernel(parts_ref, lists_ref, out_ref):
@@ -129,47 +138,52 @@
 
 
 def own_kernel(
-    margin, parts_ref, agg_ref, fine_ref, out_ref, hi_ref, low_ref, hot_ref, agg_buf, fine_buf, sems
+    margin, parts_ref, early_ref, agg_ref, fine_ref, out_ref, hi_ref, low_ref, hot_ref, agg_buf, fine_buf, sems
 ):
     shards, rows, cols = parts_ref.shape
     rows = rows // 3
-    tiles = cols // LANES
     ext = fine_ref.shape[1]
+    early = early_ref.shape[0]
     step = 2 * LANES
-    per_block = tiles * LANES // step
+    halves = cols // step
     starts = [
-        pl.multiple_of(margin + block_shard(k) * (tiles * LANES) + part * step, step)
-        for k in range(shards)
-        for part in range(per_block)
+        pl.multiple_of(margin + block_shard(k) * cols + part * step, step)
+        for k in range(early, shards)
+        for part in range(halves)
     ]
     starts += [0, ext - margin]
     sizes = [step] * (len(starts) - 2) + [margin] * 2
     fetch = pltpu.make_async_copy(agg_ref, agg_buf, sems.at[len(starts)])
     fetch.start()
     copies = []
+    at = 0
     for k, (start, size) in enumerate(zip(starts, sizes)):
         copies.append(
-            pltpu.make_async_copy(
-                fine_ref.at[0, pl.ds(start, size)], fine_buf.at[pl.ds(start, size)], sems.at[k]
-            )
+            pltpu.make_async_copy(fine_ref.at[0, pl.ds(start, size)], fine_buf.at[pl.ds(at, size)], sems.at[k])
         )
         copies[k].start()
+        at += size
+    total = jnp.zeros(out_ref.shape, F32)
+    for k in range(shards):
+        for part in range(halves):
+            block = parts_ref[k, :, part * step : (part + 1) * step]
+            if k < early:
+                weights = early_ref[k, part * step : (part + 1) * step]
+            else:
+                piece = (k - early) * halves + part
+                copies[piece].wait()
+                weights = fine_buf[piece * step : (piece + 1) * step]
+            w_hi, w_low = split2(weights)
+            both = dot(block[: 2 * rows], w_hi)
+            total = total + (both[:rows] + both[rows:] + dot(block[:rows], w_low))
+    out_ref[...] = total
     fetch.wait()
     levels = lax.broadcasted_iota(jnp.int32, hot_ref.shape, 0)
     hot_ref[...] = onehot(levels == agg_buf[...])
-    total = jnp.zeros(out_ref.shape, F32)
-    for k, start in enumerate(starts[:-2]):
-        part = k % per_block
-        block = parts_ref[k // per_block, :, part * step : (part + 1) * step]
-        copies[k].wait()
-        w_hi, w_low = split2(fine_buf[pl.ds(start, step)])
-        both = dot(block[: 2 * rows], w_hi)
-        total = total + (both[:rows] + both[rows:] + dot(block[:rows], w_low))
-    out_ref[...] = total
     for side in range(2):
-        start = starts[side - 2]
         copies[side - 2].wait()
-        hi_ref[side], low_ref[side] = split2(fine_buf[start : start + margin])
+        at = (shards - early) * cols + side * margin
+        hi_ref[side], low_ref[side] = split2(fine_buf[at : at + margin])
 
 
 def mine_kernel(halo_ref, hi_ref, low_ref, total_ref, out_ref, copy_ref):
@@ -184,16 +198,22 @@
     out_ref[...] = total_ref[...] + dot_halves(halo_ref[...], hi_ref[side], low_ref[side])
 
 
-def tail_kernel(width, got_ref, hot_ref, total_ref, out_ref):
-    subs, shards, half, _ = got_ref.shape
-    sums = [got_ref[0, shard] for shard in range(shards)]
-    for sub in range(1, subs):
-        for shard in range(shards):
-            sums[shard] = sums[shard] + got_ref[sub, shard]
+def reduce_kernel(got_ref, out_ref):
+    total = got_ref[0]
+    for sub in range(1, got_ref.shape[0]):
+        total = total + got_ref[sub]
+    out_ref[...] = total
+
+
+def tail_kernel(width, mine_ref, other_ref, hot_ref, total_ref, out_ref):
+    chips, half, _ = mine_ref.shape
+    odd = lax.axis_index("blk") & 1
     lane = lax.broadcasted_iota(jnp.int32, (half, LANES), 1)
     top, bottom = [], []
-    for pair in range(shards // 2):
-        left, right = sums[2 * pair], sums[2 * pair + 1]
+    for chip in range(chips):
+        mine, other = mine_ref[chip], other_ref[chip]
+        left = jnp.where(odd == 1, other, mine)
+        right = jnp.where(odd == 1, mine, other)
         top.append(jnp.where(lane < width, left, pltpu.roll(right, width, 1)))
         bottom.append(jnp.where(lane < width, pltpu.roll(left, width, 1), right))
     coarse = jnp.concatenate([jnp.concatenate(top, axis=1), jnp.concatenate(bottom, axis=1)], axis=0)
@@ -224,6 +244,7 @@
     margin = wanted_rows.shape[2]
     coarse_len = coarse_inverse.shape[0]
     width = coarse_len // shards
+    chips = shards // 2
     packed_rows = -(-(rows * tiles + tiles) // 8) * 8
     core_swap = [(b, b ^ 1) for b in range(shards)]
     far_swap = [(b, b ^ 2) for b in range(shards)]
@@ -264,20 +285,24 @@
     over_both = lax.ppermute(packed, "blk", both_swap)
     blocks = (packed, over_core, over_y, over_both)
 
-    send, parts = pl.pallas_call(
+    send, parts, early = pl.pallas_call(
         functools.partial(coarse_kernel, width, rows, tiles, shards),
         out_shape=(
-            jax.ShapeDtypeStruct((subs, shards, rows // 2, LANES), F32),
+            jax.ShapeDtypeStruct((subs, chips, rows // 2, LANES), F32),
             jax.ShapeDtypeStruct((shards, 3 * rows, cols), BF16),
+            jax.ShapeDtypeStruct((2, cols, cols), F32),
         ),
-        in_specs=[whole()] * (shards + 1),
-        out_specs=(whole(), whole()),
+        in_specs=[whole()] * (shards + 1) + [whole(pl.ANY)],
+        out_specs=(whole(), whole(), whole()),
+        scratch_shapes=[pltpu.SemaphoreType.DMA((2,))],
         compiler_params=limit(12),
         cost_estimate=weight(8 * 10**9),
         name="coarse",
-    )(*blocks, table)
-    flat = send.reshape((subs * shards,) + send.shape[2:])
-    got = lax.all_to_all(flat, ("sub", "blk"), 0, 0, tiled=True).reshape(send.shape)
+    )(*blocks, table, in_hbm(fine_inverse))
+    flat = send.reshape((subs * chips,) + send.shape[2:])
+    same_core = [[k for k in range(subs * shards) if k % 2 == core] for core in range(2)]
+    got = lax.all_to_all(flat, ("sub", "blk"), 0, 0, axis_index_groups=same_core, tiled=True)
+    got = got.reshape(send.shape)
 
     outgoing = pl.pallas_call(
         margin_kernel,
@@ -298,17 +323,17 @@
             jax.ShapeDtypeStruct((2, margin, cols), BF16),
             jax.ShapeDtypeStruct((coarse_len, cols), BF16),
         ),
-        in_specs=[whole(), whole(pl.ANY), whole(pl.ANY)],
+        in_specs=[whole(), whole(), whole(pl.ANY), whole(pl.ANY)],
         out_specs=(whole(),) * 4,
         scratch_shapes=[
             pltpu.VMEM(codes.shape, jnp.int32),
-            pltpu.VMEM(fine_inverse.shape[1:], F32),
+            pltpu.VMEM((fine_inverse.shape[1] - 2 * cols, cols), F32),
             pltpu.SemaphoreType.DMA((shards * tiles // 2 + 3,)),
         ],
         compiler_params=limit(16),
         cost_estimate=weight(40 * 10**9),
         name="owned",
-    )(parts, in_hbm(codes), in_hbm(fine_inverse))
+    )(parts, early, in_hbm(codes), in_hbm(fine_inverse))
 
     fine, mine = pl.pallas_call(
         mine_kernel,
@@ -333,14 +358,25 @@
         name="other",
     )(other, w_hi, w_low, fine)
 
+    sums = pl.pallas_call(
+        reduce_kernel,
+        out_shape=jax.ShapeDtypeStruct(got.shape[1:], F32),
+        in_specs=[whole()],
+        out_specs=whole(),
+        compiler_params=limit(8),
+        cost_estimate=weight(10**8),
+        name="reduce",
+    )(got)
+    other_sums = lax.ppermute(sums, "blk", core_swap)
+
     return pl.pallas_call(
         functools.partial(tail_kernel, width),
         out_shape=jax.ShapeDtypeStruct((rows, cols), F32),
-        in_specs=[whole()] * 3,
+        in_specs=[whole()] * 4,
         out_specs=whole(),
         compiler_params=limit(12),
         name="tail",
-    )(got, hot, fine)
+    )(sums, other_sums, hot, fine)
 
 
 def solution(mesh):

time: 27.8 us -> 29.4 us (1.058)
  local copies, waits for them, and re-layouts: 0 us -> 1.34 us
  waiting for transfers between devices: 3.96 us -> 2.67 us
  starting transfers between devices: 16.6 us -> 17.6 us
  Pallas kernels: 6.91 us -> 7.34 us
    ppermute x1, starting transfers between devices: 2.47 us -> 0.07 us  [on_device(): over_both = lax.ppermute(packed, 'blk', both_swap)]
    ppermute x1, starting transfers between devices: 0.64 us -> 2.59 us  [on_device(): over_y = lax.ppermute(packed, 'blk', far_swap)]
    unnamed x0 -> x4, local copies, waits for them, and re-layouts: none -> 1.34 us
    ppermute x1, waiting for transfers between devices: 1.2 us -> 0.01 us  [on_device(): other = lax.ppermute(mine, 'blk', core_swap)]
    all_to_all x1, waiting for transfers between devices: 2.29 us -> 1.26 us  [on_device(): lax.all_to_all(flat, ('sub', 'blk'), 0, 0, axis_index_groups=same_core, t...]
    pallas_call x1, Pallas kernels: 1.53 us -> 2.53 us  [on_device(): pl.pallas_call(functools.partial(coarse_kernel, width, rows, tiles, shard...]
    ppermute x0 -> x1, waiting for transfers between devices: none -> 0.96 us  [on_device(): other_sums = lax.ppermute(sums, 'blk', core_swap)]
    all_to_all x1, starting transfers between devices: 6.1 us -> 6.78 us  [on_device(): lax.all_to_all(flat, ('sub', 'blk'), 0, 0, axis_index_groups=same_core, t...]
  transfers between devices with their start and end apart: 7 -> 8, of which waited for: 3 -> 3; matrix products, arithmetic and copies ran while one was open for 0% -> 0% of each run, Pallas kernels for 18% -> 18%
where the time goes in v2:
time: 29.4 us; the launch traced here: 29.1 us
  starting transfers between devices  17.6 us (60%)
  Pallas kernels  7.34 us (25%)
  waiting for transfers between devices  2.67 us (9%)
  local copies, waits for them, and re-layouts  1.34 us (5%)
    all_to_all x1, starting transfers between devices, on_device(): lax.all_to_all(flat, ('sub', 'blk'), 0, 0, axis_index_groups=same_core, t...  6.78 us
    ppermute x1, starting transfers between devices, on_device(): halo = lax.ppermute(outgoing, ('sub', 'blk'), neighbours)  3.97 us
    ppermute x1, starting transfers between devices, on_device(): lists = lax.ppermute(lists, ('sub', 'blk'), neighbours)  3.59 us
    ppermute x1, starting transfers between devices, on_device(): over_y = lax.ppermute(packed, 'blk', far_swap)  2.59 us
    pallas_call x1, Pallas kernels, on_device(): pl.pallas_call(functools.partial(coarse_kernel, width, rows, tiles, shard...  2.53 us
    pallas_call x1, Pallas kernels, on_device(): pl.pallas_call(functools.partial(own_kernel, margin), out_shape=(jax.Shap...  2.08 us
    unnamed x4, local copies, waits for them, and re-layouts  1.34 us
    all_to_all x1, waiting for transfers between devices, on_device(): lax.all_to_all(flat, ('sub', 'blk'), 0, 0, axis_index_groups=same_core, t...  1.26 us
  transfers between devices with their start and end apart: 8, of which 3 were waited for; matrix products, arithmetic and copies ran while one was open for 0% of the time, Pallas kernels for 18%

profile of v2, /device:TPU:0, one launch (start us, length us, event | category | flops | bytes accessed | tf_op | source)
XLA Modules:
  0.0 29.1 jit_solution(14242576013564576854)
XLA Ops:
  0.0 1.2 %pack.1 = (f32[136,128]{1,0:T(8,128)S(1)}, s32[2,256]{1,0:T(2,128)S(1)}, f32[1024,128]{1,0:T(8,128)S(1)}) custom-call(f32[32,512]{1,0:T(8,128)} %residual_ref.1, s32[1,512]{1,0:T(1,128)} %bitcast.8, s32[2,256]{1,0:T(2,128)} %bitcast.7, s32[1,2]{1,0:T(1,128)} %counts_ref.1, f32[1024,128]{1,0:T(8,128)} %bitcast.6), custom_call_target="tpu_custom_call" | custom-call | tf_op jit(solution)/shard_map/pack/pallas_call | solution.py:263
  1.2 0.5 %collective-permute-start = (f32[136,128]{1,0:T(8,128)S(1)}, f32[136,128]{1,0:T(8,128)S(1)}, u32[]{:S(2)}, u32[]{:S(2)}) collective-permute-start(f32[136,128]{1,0:T(8,128)S(1)} %get-tuple-element.17.refs_0_), channel_id=1, source_target_pairs={{0,1},{1,0},{2,3},{3,2},{4,5},{5,4},{6,7},{7,6},{8,9},{9,8},{10,11... | collective-permute-start | bytes 208904 | tf_op jit(solution)/shard_map/ppermute | solution.py:284
  1.7 2.6 %collective-permute-start.1 = (f32[136,128]{1,0:T(8,128)S(1)}, f32[136,128]{1,0:T(8,128)S(1)}, u32[]{:S(2)}, u32[]{:S(2)}) collective-permute-start(f32[136,128]{1,0:T(8,128)S(1)} %get-tuple-element.17.refs_0_), channel_id=1, source_target_pairs={{0,2},{1,3},{2,0},{3,1},{4,6},{5,7},{6,4},{7,5},{8,10},{9,11},{10,... | collective-permute-start | bytes 208904 | tf_op jit(solution)/shard_map/ppermute | solution.py:283
  4.3 0.1 collective-permute-start.2
  4.4 3.6 %collective-permute-start.4 = (s32[2,256]{1,0:T(2,128)S(1)}, s32[2,256]{1,0:T(2,128)S(1)}, u32[]{:S(2)}, u32[]{:S(2)}) collective-permute-start(s32[2,256]{1,0:T(2,128)S(1)} %get-tuple-element.23), channel_id=1, source_target_pairs={{0,4},{2,6},{4,0},{5,9},{6,2},{7,11},{8,12},{9,5},{10,14},{11,7},{... | collective-permute-start | bytes 6152 | tf_op jit(solution)/shard_map/ppermute | solution.py:282
  8.0 0.0 collective-permute-done.refs_1_
  8.0 0.0 collective-permute-done.1.refs_2_
  8.0 0.4 %collective-permute-done.2.refs_3_ = f32[136,128]{1,0:T(8,128)S(1)} collective-permute-done((f32[136,128]{1,0:T(8,128)S(1)}, f32[136,128]{1,0:T(8,128)S(1)}, u32[]{:S(2)}, u32[]{:S(2)}) %collective-permute-start.2) | collective-permute-done | bytes 69664 | tf_op jit(solution)/shard_map/ppermute | solution.py:285
  8.4 2.5 %coarse.1 = (f32[8,2,16,128]{3,2,1,0:T(8,128)}, bf16[4,96,512]{2,1,0:T(8,128)(2,1)S(1)}, f32[2,512,512]{2,1,0:T(8,128)S(1)}) custom-call(f32[136,128]{1,0:T(8,128)S(1)} %get-tuple-element.17.refs_0_, f32[136,128]{1,0:T(8,128)S(1)} %collective-permute-done.refs_1_, f32[136,128]{1,0:T(8,128)S(1)} %collective-permute-done.1.refs_2_, ...), custom_call_target="tpu_custom_call" | custom-call | flops 8000000000 | tf_op jit(solution)/shard_map/coarse/pallas_call | solution.py:288
  11.0 0.0 copy-start
  11.0 1.3 %copy-done = f32[2,512,512]{2,1,0:T(8,128)} copy-done((f32[2,512,512]{2,1,0:T(8,128)}, f32[2,512,512]{2,1,0:T(8,128)S(1)}, u32[]{:S(2)}) %copy-start) | copy-done | bytes 2097176
  12.3 6.8 %all-to-all-start = ((f32[16,16,128]{2,1,0:T(8,128)}), f32[16,16,128]{2,1,0:T(8,128)S(1)}, u32[]{:S(2)}, u32[]{:S(2)}) async-start(f32[16,16,128]{2,1,0:T(8,128)} %bitcast.3), calls=%async_computation | async-start | bytes 262144 | tf_op jit(solution)/shard_map/all_to_all | solution.py:304
  19.1 0.0 collective-permute-done.4.lists_ref
  19.1 0.0 copy-start.1
  19.1 0.3 %margins.1 = f32[32,256]{1,0:T(8,128)S(1)} custom-call(bf16[4,96,512]{2,1,0:T(8,128)(2,1)S(1)} %get-tuple-element.20.parts_ref, s32[2,256]{1,0:T(2,128)S(1)} %collective-permute-done.4.lists_ref), custom_call_target="tpu_custom_call" | custom-call | flops 4000000000 | tf_op jit(solution)/shard_map/margins/pallas_call | solution.py:307
  19.4 4.0 %collective-permute-start.5 = (f32[32,256]{1,0:T(8,128)S(1)}, f32[32,256]{1,0:T(8,128)S(1)}, u32[]{:S(2)}, u32[]{:S(2)}) collective-permute-start(f32[32,256]{1,0:T(8,128)S(1)} %margins.1), channel_id=1, source_target_pairs={{0,4},{2,6},{4,0},{5,9},{6,2},{7,11},{8,12},{9,5},{10,14},{11,7},{... | collective-permute-start | bytes 98312 | tf_op jit(solution)/shard_map/ppermute | solution.py:316
  23.4 0.0 copy-done.1
  23.4 2.1 %owned.1 = (f32[32,512]{1,0:T(8,128)S(1)}, bf16[2,256,512]{2,1,0:T(8,128)(2,1)S(1)}, bf16[2,256,512]{2,1,0:T(8,128)(2,1)S(1)}, bf16[256,512]{1,0:T(8,128)(2,1)S(1)}) custom-call(bf16[4,96,512]{2,1,0:T(8,128)(2,1)S(1)} %get-tuple-element.20.parts_ref, f32[2,512,512]{2,1,0:T(8,128)S(1)} %copy-done.1, s32[1,512]{1,0:T(1,128)} %bitcast.9, f32[1,2560,512]{2,1,0:T(8,128)} %fine_ref.1), custom_call_target="tpu_custom_call" | custom-call | flops 40000000000 | tf_op jit(solution)/shard_map/owned/pallas_call | solution.py:318
  25.5 0.0 collective-permute-done.5.halo_ref
  25.5 0.2 mine.1
  25.7 0.0 collective-permute-start.6
  25.7 1.3 %all-to-all-done = f32[16,16,128]{2,1,0:T(8,128)S(1)} async-done(((f32[16,16,128]{2,1,0:T(8,128)}), f32[16,16,128]{2,1,0:T(8,128)S(1)}, u32[]{:S(2)}, u32[]{:S(2)}) %all-to-all-start) | async-done | bytes 131104 | tf_op jit(solution)/shard_map/all_to_all | solution.py:304
  27.0 0.1 collective-permute-start.3
  27.1 0.0 collective-permute-done.6.halo_ref
  27.1 0.2 other.1.total_ref
  27.3 1.0 %collective-permute-done.3.other_ref = f32[2,16,128]{2,1,0:T(8,128)S(1)} collective-permute-done((f32[2,16,128]{2,1,0:T(8,128)S(1)}, f32[2,16,128]{2,1,0:T(8,128)S(1)}, u32[]{:S(2)}, u32[]{:S(2)}) %collective-permute-start.3) | collective-permute-done | bytes 16416 | tf_op jit(solution)/shard_map/ppermute | solution.py:370
  28.2 0.9 %tail.1 = f32[32,512]{1,0:T(8,128)} custom-call(f32[2,16,128]{2,1,0:T(8,128)S(1)} %reduce.1.mine_ref, f32[2,16,128]{2,1,0:T(8,128)S(1)} %collective-permute-done.3.other_ref, bf16[256,512]{1,0:T(8,128)(2,1)S(1)} %get-tuple-element.22.hot_ref, f32[32,512]{1,0:T(8,128)S(1)} %other.1.total_ref), custom_call_target="tpu_custom_call" | custom-call | tf_op jit(solution)/shard_map/tail/pallas_call | solution.py:372
  (1 shorter events, 0.0 us)
Async XLA Ops:
  1.2 6.8 %collective-permute-start = (f32[136,128]{1,0:T(8,128)S(1)}, f32[136,128]{1,0:T(8,128)S(1)}, u32[]{:S(2)}, u32[]{:S(2)}) collective-permute-start(f32[136,128]{1,0:T(8,128)S(1)} %get-tuple-element.17.refs_0_), channel_id=1, source_target_pairs={{0,1},{1,0},{2,3},{3,2},{4,5},{5,4},{6,7},{7,6},{8,9},{9,8},{10,11... | collective-permute-start | bytes 208904 | tf_op jit(solution)/shard_map/ppermute | solution.py:284
  1.7 6.3 %collective-permute-start.1 = (f32[136,128]{1,0:T(8,128)S(1)}, f32[136,128]{1,0:T(8,128)S(1)}, u32[]{:S(2)}, u32[]{:S(2)}) collective-permute-start(f32[136,128]{1,0:T(8,128)S(1)} %get-tuple-element.17.refs_0_), channel_id=1, source_target_pairs={{0,2},{1,3},{2,0},{3,1},{4,6},{5,7},{6,4},{7,5},{8,10},{9,11},{10,... | collective-permute-start | bytes 208904 | tf_op jit(solution)/shard_map/ppermute | solution.py:283
  4.3 4.1 %collective-permute-start.2 = (f32[136,128]{1,0:T(8,128)S(1)}, f32[136,128]{1,0:T(8,128)S(1)}, u32[]{:S(2)}, u32[]{:S(2)}) collective-permute-start(f32[136,128]{1,0:T(8,128)S(1)} %get-tuple-element.17.refs_0_), channel_id=1, source_target_pairs={{0,3},{1,2},{2,1},{3,0},{4,7},{5,6},{6,5},{7,4},{8,11},{9,10},{10,... | collective-permute-start | bytes 208904 | tf_op jit(solution)/shard_map/ppermute | solution.py:285
  4.4 14.7 %collective-permute-start.4 = (s32[2,256]{1,0:T(2,128)S(1)}, s32[2,256]{1,0:T(2,128)S(1)}, u32[]{:S(2)}, u32[]{:S(2)}) collective-permute-start(s32[2,256]{1,0:T(2,128)S(1)} %get-tuple-element.23), channel_id=1, source_target_pairs={{0,4},{2,6},{4,0},{5,9},{6,2},{7,11},{8,12},{9,5},{10,14},{11,7},{... | collective-permute-start | bytes 6152 | tf_op jit(solution)/shard_map/ppermute | solution.py:282
  11.0 1.3 %copy-start = (f32[2,512,512]{2,1,0:T(8,128)}, f32[2,512,512]{2,1,0:T(8,128)S(1)}, u32[]{:S(2)}) copy-start(f32[2,512,512]{2,1,0:T(8,128)S(1)} %get-tuple-element.21.early_ref) | copy-start | bytes 6291460
  12.3 14.7 %all-to-all-start = ((f32[16,16,128]{2,1,0:T(8,128)}), f32[16,16,128]{2,1,0:T(8,128)S(1)}, u32[]{:S(2)}, u32[]{:S(2)}) async-start(f32[16,16,128]{2,1,0:T(8,128)} %bitcast.3), calls=%async_computation | async-start | bytes 262144 | tf_op jit(solution)/shard_map/all_to_all | solution.py:304
  19.1 4.3 %copy-start.1 = (f32[2,512,512]{2,1,0:T(8,128)S(1)}, f32[2,512,512]{2,1,0:T(8,128)}, u32[]{:S(2)}) copy-start(f32[2,512,512]{2,1,0:T(8,128)} %copy-done) | copy-start | bytes 6291460
  19.4 6.1 %collective-permute-start.5 = (f32[32,256]{1,0:T(8,128)S(1)}, f32[32,256]{1,0:T(8,128)S(1)}, u32[]{:S(2)}, u32[]{:S(2)}) collective-permute-start(f32[32,256]{1,0:T(8,128)S(1)} %margins.1), channel_id=1, source_target_pairs={{0,4},{2,6},{4,0},{5,9},{6,2},{7,11},{8,12},{9,5},{10,14},{11,7},{... | collective-permute-start | bytes 98312 | tf_op jit(solution)/shard_map/ppermute | solution.py:316
  25.7 1.4 %collective-permute-start.6 = (f32[32,256]{1,0:T(8,128)S(1)}, f32[32,256]{1,0:T(8,128)S(1)}, u32[]{:S(2)}, u32[]{:S(2)}) collective-permute-start(f32[32,256]{1,0:T(8,128)S(1)} %get-tuple-element.27), channel_id=1, source_target_pairs={{0,1},{1,0},{2,3},{3,2},{4,5},{5,4},{6,7},{7,6},{8,9},{9,8},{10,11... | collective-permute-start | bytes 98312 | tf_op jit(solution)/shard_map/ppermute | solution.py:350
  27.0 1.2 %collective-permute-start.3 = (f32[2,16,128]{2,1,0:T(8,128)S(1)}, f32[2,16,128]{2,1,0:T(8,128)S(1)}, u32[]{:S(2)}, u32[]{:S(2)}) collective-permute-start(f32[2,16,128]{2,1,0:T(8,128)S(1)} %reduce.1.mine_ref), channel_id=1, source_target_pairs={{0,1},{1,0},{2,3},{3,2},{4,5},{5,4},{6,7},{7,6},{8,9},{9,8},{10,11... | collective-permute-start | bytes 49160 | tf_op jit(solution)/shard_map/ppermute | solution.py:370

commit v3 on v1

--- a/solution.py
+++ b/solution.py
@@ -62,12 +62,12 @@
 
 
 def pack_kernel(
-    residual_ref, agg_ref, lists_ref, counts_ref, coarse_ref,
-    out_ref, lists_out, coarse_out,
+    residual_ref, agg_ref, lists_ref, counts_ref,
+    out_ref, lists_out,
     residual_buf, agg_buf, lists_buf, counts_buf, sems,
 ):
-    sources = (residual_ref, agg_ref, lists_ref, counts_ref, coarse_ref)
-    targets = (residual_buf, agg_buf, lists_buf, counts_buf, coarse_out)
+    sources = (residual_ref, agg_ref, lists_ref, counts_ref)
+    targets = (residual_buf, agg_buf, lists_buf, counts_buf)
     fetches = [pltpu.make_async_copy(a, b, sems.at[k]) for k, (a, b) in enumerate(zip(sources, targets))]
     for fetch in fetches:
         fetch.start()
@@ -86,14 +86,10 @@
     for side in range(2):
         used = slots < counts_buf[:, side : side + 1]
         lists_out[side : side + 1] = jnp.where(used, lists_buf[side : side + 1], -1)
-    fetches[4].wait()
-
-
-def coarse_kernel(width, rows, tiles, shards, *refs):
-    blocks, (coarse_ref, send_ref, parts_ref) = refs[:shards], refs[shards:]
-    cols = tiles * LANES
-    coarse_len = width * shards
-    levels = lax.broadcasted_iota(jnp.int32, (coarse_len, cols), 0)
+
+
+def right_hand_side(rows, tiles, coarse_len, blocks, parts_ref):
+    levels = lax.broadcasted_iota(jnp.int32, (coarse_len, tiles * LANES), 0)
     rhs = jnp.zeros((3 * rows, coarse_len), F32)
     for k, ref in enumerate(blocks):
         codes = [ref[pl.ds(tiles * rows + t, 1)] for t in range(tiles)]
@@ -101,37 +97,61 @@
         parts = split3(block_rows(ref, rows, 0, tiles))
         parts_ref[k] = parts
         rhs = rhs + dot(parts, onehot(levels == unknowns), NT)
-    rhs = fold3(rhs)
+    return fold3(rhs)
+
+
+def near_kernel(
+    rows, tiles, packed_ref, core_ref, coarse_ref, rhs_ref, parts_ref, hi_ref, low_ref, coarse_buf, sem
+):
+    fetch = pltpu.make_async_copy(coarse_ref, coarse_buf, sem)
+    fetch.start()
+    coarse_len = hi_ref.shape[0]
+    rhs_ref[...] = right_hand_side(rows, tiles, coarse_len, (packed_ref, core_ref), parts_ref)
+    stride = coarse_buf.shape[0] // coarse_len
+    fetch.wait()
+    for tile in range(stride):
+        at = slice(tile * LANES, (tile + 1) * LANES)
+        hi_ref[:, at], low_ref[:, at] = split2(coarse_buf[pl.ds(tile, coarse_len, stride=stride), :])
+
+
+def coarse_kernel(
+    width, rows, tiles, y_ref, both_ref, rhs_ref, hi_ref, low_ref, send_ref, parts_ref
+):
+    coarse_len = hi_ref.shape[0]
+    rhs = rhs_ref[...] + right_hand_side(rows, tiles, coarse_len, (y_ref, both_ref), parts_ref)
     half = rows // 2
     lane = lax.broadcasted_iota(jnp.int32, (half, LANES), 1)
-    stride = coarse_ref.shape[0] // coarse_len
-    for tile in range(0, stride, 2):
-        parts = [coarse_ref[pl.ds(tile + k, coarse_len, stride=stride), :] for k in range(2)]
-        value = dot_halves(rhs, *split2(jnp.concatenate(parts, axis=1)))
+    step = 2 * LANES
+    for first in range(0, hi_ref.shape[1], step):
+        at = slice(first, first + step)
+        value = dot_halves(rhs, hi_ref[:, at], low_ref[:, at])
         for k in range(2):
+            to = 2 * (first // LANES + k)
             part = value[:, k * LANES : (k + 1) * LANES]
             turned = pltpu.roll(part, width, 1)
             left = jnp.where(lane < width, part[:half], turned[half:])
             right = jnp.where(lane < width, turned[:half], part[half:])
-            for copy in range(shards):
-                send_ref[2 * (tile + k), copy] = left
-                send_ref[2 * (tile + k) + 1, copy] = right
-
-
-def margin_kernel(parts_ref, lists_ref, out_ref):
-    shards, rows, cols = parts_ref.shape
+            for copy in range(send_ref.shape[1]):
+                send_ref[to, copy] = left
+                send_ref[to + 1, copy] = right
+
+
+def margin_kernel(near_ref, far_ref, lists_ref, out_ref):
+    half, rows, cols = near_ref.shape
     wanted = jnp.where(facing() == 1, lists_ref[1:2], lists_ref[0:1])
     local = lax.broadcasted_iota(jnp.int32, (cols, wanted.shape[1]), 0)
     total = jnp.zeros((rows, wanted.shape[1]), F32)
-    for k in range(shards):
-        total = total + dot(parts_ref[k], onehot(local == wanted - block_shard(k) * cols))
+    for k in range(2 * half):
+        part = near_ref[k] if k < half else far_ref[k - half]
+        total = total + dot(part, onehot(local == wanted - block_shard(k) * cols))
     out_ref[...] = fold3(total)
 
 
 def own_kernel(
-    margin, parts_ref, agg_ref, fine_ref, out_ref, hi_ref, low_ref, hot_ref, agg_buf, fine_buf, sems
+    margin, near_ref, far_ref, agg_ref, fine_ref, out_ref, hi_ref, low_ref, hot_ref, agg_buf, fine_buf, sems
 ):
-    shards, rows, cols = parts_ref.shape
+    half, rows, cols = near_ref.shape
+    shards = 2 * half
     rows = rows // 3
     tiles = cols // LANES
     ext = fine_ref.shape[1]
@@ -160,7 +180,9 @@
     total = jnp.zeros(out_ref.shape, F32)
     for k, start in enumerate(starts[:-2]):
         part = k % per_block
-        block = parts_ref[k // per_block, :, part * step : (part + 1) * step]
+        at = k // per_block
+        ref = near_ref if at < half else far_ref
+        block = ref[at % half, :, part * step : (part + 1) * step]
         copies[k].wait()
         w_hi, w_low = split2(fine_buf[pl.ds(start, step)])
         both = dot(block[: 2 * rows], w_hi)
@@ -184,16 +206,22 @@
     out_ref[...] = total_ref[...] + dot_halves(halo_ref[...], hi_ref[side], low_ref[side])
 
 
-def tail_kernel(width, got_ref, hot_ref, total_ref, out_ref):
-    subs, shards, half, _ = got_ref.shape
-    sums = [got_ref[0, shard] for shard in range(shards)]
-    for sub in range(1, subs):
-        for shard in range(shards):
-            sums[shard] = sums[shard] + got_ref[sub, shard]
+def reduce_kernel(got_ref, out_ref):
+    total = got_ref[0]
+    for sub in range(1, got_ref.shape[0]):
+        total = total + got_ref[sub]
+    out_ref[...] = total
+
+
+def tail_kernel(width, mine_ref, other_ref, hot_ref, total_ref, out_ref):
+    chips, half, _ = mine_ref.shape
+    odd = lax.axis_index("blk") & 1
     lane = lax.broadcasted_iota(jnp.int32, (half, LANES), 1)
     top, bottom = [], []
-    for pair in range(shards // 2):
-        left, right = sums[2 * pair], sums[2 * pair + 1]
+    for chip in range(chips):
+        mine, other = mine_ref[chip], other_ref[chip]
+        left = jnp.where(odd == 1, other, mine)
+        right = jnp.where(odd == 1, mine, other)
         top.append(jnp.where(lane < width, left, pltpu.roll(right, width, 1)))
         bottom.append(jnp.where(lane < width, pltpu.roll(left, width, 1), right))
     coarse = jnp.concatenate([jnp.concatenate(top, axis=1), jnp.concatenate(bottom, axis=1)], axis=0)
@@ -224,6 +252,7 @@
     margin = wanted_rows.shape[2]
     coarse_len = coarse_inverse.shape[0]
     width = coarse_len // shards
+    chips = shards // 2
     packed_rows = -(-(rows * tiles + tiles) // 8) * 8
     core_swap = [(b, b ^ 1) for b in range(shards)]
     far_swap = [(b, b ^ 2) for b in range(shards)]
@@ -239,55 +268,70 @@
     table = coarse_inverse.reshape(-1, LANES)
     packed_shape = (packed_rows, LANES)
 
-    packed, lists, table = pl.pallas_call(
+    packed, lists = pl.pallas_call(
         pack_kernel,
         out_shape=(
             jax.ShapeDtypeStruct(packed_shape, F32),
             jax.ShapeDtypeStruct(lists.shape, jnp.int32),
-            jax.ShapeDtypeStruct(table.shape, F32),
         ),
-        in_specs=[whole(pl.ANY)] * 5,
-        out_specs=(whole(), whole(), whole()),
+        in_specs=[whole(pl.ANY)] * 4,
+        out_specs=(whole(), whole()),
         scratch_shapes=[
             pltpu.VMEM(residual.shape, F32),
             pltpu.VMEM(codes.shape, jnp.int32),
             pltpu.VMEM(lists.shape, jnp.int32),
             pltpu.VMEM(wanted_count.shape, jnp.int32),
-            pltpu.SemaphoreType.DMA((5,)),
+            pltpu.SemaphoreType.DMA((4,)),
         ],
         compiler_params=limit(4),
         name="pack",
-    )(in_hbm(residual), in_hbm(codes), in_hbm(lists), in_hbm(wanted_count), in_hbm(table))
+    )(in_hbm(residual), in_hbm(codes), in_hbm(lists), in_hbm(wanted_count))
     lists = lax.ppermute(lists, ("sub", "blk"), neighbours)
     over_y = lax.ppermute(packed, "blk", far_swap)
     over_core = lax.ppermute(packed, "blk", core_swap)
     over_both = lax.ppermute(packed, "blk", both_swap)
-    blocks = (packed, over_core, over_y, over_both)
-
-    send, parts = pl.pallas_call(
-        functools.partial(coarse_kernel, width, rows, tiles, shards),
+
+    rhs, near, m_hi, m_low = pl.pallas_call(
+        functools.partial(near_kernel, rows, tiles),
         out_shape=(
-            jax.ShapeDtypeStruct((subs, shards, rows // 2, LANES), F32),
-            jax.ShapeDtypeStruct((shards, 3 * rows, cols), BF16),
+            jax.ShapeDtypeStruct((rows, coarse_len), F32),
+            jax.ShapeDtypeStruct((2, 3 * rows, cols), BF16),
+            jax.ShapeDtypeStruct((coarse_len, subs * width), BF16),
+            jax.ShapeDtypeStruct((coarse_len, subs * width), BF16),
         ),
-        in_specs=[whole()] * (shards + 1),
+        in_specs=[whole(), whole(), whole(pl.ANY)],
+        out_specs=(whole(),) * 4,
+        scratch_shapes=[pltpu.VMEM(table.shape, F32), pltpu.SemaphoreType.DMA],
+        compiler_params=limit(12),
+        cost_estimate=weight(2 * 10**9),
+        name="near",
+    )(packed, over_core, in_hbm(table))
+    send, far = pl.pallas_call(
+        functools.partial(coarse_kernel, width, rows, tiles),
+        out_shape=(
+            jax.ShapeDtypeStruct((subs, chips, rows // 2, LANES), F32),
+            jax.ShapeDtypeStruct((shards - 2, 3 * rows, cols), BF16),
+        ),
+        in_specs=[whole()] * 5,
         out_specs=(whole(), whole()),
         compiler_params=limit(12),
         cost_estimate=weight(8 * 10**9),
         name="coarse",
-    )(*blocks, table)
-    flat = send.reshape((subs * shards,) + send.shape[2:])
-    got = lax.all_to_all(flat, ("sub", "blk"), 0, 0, tiled=True).reshape(send.shape)
+    )(over_y, over_both, rhs, m_hi, m_low)
+    flat = send.reshape((subs * chips,) + send.shape[2:])
+    same_core = [[k for k in range(subs * shards) if k % 2 == core] for core in range(2)]
+    got = lax.all_to_all(flat, ("sub", "blk"), 0, 0, axis_index_groups=same_core, tiled=True)
+    got = got.reshape(send.shape)
 
     outgoing = pl.pallas_call(
         margin_kernel,
         out_shape=jax.ShapeDtypeStruct((rows, margin), F32),
-        in_specs=[whole()] * 2,
+        in_specs=[whole()] * 3,
         out_specs=whole(),
         compiler_params=limit(8),
         cost_estimate=weight(4 * 10**9),
         name="margins",
-    )(parts, lists)
+    )(near, far, lists)
     halo = lax.ppermute(outgoing, ("sub", "blk"), neighbours)
 
     owned, w_hi, w_low, hot = pl.pallas_call(
@@ -298,7 +342,7 @@
             jax.ShapeDtypeStruct((2, margin, cols), BF16),
             jax.ShapeDtypeStruct((coarse_len, cols), BF16),
         ),
-        in_specs=[whole(), whole(pl.ANY), whole(pl.ANY)],
+        in_specs=[whole(), whole(), whole(pl.ANY), whole(pl.ANY)],
         out_specs=(whole(),) * 4,
         scratch_shapes=[
             pltpu.VMEM(codes.shape, jnp.int32),
@@ -308,7 +352,7 @@
         compiler_params=limit(16),
         cost_estimate=weight(40 * 10**9),
         name="owned",
-    )(parts, in_hbm(codes), in_hbm(fine_inverse))
+    )(near, far, in_hbm(codes), in_hbm(fine_inverse))
 
     fine, mine = pl.pallas_call(
         mine_kernel,
@@ -333,14 +377,25 @@
         name="other",
     )(other, w_hi, w_low, fine)
 
+    sums = pl.pallas_call(
+        reduce_kernel,
+        out_shape=jax.ShapeDtypeStruct(got.shape[1:], F32),
+        in_specs=[whole()],
+        out_specs=whole(),
+        compiler_params=limit(8),
+        cost_estimate=weight(10**8),
+        name="reduce",
+    )(got)
+    other_sums = lax.ppermute(sums, "blk", core_swap)
+
     return pl.pallas_call(
         functools.partial(tail_kernel, width),
         out_shape=jax.ShapeDtypeStruct((rows, cols), F32),
-        in_specs=[whole()] * 3,
+        in_specs=[whole()] * 4,
         out_specs=whole(),
         compiler_params=limit(12),
         name="tail",
-    )(got, hot, fine)
+    )(sums, other_sums, hot, fine)
 
 
 def solution(mesh):

time: 27.8 us -> 27 us (0.971)
  waiting for transfers between devices: 3.96 us -> 1.72 us
  Pallas kernels: 6.91 us -> 7.78 us
  starting transfers between devices: 16.6 us -> 17 us
    all_to_all x1, waiting for transfers between devices: 2.29 us -> 0.73 us  [on_device(): lax.all_to_all(flat, ('sub', 'blk'), 0, 0, axis_index_groups=same_core, t...]
    pallas_call x1 -> x3, Pallas kernels: 1.53 us -> 2.6 us  [the longest x1 1.3 us: on_device(): pl.pallas_call(functools.partial(coarse_kernel, width, rows, tiles), out_...]
    ppermute x1, waiting for transfers between devices: 1.2 us -> 0.38 us  [on_device(): other = lax.ppermute(mine, 'blk', core_swap)]
    ppermute x0 -> x1, waiting for transfers between devices: none -> 0.6 us  [on_device(): other_sums = lax.ppermute(sums, 'blk', core_swap)]
    ppermute x1, starting transfers between devices: 0.64 us -> 0.04 us  [on_device(): over_y = lax.ppermute(packed, 'blk', far_swap)]
    ppermute x1, starting transfers between devices: 0.04 us -> 0.52 us  [on_device(): over_core = lax.ppermute(packed, 'blk', core_swap)]
    ppermute x1, waiting for transfers between devices: 0.45 us -> 0.01 us  [on_device(): over_y = lax.ppermute(packed, 'blk', far_swap)]
  transfers between devices with their start and end apart: 7 -> 8, of which waited for: 3 -> 3; matrix products, arithmetic and copies ran while one was open for 0% -> 0% of each run, Pallas kernels for 18% -> 22%
where the time goes in v3:
time: 27 us; the launch traced here: 26.6 us
  starting transfers between devices  17 us (63%)
  Pallas kernels  7.78 us (29%)
  waiting for transfers between devices  1.72 us (6%)
    all_to_all x1, starting transfers between devices, on_device(): lax.all_to_all(flat, ('sub', 'blk'), 0, 0, axis_index_groups=same_core, t...  6.04 us
    ppermute x1, starting transfers between devices, on_device(): lists = lax.ppermute(lists, ('sub', 'blk'), neighbours)  3.85 us
    ppermute x1, starting transfers between devices, on_device(): halo = lax.ppermute(outgoing, ('sub', 'blk'), neighbours)  3.84 us
    pallas_call x1, Pallas kernels, on_device(): pl.pallas_call(functools.partial(own_kernel, margin), out_shape=(jax.Shap...  2.67 us
    ppermute x1, starting transfers between devices, on_device(): over_both = lax.ppermute(packed, 'blk', both_swap)  2.64 us
    pallas_call x1, Pallas kernels, on_device(): pl.pallas_call(functools.partial(coarse_kernel, width, rows, tiles), out_...  1.3 us
    pallas_call x1, Pallas kernels, on_device(): pl.pallas_call(functools.partial(near_kernel, rows, tiles), out_shape=(ja...  1.29 us
    pallas_call x1, Pallas kernels, on_device(): pl.pallas_call(pack_kernel, out_shape=(jax.ShapeDtypeStruct(packed_shape,...  0.96 us
  transfers between devices with their start and end apart: 8, of which 3 were waited for; matrix products, arithmetic and copies ran while one was open for 0% of the time, Pallas kernels for 22%

profile of v3, /device:TPU:0, one launch (start us, length us, event | category | flops | bytes accessed | tf_op | source)
XLA Modules:
  0.0 26.6 jit_solution(5436583512627983168)
XLA Ops:
  0.0 1.0 %pack.1 = (f32[136,128]{1,0:T(8,128)S(1)}, s32[2,256]{1,0:T(2,128)S(1)}) custom-call(f32[32,512]{1,0:T(8,128)} %residual_ref.1, s32[1,512]{1,0:T(1,128)} %bitcast.7, s32[2,256]{1,0:T(2,128)} %bitcast.6, s32[1,2]{1,0:T(1,128)} %counts_ref.1), custom_call_target="tpu_custom_call" | custom-call | tf_op jit(solution)/shard_map/pack/pallas_call | solution.py:271
  1.0 0.5 %collective-permute-start.2 = (f32[136,128]{1,0:T(8,128)S(1)}, f32[136,128]{1,0:T(8,128)S(1)}, u32[]{:S(2)}, u32[]{:S(2)}) collective-permute-start(f32[136,128]{1,0:T(8,128)S(1)} %get-tuple-element.19.packed_ref), channel_id=1, source_target_pairs={{0,1},{1,0},{2,3},{3,2},{4,5},{5,4},{6,7},{7,6},{8,9},{9,8},{10,11... | collective-permute-start | bytes 208904 | tf_op jit(solution)/shard_map/ppermute | solution.py:291
  1.5 2.6 %collective-permute-start.1 = (f32[136,128]{1,0:T(8,128)S(1)}, f32[136,128]{1,0:T(8,128)S(1)}, u32[]{:S(2)}, u32[]{:S(2)}) collective-permute-start(f32[136,128]{1,0:T(8,128)S(1)} %get-tuple-element.19.packed_ref), channel_id=1, source_target_pairs={{0,3},{1,2},{2,1},{3,0},{4,7},{5,6},{6,5},{7,4},{8,11},{9,10},{10,... | collective-permute-start | bytes 208904 | tf_op jit(solution)/shard_map/ppermute | solution.py:292
  4.1 0.0 collective-permute-start
  4.2 3.9 %collective-permute-start.4 = (s32[2,256]{1,0:T(2,128)S(1)}, s32[2,256]{1,0:T(2,128)S(1)}, u32[]{:S(2)}, u32[]{:S(2)}) collective-permute-start(s32[2,256]{1,0:T(2,128)S(1)} %get-tuple-element.27), channel_id=1, source_target_pairs={{0,4},{2,6},{4,0},{5,9},{6,2},{7,11},{8,12},{9,5},{10,14},{11,7},{... | collective-permute-start | bytes 6152 | tf_op jit(solution)/shard_map/ppermute | solution.py:289
  8.0 0.0 collective-permute-done.2.core_ref
  8.0 1.3 %near.1 = (f32[32,256]{1,0:T(8,128)S(1)}, bf16[2,96,512]{2,1,0:T(8,128)(2,1)S(1)}, bf16[256,512]{1,0:T(8,128)(2,1)S(1)}, bf16[256,512]{1,0:T(8,128)(2,1)S(1)}) custom-call(f32[136,128]{1,0:T(8,128)S(1)} %get-tuple-element.19.packed_ref, f32[136,128]{1,0:T(8,128)S(1)} %collective-permute-done.2.core_ref, f32[1024,128]{1,0:T(8,128)} %bitcast.9), custom_call_target="tpu_custom_call" | custom-call | flops 2000000000 | tf_op jit(solution)/shard_map/near/pallas_call | solution.py:294
  9.3 0.0 collective-permute-done.1.both_ref
  9.4 0.0 collective-permute-done.y_ref
  9.4 1.3 %coarse.1 = (f32[8,2,16,128]{3,2,1,0:T(8,128)}, bf16[2,96,512]{2,1,0:T(8,128)(2,1)S(1)}) custom-call(f32[136,128]{1,0:T(8,128)S(1)} %collective-permute-done.y_ref, f32[136,128]{1,0:T(8,128)S(1)} %collective-permute-done.1.both_ref, f32[32,256]{1,0:T(8,128)S(1)} %get-tuple-element.20.rhs_ref, bf16[256,512]{1,0:T(8,128)(2,1)S(1)} %get-tuple-element.21.hi_ref, ...), custom_call_target="tpu_custom_call" | custom-call | flops 8000000000 | tf_op jit(solution)/shard_map/coarse/pallas_call | solution.py:309
  10.7 6.0 %all-to-all-start = ((f32[16,16,128]{2,1,0:T(8,128)}), f32[16,16,128]{2,1,0:T(8,128)S(1)}, u32[]{:S(2)}, u32[]{:S(2)}) async-start(f32[16,16,128]{2,1,0:T(8,128)} %bitcast.3), calls=%async_computation | async-start | bytes 262144 | tf_op jit(solution)/shard_map/all_to_all | solution.py:323
  16.7 0.0 collective-permute-done.4.lists_ref
  16.7 0.3 %margins.1 = f32[32,256]{1,0:T(8,128)S(1)} custom-call(bf16[2,96,512]{2,1,0:T(8,128)(2,1)S(1)} %get-tuple-element.24.near_ref, bf16[2,96,512]{2,1,0:T(8,128)(2,1)S(1)} %get-tuple-element.25.far_ref, s32[2,256]{1,0:T(2,128)S(1)} %collective-permute-done.4.lists_ref), custom_call_target="tpu_custom_call" | custom-call | flops 4000000000 | tf_op jit(solution)/shard_map/margins/pallas_call | solution.py:326
  17.0 3.8 %collective-permute-start.5 = (f32[32,256]{1,0:T(8,128)S(1)}, f32[32,256]{1,0:T(8,128)S(1)}, u32[]{:S(2)}, u32[]{:S(2)}) collective-permute-start(f32[32,256]{1,0:T(8,128)S(1)} %margins.1), channel_id=1, source_target_pairs={{0,4},{2,6},{4,0},{5,9},{6,2},{7,11},{8,12},{9,5},{10,14},{11,7},{... | collective-permute-start | bytes 98312 | tf_op jit(solution)/shard_map/ppermute | solution.py:335
  20.9 2.7 %owned.1 = (f32[32,512]{1,0:T(8,128)S(1)}, bf16[2,256,512]{2,1,0:T(8,128)(2,1)S(1)}, bf16[2,256,512]{2,1,0:T(8,128)(2,1)S(1)}, bf16[256,512]{1,0:T(8,128)(2,1)S(1)}) custom-call(bf16[2,96,512]{2,1,0:T(8,128)(2,1)S(1)} %get-tuple-element.24.near_ref, bf16[2,96,512]{2,1,0:T(8,128)(2,1)S(1)} %get-tuple-element.25.far_ref, s32[1,512]{1,0:T(1,128)} %bitcast.8, ...), custom_call_target="tpu_custom_call" | custom-call | flops 40000000000 | tf_op jit(solution)/shard_map/owned/pallas_call | solution.py:337
  23.6 0.0 collective-permute-done.5.halo_ref
  23.6 0.2 mine.1
  23.8 0.0 collective-permute-start.6
  23.8 0.7 %all-to-all-done = f32[16,16,128]{2,1,0:T(8,128)S(1)} async-done(((f32[16,16,128]{2,1,0:T(8,128)}), f32[16,16,128]{2,1,0:T(8,128)S(1)}, u32[]{:S(2)}, u32[]{:S(2)}) %all-to-all-start) | async-done | bytes 131104 | tf_op jit(solution)/shard_map/all_to_all | solution.py:323
  24.5 0.1 collective-permute-start.3
  24.6 0.4 %collective-permute-done.6.halo_ref = f32[32,256]{1,0:T(8,128)S(1)} collective-permute-done((f32[32,256]{1,0:T(8,128)S(1)}, f32[32,256]{1,0:T(8,128)S(1)}, u32[]{:S(2)}, u32[]{:S(2)}) %collective-permute-start.6) | collective-permute-done | bytes 32800 | tf_op jit(solution)/shard_map/ppermute | solution.py:369
  25.0 0.2 other.1.total_ref
  25.2 0.6 %collective-permute-done.3.other_ref = f32[2,16,128]{2,1,0:T(8,128)S(1)} collective-permute-done((f32[2,16,128]{2,1,0:T(8,128)S(1)}, f32[2,16,128]{2,1,0:T(8,128)S(1)}, u32[]{:S(2)}, u32[]{:S(2)}) %collective-permute-start.3) | collective-permute-done | bytes 16416 | tf_op jit(solution)/shard_map/ppermute | solution.py:389
  25.8 0.9 %tail.1 = f32[32,512]{1,0:T(8,128)} custom-call(f32[2,16,128]{2,1,0:T(8,128)S(1)} %reduce.1.mine_ref, f32[2,16,128]{2,1,0:T(8,128)S(1)} %collective-permute-done.3.other_ref, bf16[256,512]{1,0:T(8,128)(2,1)S(1)} %get-tuple-element.26.hot_ref, f32[32,512]{1,0:T(8,128)S(1)} %other.1.total_ref), custom_call_target="tpu_custom_call" | custom-call | tf_op jit(solution)/shard_map/tail/pallas_call | solution.py:391
  (1 shorter events, 0.0 us)
Async XLA Ops:
  1.0 7.1 %collective-permute-start.2 = (f32[136,128]{1,0:T(8,128)S(1)}, f32[136,128]{1,0:T(8,128)S(1)}, u32[]{:S(2)}, u32[]{:S(2)}) collective-permute-start(f32[136,128]{1,0:T(8,128)S(1)} %get-tuple-element.19.packed_ref), channel_id=1, source_target_pairs={{0,1},{1,0},{2,3},{3,2},{4,5},{5,4},{6,7},{7,6},{8,9},{9,8},{10,11... | collective-permute-start | bytes 208904 | tf_op jit(solution)/shard_map/ppermute | solution.py:291
  1.5 7.9 %collective-permute-start.1 = (f32[136,128]{1,0:T(8,128)S(1)}, f32[136,128]{1,0:T(8,128)S(1)}, u32[]{:S(2)}, u32[]{:S(2)}) collective-permute-start(f32[136,128]{1,0:T(8,128)S(1)} %get-tuple-element.19.packed_ref), channel_id=1, source_target_pairs={{0,3},{1,2},{2,1},{3,0},{4,7},{5,6},{6,5},{7,4},{8,11},{9,10},{10,... | collective-permute-start | bytes 208904 | tf_op jit(solution)/shard_map/ppermute | solution.py:292
  4.1 5.2 %collective-permute-start = (f32[136,128]{1,0:T(8,128)S(1)}, f32[136,128]{1,0:T(8,128)S(1)}, u32[]{:S(2)}, u32[]{:S(2)}) collective-permute-start(f32[136,128]{1,0:T(8,128)S(1)} %get-tuple-element.19.packed_ref), channel_id=1, source_target_pairs={{0,2},{1,3},{2,0},{3,1},{4,6},{5,7},{6,4},{7,5},{8,10},{9,11},{10,... | collective-permute-start | bytes 208904 | tf_op jit(solution)/shard_map/ppermute | solution.py:290
  4.2 12.5 %collective-permute-start.4 = (s32[2,256]{1,0:T(2,128)S(1)}, s32[2,256]{1,0:T(2,128)S(1)}, u32[]{:S(2)}, u32[]{:S(2)}) collective-permute-start(s32[2,256]{1,0:T(2,128)S(1)} %get-tuple-element.27), channel_id=1, source_target_pairs={{0,4},{2,6},{4,0},{5,9},{6,2},{7,11},{8,12},{9,5},{10,14},{11,7},{... | collective-permute-start | bytes 6152 | tf_op jit(solution)/shard_map/ppermute | solution.py:289
  10.7 13.8 %all-to-all-start = ((f32[16,16,128]{2,1,0:T(8,128)}), f32[16,16,128]{2,1,0:T(8,128)S(1)}, u32[]{:S(2)}, u32[]{:S(2)}) async-start(f32[16,16,128]{2,1,0:T(8,128)} %bitcast.3), calls=%async_computation | async-start | bytes 262144 | tf_op jit(solution)/shard_map/all_to_all | solution.py:323
  17.0 6.5 %collective-permute-start.5 = (f32[32,256]{1,0:T(8,128)S(1)}, f32[32,256]{1,0:T(8,128)S(1)}, u32[]{:S(2)}, u32[]{:S(2)}) collective-permute-start(f32[32,256]{1,0:T(8,128)S(1)} %margins.1), channel_id=1, source_target_pairs={{0,4},{2,6},{4,0},{5,9},{6,2},{7,11},{8,12},{9,5},{10,14},{11,7},{... | collective-permute-start | bytes 98312 | tf_op jit(solution)/shard_map/ppermute | solution.py:335
  23.8 1.2 %collective-permute-start.6 = (f32[32,256]{1,0:T(8,128)S(1)}, f32[32,256]{1,0:T(8,128)S(1)}, u32[]{:S(2)}, u32[]{:S(2)}) collective-permute-start(f32[32,256]{1,0:T(8,128)S(1)} %get-tuple-element.31), channel_id=1, source_target_pairs={{0,1},{1,0},{2,3},{3,2},{4,5},{5,4},{6,7},{7,6},{8,9},{9,8},{10,11... | collective-permute-start | bytes 98312 | tf_op jit(solution)/shard_map/ppermute | solution.py:369
  24.5 1.2 %collective-permute-start.3 = (f32[2,16,128]{2,1,0:T(8,128)S(1)}, f32[2,16,128]{2,1,0:T(8,128)S(1)}, u32[]{:S(2)}, u32[]{:S(2)}) collective-permute-start(f32[2,16,128]{2,1,0:T(8,128)S(1)} %reduce.1.mine_ref), channel_id=1, source_target_pairs={{0,1},{1,0},{2,3},{3,2},{4,5},{5,4},{6,7},{7,6},{8,9},{9,8},{10,11... | collective-permute-start | bytes 49160 | tf_op jit(solution)/shard_map/ppermute | solution.py:389

commit v4 on v3

--- a/solution.py
+++ b/solution.py
@@ -62,12 +62,12 @@
 
 
 def pack_kernel(
-    residual_ref, agg_ref, lists_ref, counts_ref,
-    out_ref, lists_out,
+    residual_ref, agg_ref, lists_ref, counts_ref, coarse_ref,
+    out_ref, lists_out, coarse_out,
     residual_buf, agg_buf, lists_buf, counts_buf, sems,
 ):
-    sources = (residual_ref, agg_ref, lists_ref, counts_ref)
-    targets = (residual_buf, agg_buf, lists_buf, counts_buf)
+    sources = (residual_ref, agg_ref, lists_ref, counts_ref, coarse_ref)
+    targets = (residual_buf, agg_buf, lists_buf, counts_buf, coarse_out)
     fetches = [pltpu.make_async_copy(a, b, sems.at[k]) for k, (a, b) in enumerate(zip(sources, targets))]
     for fetch in fetches:
         fetch.start()
@@ -86,6 +86,7 @@
     for side in range(2):
         used = slots < counts_buf[:, side : side + 1]
         lists_out[side : side + 1] = jnp.where(used, lists_buf[side : side + 1], -1)
+    fetches[4].wait()
 
 
 def right_hand_side(rows, tiles, coarse_len, blocks, parts_ref):
@@ -101,17 +102,14 @@
 
 
 def near_kernel(
-    rows, tiles, packed_ref, core_ref, coarse_ref, rhs_ref, parts_ref, hi_ref, low_ref, coarse_buf, sem
+    rows, tiles, packed_ref, core_ref, coarse_ref, rhs_ref, parts_ref, hi_ref, low_ref
 ):
-    fetch = pltpu.make_async_copy(coarse_ref, coarse_buf, sem)
-    fetch.start()
     coarse_len = hi_ref.shape[0]
     rhs_ref[...] = right_hand_side(rows, tiles, coarse_len, (packed_ref, core_ref), parts_ref)
-    stride = coarse_buf.shape[0] // coarse_len
-    fetch.wait()
+    stride = coarse_ref.shape[0] // coarse_len
     for tile in range(stride):
         at = slice(tile * LANES, (tile + 1) * LANES)
-        hi_ref[:, at], low_ref[:, at] = split2(coarse_buf[pl.ds(tile, coarse_len, stride=stride), :])
+        hi_ref[:, at], low_ref[:, at] = split2(coarse_ref[pl.ds(tile, coarse_len, stride=stride), :])
 
 
 def coarse_kernel(
@@ -131,9 +129,8 @@
             turned = pltpu.roll(part, width, 1)
             left = jnp.where(lane < width, part[:half], turned[half:])
             right = jnp.where(lane < width, turned[:half], part[half:])
-            for copy in range(send_ref.shape[1]):
-                send_ref[to, copy] = left
-                send_ref[to + 1, copy] = right
+            send_ref[to] = left
+            send_ref[to + 1] = right
 
 
 def margin_kernel(near_ref, far_ref, lists_ref, out_ref):
@@ -213,18 +210,20 @@
     out_ref[...] = total
 
 
-def tail_kernel(width, mine_ref, other_ref, hot_ref, total_ref, out_ref):
-    chips, half, _ = mine_ref.shape
-    odd = lax.axis_index("blk") & 1
+def tail_kernel(width, mine_ref, core_ref, y_ref, both_ref, hot_ref, total_ref, out_ref):
+    half = mine_ref.shape[0]
+    place = lax.axis_index("blk")
+    odd, upper = (place & 1) == 1, place >= 2
     lane = lax.broadcasted_iota(jnp.int32, (half, LANES), 1)
-    top, bottom = [], []
-    for chip in range(chips):
-        mine, other = mine_ref[chip], other_ref[chip]
-        left = jnp.where(odd == 1, other, mine)
-        right = jnp.where(odd == 1, mine, other)
-        top.append(jnp.where(lane < width, left, pltpu.roll(right, width, 1)))
-        bottom.append(jnp.where(lane < width, pltpu.roll(left, width, 1), right))
-    coarse = jnp.concatenate([jnp.concatenate(top, axis=1), jnp.concatenate(bottom, axis=1)], axis=0)
+    tiles = []
+    for even_ref, odd_ref in ((mine_ref, core_ref), (y_ref, both_ref)):
+        this, that = even_ref[...], odd_ref[...]
+        left, right = jnp.where(odd, that, this), jnp.where(odd, this, that)
+        top = jnp.where(lane < width, left, pltpu.roll(right, width, 1))
+        bottom = jnp.where(lane < width, pltpu.roll(left, width, 1), right)
+        tiles.append(jnp.concatenate([top, bottom], axis=0))
+    first, second = jnp.where(upper, tiles[1], tiles[0]), jnp.where(upper, tiles[0], tiles[1])
+    coarse = jnp.concatenate([first, second], axis=1)
     out_ref[...] = total_ref[...] + fold3(dot(split3(coarse), hot_ref[...]))
 
 
@@ -252,7 +251,6 @@
     margin = wanted_rows.shape[2]
     coarse_len = coarse_inverse.shape[0]
     width = coarse_len // shards
-    chips = shards // 2
     packed_rows = -(-(rows * tiles + tiles) // 8) * 8
     core_swap = [(b, b ^ 1) for b in range(shards)]
     far_swap = [(b, b ^ 2) for b in range(shards)]
@@ -268,24 +266,25 @@
     table = coarse_inverse.reshape(-1, LANES)
     packed_shape = (packed_rows, LANES)
 
-    packed, lists = pl.pallas_call(
+    packed, lists, table = pl.pallas_call(
         pack_kernel,
         out_shape=(
             jax.ShapeDtypeStruct(packed_shape, F32),
             jax.ShapeDtypeStruct(lists.shape, jnp.int32),
+            jax.ShapeDtypeStruct(table.shape, F32),
         ),
-        in_specs=[whole(pl.ANY)] * 4,
-        out_specs=(whole(), whole()),
+        in_specs=[whole(pl.ANY)] * 5,
+        out_specs=(whole(),) * 3,
         scratch_shapes=[
             pltpu.VMEM(residual.shape, F32),
             pltpu.VMEM(codes.shape, jnp.int32),
             pltpu.VMEM(lists.shape, jnp.int32),
             pltpu.VMEM(wanted_count.shape, jnp.int32),
-            pltpu.SemaphoreType.DMA((4,)),
+            pltpu.SemaphoreType.DMA((5,)),
         ],
         compiler_params=limit(4),
         name="pack",
-    )(in_hbm(residual), in_hbm(codes), in_hbm(lists), in_hbm(wanted_count))
+    )(in_hbm(residual), in_hbm(codes), in_hbm(lists), in_hbm(wanted_count), in_hbm(table))
     lists = lax.ppermute(lists, ("sub", "blk"), neighbours)
     over_y = lax.ppermute(packed, "blk", far_swap)
     over_core = lax.ppermute(packed, "blk", core_swap)
@@ -299,17 +298,16 @@
             jax.ShapeDtypeStruct((coarse_len, subs * width), BF16),
             jax.ShapeDtypeStruct((coarse_len, subs * width), BF16),
         ),
-        in_specs=[whole(), whole(), whole(pl.ANY)],
+        in_specs=[whole()] * 3,
         out_specs=(whole(),) * 4,
-        scratch_shapes=[pltpu.VMEM(table.shape, F32), pltpu.SemaphoreType.DMA],
         compiler_params=limit(12),
         cost_estimate=weight(2 * 10**9),
         name="near",
-    )(packed, over_core, in_hbm(table))
+    )(packed, over_core, table)
     send, far = pl.pallas_call(
         functools.partial(coarse_kernel, width, rows, tiles),
         out_shape=(
-            jax.ShapeDtypeStruct((subs, chips, rows // 2, LANES), F32),
+            jax.ShapeDtypeStruct((subs, rows // 2, LANES), F32),
             jax.ShapeDtypeStruct((shards - 2, 3 * rows, cols), BF16),
         ),
         in_specs=[whole()] * 5,
@@ -318,10 +316,7 @@
         cost_estimate=weight(8 * 10**9),
         name="coarse",
     )(over_y, over_both, rhs, m_hi, m_low)
-    flat = send.reshape((subs * chips,) + send.shape[2:])
-    same_core = [[k for k in range(subs * shards) if k % 2 == core] for core in range(2)]
-    got = lax.all_to_all(flat, ("sub", "blk"), 0, 0, axis_index_groups=same_core, tiled=True)
-    got = got.reshape(send.shape)
+    got = lax.all_to_all(send, "sub", 0, 0, tiled=True)
 
     outgoing = pl.pallas_call(
         margin_kernel,
@@ -386,16 +381,16 @@
         cost_estimate=weight(10**8),
         name="reduce",
     )(got)
-    other_sums = lax.ppermute(sums, "blk", core_swap)
+    sums_over = [lax.ppermute(sums, "blk", swap) for swap in (core_swap, far_swap, both_swap)]
 
     return pl.pallas_call(
         functools.partial(tail_kernel, width),
         out_shape=jax.ShapeDtypeStruct((rows, cols), F32),
-        in_specs=[whole()] * 4,
+        in_specs=[whole()] * 6,
         out_specs=whole(),
         compiler_params=limit(12),
         name="tail",
-    )(sums, other_sums, hot, fine)
+    )(sums, *sums_over, hot, fine)
 
 
 def solution(mesh):

time: 27 us -> 29.5 us (1.093)
  starting transfers between devices: 17 us -> 19.1 us
  waiting for transfers between devices: 1.72 us -> 2.98 us
  Pallas kernels: 7.78 us -> 7.04 us
    ppermute x1 -> x3, waiting for transfers between devices: 0.6 us -> 2.95 us  [on_device(): lax.ppermute(sums, 'blk', swap)]
    ppermute x1 -> x3, starting transfers between devices: 0.07 us -> 2.19 us  [on_device(): lax.ppermute(sums, 'blk', swap)]
    pallas_call x1, Pallas kernels: 1.29 us -> 0.36 us  [on_device(): pl.pallas_call(functools.partial(near_kernel, rows, tiles), out_shape=(ja...]
    all_to_all x1, waiting for transfers between devices: 0.73 us -> 0.01 us  [on_device(): got = lax.all_to_all(send, 'sub', 0, 0, tiled=True)]
    ppermute x1, waiting for transfers between devices: 0.38 us -> 0.01 us  [on_device(): other = lax.ppermute(mine, 'blk', core_swap)]
  transfers between devices with their start and end apart: 8 -> 10, of which waited for: 3 -> 2; matrix products, arithmetic and copies ran while one was open for 0% -> 0% of each run, Pallas kernels for 22% -> 17%
where the time goes in v4:
time: 29.5 us; the launch traced here: 29.2 us
  starting transfers between devices  19.1 us (65%)
  Pallas kernels  7.04 us (24%)
  waiting for transfers between devices  2.98 us (10%)
    all_to_all x1, starting transfers between devices, on_device(): got = lax.all_to_all(send, 'sub', 0, 0, tiled=True)  5.9 us
    ppermute x1, starting transfers between devices, on_device(): halo = lax.ppermute(outgoing, ('sub', 'blk'), neighbours)  3.94 us
    ppermute x1, starting transfers between devices, on_device(): lists = lax.ppermute(lists, ('sub', 'blk'), neighbours)  3.85 us
    ppermute x3, waiting for transfers between devices, on_device(): lax.ppermute(sums, 'blk', swap)  2.95 us
    pallas_call x1, Pallas kernels, on_device(): pl.pallas_call(functools.partial(own_kernel, margin), out_shape=(jax.Shap...  2.67 us
    ppermute x1, starting transfers between devices, on_device(): over_both = lax.ppermute(packed, 'blk', both_swap)  2.64 us
    ppermute x3, starting transfers between devices, on_device(): lax.ppermute(sums, 'blk', swap)  2.19 us
    pallas_call x1, Pallas kernels, on_device(): pl.pallas_call(functools.partial(coarse_kernel, width, rows, tiles), out_...  1.28 us
  transfers between devices with their start and end apart: 10, of which 2 were waited for; matrix products, arithmetic and copies ran while one was open for 0% of the time, Pallas kernels for 17%

profile of v4, /device:TPU:0, one launch (start us, length us, event | category | flops | bytes accessed | tf_op | source)
XLA Modules:
  0.0 29.2 jit_solution(6561774143275310947)
XLA Ops:
  0.0 1.2 %pack.1 = (f32[136,128]{1,0:T(8,128)S(1)}, s32[2,256]{1,0:T(2,128)S(1)}, f32[1024,128]{1,0:T(8,128)S(1)}) custom-call(f32[32,512]{1,0:T(8,128)} %residual_ref.1, s32[1,512]{1,0:T(1,128)} %bitcast.5, s32[2,256]{1,0:T(2,128)} %bitcast.4, s32[1,2]{1,0:T(1,128)} %counts_ref.1, f32[1024,128]{1,0:T(8,128)} %bitcast.3), custom_call_target="tpu_custom_call" | custom-call | tf_op jit(solution)/shard_map/pack/pallas_call | solution.py:269
  1.2 0.5 %collective-permute-start.2 = (f32[136,128]{1,0:T(8,128)S(1)}, f32[136,128]{1,0:T(8,128)S(1)}, u32[]{:S(2)}, u32[]{:S(2)}) collective-permute-start(f32[136,128]{1,0:T(8,128)S(1)} %get-tuple-element.20.packed_ref), channel_id=1, source_target_pairs={{0,1},{1,0},{2,3},{3,2},{4,5},{5,4},{6,7},{7,6},{8,9},{9,8},{10,11... | collective-permute-start | bytes 208904 | tf_op jit(solution)/shard_map/ppermute | solution.py:290
  1.7 2.6 %collective-permute-start.1 = (f32[136,128]{1,0:T(8,128)S(1)}, f32[136,128]{1,0:T(8,128)S(1)}, u32[]{:S(2)}, u32[]{:S(2)}) collective-permute-start(f32[136,128]{1,0:T(8,128)S(1)} %get-tuple-element.20.packed_ref), channel_id=1, source_target_pairs={{0,3},{1,2},{2,1},{3,0},{4,7},{5,6},{6,5},{7,4},{8,11},{9,10},{10,... | collective-permute-start | bytes 208904 | tf_op jit(solution)/shard_map/ppermute | solution.py:291
  4.3 0.0 collective-permute-start
  4.4 3.9 %collective-permute-start.6 = (s32[2,256]{1,0:T(2,128)S(1)}, s32[2,256]{1,0:T(2,128)S(1)}, u32[]{:S(2)}, u32[]{:S(2)}) collective-permute-start(s32[2,256]{1,0:T(2,128)S(1)} %get-tuple-element.29), channel_id=1, source_target_pairs={{0,4},{2,6},{4,0},{5,9},{6,2},{7,11},{8,12},{9,5},{10,14},{11,7},{... | collective-permute-start | bytes 6152 | tf_op jit(solution)/shard_map/ppermute | solution.py:288
  8.2 0.0 collective-permute-done.2.core_ref
  8.3 0.4 %near.1 = (f32[32,256]{1,0:T(8,128)S(1)}, bf16[2,96,512]{2,1,0:T(8,128)(2,1)S(1)}, bf16[256,512]{1,0:T(8,128)(2,1)S(1)}, bf16[256,512]{1,0:T(8,128)(2,1)S(1)}) custom-call(f32[136,128]{1,0:T(8,128)S(1)} %get-tuple-element.20.packed_ref, f32[136,128]{1,0:T(8,128)S(1)} %collective-permute-done.2.core_ref, f32[1024,128]{1,0:T(8,128)S(1)} %get-tuple-element.21.coarse_ref), custom_call_target="tpu_custom_call" | custom-call | flops 2000000000 | tf_op jit(solution)/shard_map/near/pallas_call | solution.py:293
  8.6 0.0 collective-permute-done.1.both_ref
  8.6 0.0 collective-permute-done.y_ref
  8.7 1.3 %coarse.1 = (f32[8,16,128]{2,1,0:T(8,128)}, bf16[2,96,512]{2,1,0:T(8,128)(2,1)S(1)}) custom-call(f32[136,128]{1,0:T(8,128)S(1)} %collective-permute-done.y_ref, f32[136,128]{1,0:T(8,128)S(1)} %collective-permute-done.1.both_ref, f32[32,256]{1,0:T(8,128)S(1)} %get-tuple-element.22.rhs_ref, bf16[256,512]{1,0:T(8,128)(2,1)S(1)} %get-tuple-element.23.hi_ref, ...), custom_call_target="tpu_custom_call" | custom-call | flops 8000000000 | tf_op jit(solution)/shard_map/coarse/pallas_call | solution.py:307
  9.9 5.9 %all-to-all-start = ((f32[8,16,128]{2,1,0:T(8,128)}), f32[8,16,128]{2,1,0:T(8,128)S(1)}, u32[]{:S(2)}, u32[]{:S(2)}) async-start(f32[8,16,128]{2,1,0:T(8,128)} %get-tuple-element.25), calls=%async_computation | async-start | bytes 131072 | tf_op jit(solution)/shard_map/all_to_all | solution.py:319
  15.8 0.0 collective-permute-done.6.lists_ref
  15.8 0.3 %margins.1 = f32[32,256]{1,0:T(8,128)S(1)} custom-call(bf16[2,96,512]{2,1,0:T(8,128)(2,1)S(1)} %get-tuple-element.26.near_ref, bf16[2,96,512]{2,1,0:T(8,128)(2,1)S(1)} %get-tuple-element.27.far_ref, s32[2,256]{1,0:T(2,128)S(1)} %collective-permute-done.6.lists_ref), custom_call_target="tpu_custom_call" | custom-call | flops 4000000000 | tf_op jit(solution)/shard_map/margins/pallas_call | solution.py:321
  16.1 3.9 %collective-permute-start.7 = (f32[32,256]{1,0:T(8,128)S(1)}, f32[32,256]{1,0:T(8,128)S(1)}, u32[]{:S(2)}, u32[]{:S(2)}) collective-permute-start(f32[32,256]{1,0:T(8,128)S(1)} %margins.1), channel_id=1, source_target_pairs={{0,4},{2,6},{4,0},{5,9},{6,2},{7,11},{8,12},{9,5},{10,14},{11,7},{... | collective-permute-start | bytes 98312 | tf_op jit(solution)/shard_map/ppermute | solution.py:330
  20.1 2.7 %owned.1 = (f32[32,512]{1,0:T(8,128)S(1)}, bf16[2,256,512]{2,1,0:T(8,128)(2,1)S(1)}, bf16[2,256,512]{2,1,0:T(8,128)(2,1)S(1)}, bf16[256,512]{1,0:T(8,128)(2,1)S(1)}) custom-call(bf16[2,96,512]{2,1,0:T(8,128)(2,1)S(1)} %get-tuple-element.26.near_ref, bf16[2,96,512]{2,1,0:T(8,128)(2,1)S(1)} %get-tuple-element.27.far_ref, s32[1,512]{1,0:T(1,128)} %bitcast.6, ...), custom_call_target="tpu_custom_call" | custom-call | flops 40000000000 | tf_op jit(solution)/shard_map/owned/pallas_call | solution.py:332
  22.8 0.0 collective-permute-done.7.halo_ref
  22.8 0.2 mine.1
  23.0 0.0 collective-permute-start.8
  23.0 0.0 all-to-all-done.got_ref
  23.0 1.7 %collective-permute-start.5 = (f32[16,128]{1,0:T(8,128)S(1)}, f32[16,128]{1,0:T(8,128)S(1)}, u32[]{:S(2)}, u32[]{:S(2)}) collective-permute-start(f32[16,128]{1,0:T(8,128)S(1)} %reduce.1.mine_ref), channel_id=1, source_target_pairs={{0,3},{1,2},{2,1},{3,0},{4,7},{5,6},{6,5},{7,4},{8,11},{9,10},{10,... | collective-permute-start | bytes 24584 | tf_op jit(solution)/shard_map/ppermute | solution.py:384
  24.7 0.5 %collective-permute-start.4 = (f32[16,128]{1,0:T(8,128)S(1)}, f32[16,128]{1,0:T(8,128)S(1)}, u32[]{:S(2)}, u32[]{:S(2)}) collective-permute-start(f32[16,128]{1,0:T(8,128)S(1)} %reduce.1.mine_ref), channel_id=1, source_target_pairs={{0,2},{1,3},{2,0},{3,1},{4,6},{5,7},{6,4},{7,5},{8,10},{9,11},{10,... | collective-permute-start | bytes 24584 | tf_op jit(solution)/shard_map/ppermute | solution.py:384
  25.2 0.0 collective-permute-start.3
  25.2 0.0 collective-permute-done.8.halo_ref
  25.2 0.2 other.1.total_ref
  25.4 0.8 %collective-permute-done.5.both_ref = f32[16,128]{1,0:T(8,128)S(1)} collective-permute-done((f32[16,128]{1,0:T(8,128)S(1)}, f32[16,128]{1,0:T(8,128)S(1)}, u32[]{:S(2)}, u32[]{:S(2)}) %collective-permute-start.5) | collective-permute-done | bytes 8224 | tf_op jit(solution)/shard_map/ppermute | solution.py:384
  26.2 2.2 %collective-permute-done.4.y_ref = f32[16,128]{1,0:T(8,128)S(1)} collective-permute-done((f32[16,128]{1,0:T(8,128)S(1)}, f32[16,128]{1,0:T(8,128)S(1)}, u32[]{:S(2)}, u32[]{:S(2)}) %collective-permute-start.4) | collective-permute-done | bytes 8224 | tf_op jit(solution)/shard_map/ppermute | solution.py:384
  28.4 0.0 collective-permute-done.3.core_ref
  28.4 0.9 %tail.1 = f32[32,512]{1,0:T(8,128)} custom-call(f32[16,128]{1,0:T(8,128)S(1)} %reduce.1.mine_ref, f32[16,128]{1,0:T(8,128)S(1)} %collective-permute-done.3.core_ref, f32[16,128]{1,0:T(8,128)S(1)} %collective-permute-done.4.y_ref, f32[16,128]{1,0:T(8,128)S(1)} %collective-permute-done.5.both_ref, bf16[256,512]{1,0:T(8,128)(2,1)S(1)} %get-tuple-element.28.hot_ref, ...), custom_call_target="tpu_custom_call" | custom-call | tf_op jit(solution)/shard_map/tail/pallas_call | solution.py:386
  (1 shorter events, 0.0 us)
Async XLA Ops:
  1.2 7.1 %collective-permute-start.2 = (f32[136,128]{1,0:T(8,128)S(1)}, f32[136,128]{1,0:T(8,128)S(1)}, u32[]{:S(2)}, u32[]{:S(2)}) collective-permute-start(f32[136,128]{1,0:T(8,128)S(1)} %get-tuple-element.20.packed_ref), channel_id=1, source_target_pairs={{0,1},{1,0},{2,3},{3,2},{4,5},{5,4},{6,7},{7,6},{8,9},{9,8},{10,11... | collective-permute-start | bytes 208904 | tf_op jit(solution)/shard_map/ppermute | solution.py:290
  1.7 6.9 %collective-permute-start.1 = (f32[136,128]{1,0:T(8,128)S(1)}, f32[136,128]{1,0:T(8,128)S(1)}, u32[]{:S(2)}, u32[]{:S(2)}) collective-permute-start(f32[136,128]{1,0:T(8,128)S(1)} %get-tuple-element.20.packed_ref), channel_id=1, source_target_pairs={{0,3},{1,2},{2,1},{3,0},{4,7},{5,6},{6,5},{7,4},{8,11},{9,10},{10,... | collective-permute-start | bytes 208904 | tf_op jit(solution)/shard_map/ppermute | solution.py:291
  4.3 4.3 %collective-permute-start = (f32[136,128]{1,0:T(8,128)S(1)}, f32[136,128]{1,0:T(8,128)S(1)}, u32[]{:S(2)}, u32[]{:S(2)}) collective-permute-start(f32[136,128]{1,0:T(8,128)S(1)} %get-tuple-element.20.packed_ref), channel_id=1, source_target_pairs={{0,2},{1,3},{2,0},{3,1},{4,6},{5,7},{6,4},{7,5},{8,10},{9,11},{10,... | collective-permute-start | bytes 208904 | tf_op jit(solution)/shard_map/ppermute | solution.py:289
  4.4 11.4 %collective-permute-start.6 = (s32[2,256]{1,0:T(2,128)S(1)}, s32[2,256]{1,0:T(2,128)S(1)}, u32[]{:S(2)}, u32[]{:S(2)}) collective-permute-start(s32[2,256]{1,0:T(2,128)S(1)} %get-tuple-element.29), channel_id=1, source_target_pairs={{0,4},{2,6},{4,0},{5,9},{6,2},{7,11},{8,12},{9,5},{10,14},{11,7},{... | collective-permute-start | bytes 6152 | tf_op jit(solution)/shard_map/ppermute | solution.py:288
  9.9 13.1 %all-to-all-start = ((f32[8,16,128]{2,1,0:T(8,128)}), f32[8,16,128]{2,1,0:T(8,128)S(1)}, u32[]{:S(2)}, u32[]{:S(2)}) async-start(f32[8,16,128]{2,1,0:T(8,128)} %get-tuple-element.25), calls=%async_computation | async-start | bytes 131072 | tf_op jit(solution)/shard_map/all_to_all | solution.py:319
  16.1 6.6 %collective-permute-start.7 = (f32[32,256]{1,0:T(8,128)S(1)}, f32[32,256]{1,0:T(8,128)S(1)}, u32[]{:S(2)}, u32[]{:S(2)}) collective-permute-start(f32[32,256]{1,0:T(8,128)S(1)} %margins.1), channel_id=1, source_target_pairs={{0,4},{2,6},{4,0},{5,9},{6,2},{7,11},{8,12},{9,5},{10,14},{11,7},{... | collective-permute-start | bytes 98312 | tf_op jit(solution)/shard_map/ppermute | solution.py:330
  23.0 2.2 %collective-permute-start.8 = (f32[32,256]{1,0:T(8,128)S(1)}, f32[32,256]{1,0:T(8,128)S(1)}, u32[]{:S(2)}, u32[]{:S(2)}) collective-permute-start(f32[32,256]{1,0:T(8,128)S(1)} %get-tuple-element.33), channel_id=1, source_target_pairs={{0,1},{1,0},{2,3},{3,2},{4,5},{5,4},{6,7},{7,6},{8,9},{9,8},{10,11... | collective-permute-start | bytes 98312 | tf_op jit(solution)/shard_map/ppermute | solution.py:364
  23.0 3.1 %collective-permute-start.5 = (f32[16,128]{1,0:T(8,128)S(1)}, f32[16,128]{1,0:T(8,128)S(1)}, u32[]{:S(2)}, u32[]{:S(2)}) collective-permute-start(f32[16,128]{1,0:T(8,128)S(1)} %reduce.1.mine_ref), channel_id=1, source_target_pairs={{0,3},{1,2},{2,1},{3,0},{4,7},{5,6},{6,5},{7,4},{8,11},{9,10},{10,... | collective-permute-start | bytes 24584 | tf_op jit(solution)/shard_map/ppermute | solution.py:384
  24.7 3.7 %collective-permute-start.4 = (f32[16,128]{1,0:T(8,128)S(1)}, f32[16,128]{1,0:T(8,128)S(1)}, u32[]{:S(2)}, u32[]{:S(2)}) collective-permute-start(f32[16,128]{1,0:T(8,128)S(1)} %reduce.1.mine_ref), channel_id=1, source_target_pairs={{0,2},{1,3},{2,0},{3,1},{4,6},{5,7},{6,4},{7,5},{8,10},{9,11},{10,... | collective-permute-start | bytes 24584 | tf_op jit(solution)/shard_map/ppermute | solution.py:384
  25.2 3.1 %collective-permute-start.3 = (f32[16,128]{1,0:T(8,128)S(1)}, f32[16,128]{1,0:T(8,128)S(1)}, u32[]{:S(2)}, u32[]{:S(2)}) collective-permute-start(f32[16,128]{1,0:T(8,128)S(1)} %reduce.1.mine_ref), channel_id=1, source_target_pairs={{0,1},{1,0},{2,3},{3,2},{4,5},{5,4},{6,7},{7,6},{8,9},{9,8},{10,11... | collective-permute-start | bytes 24584 | tf_op jit(solution)/shard_map/ppermute | solution.py:384

commit v5 on v3

--- a/solution.py
+++ b/solution.py
@@ -62,12 +62,12 @@
 
 
 def pack_kernel(
-    residual_ref, agg_ref, lists_ref, counts_ref,
-    out_ref, lists_out,
+    residual_ref, agg_ref, lists_ref, counts_ref, coarse_ref,
+    out_ref, lists_out, coarse_out,
     residual_buf, agg_buf, lists_buf, counts_buf, sems,
 ):
-    sources = (residual_ref, agg_ref, lists_ref, counts_ref)
-    targets = (residual_buf, agg_buf, lists_buf, counts_buf)
+    sources = (residual_ref, agg_ref, lists_ref, counts_ref, coarse_ref)
+    targets = (residual_buf, agg_buf, lists_buf, counts_buf, coarse_out)
     fetches = [pltpu.make_async_copy(a, b, sems.at[k]) for k, (a, b) in enumerate(zip(sources, targets))]
     for fetch in fetches:
         fetch.start()
@@ -86,6 +86,7 @@
     for side in range(2):
         used = slots < counts_buf[:, side : side + 1]
         lists_out[side : side + 1] = jnp.where(used, lists_buf[side : side + 1], -1)
+    fetches[4].wait()
 
 
 def right_hand_side(rows, tiles, coarse_len, blocks, parts_ref):
@@ -101,17 +102,14 @@
 
 
 def near_kernel(
-    rows, tiles, packed_ref, core_ref, coarse_ref, rhs_ref, parts_ref, hi_ref, low_ref, coarse_buf, sem
+    rows, tiles, packed_ref, core_ref, coarse_ref, rhs_ref, parts_ref, hi_ref, low_ref
 ):
-    fetch = pltpu.make_async_copy(coarse_ref, coarse_buf, sem)
-    fetch.start()
     coarse_len = hi_ref.shape[0]
     rhs_ref[...] = right_hand_side(rows, tiles, coarse_len, (packed_ref, core_ref), parts_ref)
-    stride = coarse_buf.shape[0] // coarse_len
-    fetch.wait()
+    stride = coarse_ref.shape[0] // coarse_len
     for tile in range(stride):
         at = slice(tile * LANES, (tile + 1) * LANES)
-        hi_ref[:, at], low_ref[:, at] = split2(coarse_buf[pl.ds(tile, coarse_len, stride=stride), :])
+        hi_ref[:, at], low_ref[:, at] = split2(coarse_ref[pl.ds(tile, coarse_len, stride=stride), :])
 
 
 def coarse_kernel(
@@ -268,24 +266,25 @@
     table = coarse_inverse.reshape(-1, LANES)
     packed_shape = (packed_rows, LANES)
 
-    packed, lists = pl.pallas_call(
+    packed, lists, table = pl.pallas_call(
         pack_kernel,
         out_shape=(
             jax.ShapeDtypeStruct(packed_shape, F32),
             jax.ShapeDtypeStruct(lists.shape, jnp.int32),
+            jax.ShapeDtypeStruct(table.shape, F32),
         ),
-        in_specs=[whole(pl.ANY)] * 4,
-        out_specs=(whole(), whole()),
+        in_specs=[whole(pl.ANY)] * 5,
+        out_specs=(whole(),) * 3,
         scratch_shapes=[
             pltpu.VMEM(residual.shape, F32),
             pltpu.VMEM(codes.shape, jnp.int32),
             pltpu.VMEM(lists.shape, jnp.int32),
             pltpu.VMEM(wanted_count.shape, jnp.int32),
-            pltpu.SemaphoreType.DMA((4,)),
+            pltpu.SemaphoreType.DMA((5,)),
         ],
         compiler_params=limit(4),
         name="pack",
-    )(in_hbm(residual), in_hbm(codes), in_hbm(lists), in_hbm(wanted_count))
+    )(in_hbm(residual), in_hbm(codes), in_hbm(lists), in_hbm(wanted_count), in_hbm(table))
     lists = lax.ppermute(lists, ("sub", "blk"), neighbours)
     over_y = lax.ppermute(packed, "blk", far_swap)
     over_core = lax.ppermute(packed, "blk", core_swap)
@@ -299,13 +298,12 @@
             jax.ShapeDtypeStruct((coarse_len, subs * width), BF16),
             jax.ShapeDtypeStruct((coarse_len, subs * width), BF16),
         ),
-        in_specs=[whole(), whole(), whole(pl.ANY)],
+        in_specs=[whole()] * 3,
         out_specs=(whole(),) * 4,
-        scratch_shapes=[pltpu.VMEM(table.shape, F32), pltpu.SemaphoreType.DMA],
         compiler_params=limit(12),
         cost_estimate=weight(2 * 10**9),
         name="near",
-    )(packed, over_core, in_hbm(table))
+    )(packed, over_core, table)
     send, far = pl.pallas_call(
         functools.partial(coarse_kernel, width, rows, tiles),
         out_shape=(

time: 27 us -> 27.1 us (level)
  starting transfers between devices: 17 us -> 17.9 us
  Pallas kernels: 7.78 us -> 7.06 us
    pallas_call x1, Pallas kernels: 1.29 us -> 0.36 us  [on_device(): pl.pallas_call(functools.partial(near_kernel, rows, tiles), out_shape=(ja...]
    all_to_all x1, starting transfers between devices: 6.04 us -> 6.96 us  [on_device(): lax.all_to_all(flat, ('sub', 'blk'), 0, 0, axis_index_groups=same_core, t...]
  transfers between devices with their start and end apart: 8 -> 8, of which waited for: 3 -> 3; matrix products, arithmetic and copies ran while one was open for 0% -> 0% of each run, Pallas kernels for 22% -> 19%
where the time goes in v5:
time: 27.1 us; the launch traced here: 26.8 us
  starting transfers between devices  17.9 us (66%)
  Pallas kernels  7.06 us (26%)
  waiting for transfers between devices  1.74 us (6%)
    all_to_all x1, starting transfers between devices, on_device(): lax.all_to_all(flat, ('sub', 'blk'), 0, 0, axis_index_groups=same_core, t...  6.96 us
    ppermute x1, starting transfers between devices, on_device(): lists = lax.ppermute(lists, ('sub', 'blk'), neighbours)  3.85 us
    ppermute x1, starting transfers between devices, on_device(): halo = lax.ppermute(outgoing, ('sub', 'blk'), neighbours)  3.84 us
    pallas_call x1, Pallas kernels, on_device(): pl.pallas_call(functools.partial(own_kernel, margin), out_shape=(jax.Shap...  2.67 us
    ppermute x1, starting transfers between devices, on_device(): over_both = lax.ppermute(packed, 'blk', both_swap)  2.64 us
    pallas_call x1, Pallas kernels, on_device(): pl.pallas_call(functools.partial(coarse_kernel, width, rows, tiles), out_...  1.3 us
    pallas_call x1, Pallas kernels, on_device(): pl.pallas_call(pack_kernel, out_shape=(jax.ShapeDtypeStruct(packed_shape,...  1.17 us
    pallas_call x1, Pallas kernels, on_device(): pl.pallas_call(functools.partial(tail_kernel, width), out_shape=jax.Shape...  0.86 us
  transfers between devices with their start and end apart: 8, of which 3 were waited for; matrix products, arithmetic and copies ran while one was open for 0% of the time, Pallas kernels for 19%

profile of v5, /device:TPU:0, one launch (start us, length us, event | category | flops | bytes accessed | tf_op | source)
XLA Modules:
  0.0 26.8 jit_solution(17281307462872760994)
XLA Ops:
  0.0 1.2 %pack.1 = (f32[136,128]{1,0:T(8,128)S(1)}, s32[2,256]{1,0:T(2,128)S(1)}, f32[1024,128]{1,0:T(8,128)S(1)}) custom-call(f32[32,512]{1,0:T(8,128)} %residual_ref.1, s32[1,512]{1,0:T(1,128)} %bitcast.8, s32[2,256]{1,0:T(2,128)} %bitcast.7, s32[1,2]{1,0:T(1,128)} %counts_ref.1, f32[1024,128]{1,0:T(8,128)} %bitcast.6), custom_call_target="tpu_custom_call" | custom-call | tf_op jit(solution)/shard_map/pack/pallas_call | solution.py:269
  1.2 0.5 %collective-permute-start.2 = (f32[136,128]{1,0:T(8,128)S(1)}, f32[136,128]{1,0:T(8,128)S(1)}, u32[]{:S(2)}, u32[]{:S(2)}) collective-permute-start(f32[136,128]{1,0:T(8,128)S(1)} %get-tuple-element.20.packed_ref), channel_id=1, source_target_pairs={{0,1},{1,0},{2,3},{3,2},{4,5},{5,4},{6,7},{7,6},{8,9},{9,8},{10,11... | collective-permute-start | bytes 208904 | tf_op jit(solution)/shard_map/ppermute | solution.py:290
  1.7 2.6 %collective-permute-start.1 = (f32[136,128]{1,0:T(8,128)S(1)}, f32[136,128]{1,0:T(8,128)S(1)}, u32[]{:S(2)}, u32[]{:S(2)}) collective-permute-start(f32[136,128]{1,0:T(8,128)S(1)} %get-tuple-element.20.packed_ref), channel_id=1, source_target_pairs={{0,3},{1,2},{2,1},{3,0},{4,7},{5,6},{6,5},{7,4},{8,11},{9,10},{10,... | collective-permute-start | bytes 208904 | tf_op jit(solution)/shard_map/ppermute | solution.py:291
  4.3 0.0 collective-permute-start
  4.4 3.9 %collective-permute-start.4 = (s32[2,256]{1,0:T(2,128)S(1)}, s32[2,256]{1,0:T(2,128)S(1)}, u32[]{:S(2)}, u32[]{:S(2)}) collective-permute-start(s32[2,256]{1,0:T(2,128)S(1)} %get-tuple-element.29), channel_id=1, source_target_pairs={{0,4},{2,6},{4,0},{5,9},{6,2},{7,11},{8,12},{9,5},{10,14},{11,7},{... | collective-permute-start | bytes 6152 | tf_op jit(solution)/shard_map/ppermute | solution.py:288
  8.2 0.0 collective-permute-done.2.core_ref
  8.3 0.4 %near.1 = (f32[32,256]{1,0:T(8,128)S(1)}, bf16[2,96,512]{2,1,0:T(8,128)(2,1)S(1)}, bf16[256,512]{1,0:T(8,128)(2,1)S(1)}, bf16[256,512]{1,0:T(8,128)(2,1)S(1)}) custom-call(f32[136,128]{1,0:T(8,128)S(1)} %get-tuple-element.20.packed_ref, f32[136,128]{1,0:T(8,128)S(1)} %collective-permute-done.2.core_ref, f32[1024,128]{1,0:T(8,128)S(1)} %get-tuple-element.21.coarse_ref), custom_call_target="tpu_custom_call" | custom-call | flops 2000000000 | tf_op jit(solution)/shard_map/near/pallas_call | solution.py:293
  8.6 0.0 collective-permute-done.1.both_ref
  8.6 0.0 collective-permute-done.y_ref
  8.7 1.3 %coarse.1 = (f32[8,2,16,128]{3,2,1,0:T(8,128)}, bf16[2,96,512]{2,1,0:T(8,128)(2,1)S(1)}) custom-call(f32[136,128]{1,0:T(8,128)S(1)} %collective-permute-done.y_ref, f32[136,128]{1,0:T(8,128)S(1)} %collective-permute-done.1.both_ref, f32[32,256]{1,0:T(8,128)S(1)} %get-tuple-element.22.rhs_ref, bf16[256,512]{1,0:T(8,128)(2,1)S(1)} %get-tuple-element.23.hi_ref, ...), custom_call_target="tpu_custom_call" | custom-call | flops 8000000000 | tf_op jit(solution)/shard_map/coarse/pallas_call | solution.py:307
  10.0 7.0 %all-to-all-start = ((f32[16,16,128]{2,1,0:T(8,128)}), f32[16,16,128]{2,1,0:T(8,128)S(1)}, u32[]{:S(2)}, u32[]{:S(2)}) async-start(f32[16,16,128]{2,1,0:T(8,128)} %bitcast.3), calls=%async_computation | async-start | bytes 262144 | tf_op jit(solution)/shard_map/all_to_all | solution.py:321
  16.9 0.0 collective-permute-done.4.lists_ref
  16.9 0.3 %margins.1 = f32[32,256]{1,0:T(8,128)S(1)} custom-call(bf16[2,96,512]{2,1,0:T(8,128)(2,1)S(1)} %get-tuple-element.26.near_ref, bf16[2,96,512]{2,1,0:T(8,128)(2,1)S(1)} %get-tuple-element.27.far_ref, s32[2,256]{1,0:T(2,128)S(1)} %collective-permute-done.4.lists_ref), custom_call_target="tpu_custom_call" | custom-call | flops 4000000000 | tf_op jit(solution)/shard_map/margins/pallas_call | solution.py:324
  17.2 3.8 %collective-permute-start.5 = (f32[32,256]{1,0:T(8,128)S(1)}, f32[32,256]{1,0:T(8,128)S(1)}, u32[]{:S(2)}, u32[]{:S(2)}) collective-permute-start(f32[32,256]{1,0:T(8,128)S(1)} %margins.1), channel_id=1, source_target_pairs={{0,4},{2,6},{4,0},{5,9},{6,2},{7,11},{8,12},{9,5},{10,14},{11,7},{... | collective-permute-start | bytes 98312 | tf_op jit(solution)/shard_map/ppermute | solution.py:333
  21.1 2.7 %owned.1 = (f32[32,512]{1,0:T(8,128)S(1)}, bf16[2,256,512]{2,1,0:T(8,128)(2,1)S(1)}, bf16[2,256,512]{2,1,0:T(8,128)(2,1)S(1)}, bf16[256,512]{1,0:T(8,128)(2,1)S(1)}) custom-call(bf16[2,96,512]{2,1,0:T(8,128)(2,1)S(1)} %get-tuple-element.26.near_ref, bf16[2,96,512]{2,1,0:T(8,128)(2,1)S(1)} %get-tuple-element.27.far_ref, s32[1,512]{1,0:T(1,128)} %bitcast.9, ...), custom_call_target="tpu_custom_call" | custom-call | flops 40000000000 | tf_op jit(solution)/shard_map/owned/pallas_call | solution.py:335
  23.8 0.0 collective-permute-done.5.halo_ref
  23.8 0.2 mine.1
  24.0 0.0 collective-permute-start.6
  24.0 0.7 %all-to-all-done = f32[16,16,128]{2,1,0:T(8,128)S(1)} async-done(((f32[16,16,128]{2,1,0:T(8,128)}), f32[16,16,128]{2,1,0:T(8,128)S(1)}, u32[]{:S(2)}, u32[]{:S(2)}) %all-to-all-start) | async-done | bytes 131104 | tf_op jit(solution)/shard_map/all_to_all | solution.py:321
  24.7 0.1 collective-permute-start.3
  24.8 0.4 %collective-permute-done.6.halo_ref = f32[32,256]{1,0:T(8,128)S(1)} collective-permute-done((f32[32,256]{1,0:T(8,128)S(1)}, f32[32,256]{1,0:T(8,128)S(1)}, u32[]{:S(2)}, u32[]{:S(2)}) %collective-permute-start.6) | collective-permute-done | bytes 32800 | tf_op jit(solution)/shard_map/ppermute | solution.py:367
  25.2 0.2 other.1.total_ref
  25.4 0.6 %collective-permute-done.3.other_ref = f32[2,16,128]{2,1,0:T(8,128)S(1)} collective-permute-done((f32[2,16,128]{2,1,0:T(8,128)S(1)}, f32[2,16,128]{2,1,0:T(8,128)S(1)}, u32[]{:S(2)}, u32[]{:S(2)}) %collective-permute-start.3) | collective-permute-done | bytes 16416 | tf_op jit(solution)/shard_map/ppermute | solution.py:387
  26.0 0.9 %tail.1 = f32[32,512]{1,0:T(8,128)} custom-call(f32[2,16,128]{2,1,0:T(8,128)S(1)} %reduce.1.mine_ref, f32[2,16,128]{2,1,0:T(8,128)S(1)} %collective-permute-done.3.other_ref, bf16[256,512]{1,0:T(8,128)(2,1)S(1)} %get-tuple-element.28.hot_ref, f32[32,512]{1,0:T(8,128)S(1)} %other.1.total_ref), custom_call_target="tpu_custom_call" | custom-call | tf_op jit(solution)/shard_map/tail/pallas_call | solution.py:389
  (1 shorter events, 0.0 us)
Async XLA Ops:
  1.2 7.1 %collective-permute-start.2 = (f32[136,128]{1,0:T(8,128)S(1)}, f32[136,128]{1,0:T(8,128)S(1)}, u32[]{:S(2)}, u32[]{:S(2)}) collective-permute-start(f32[136,128]{1,0:T(8,128)S(1)} %get-tuple-element.20.packed_ref), channel_id=1, source_target_pairs={{0,1},{1,0},{2,3},{3,2},{4,5},{5,4},{6,7},{7,6},{8,9},{9,8},{10,11... | collective-permute-start | bytes 208904 | tf_op jit(solution)/shard_map/ppermute | solution.py:290
  1.7 6.9 %collective-permute-start.1 = (f32[136,128]{1,0:T(8,128)S(1)}, f32[136,128]{1,0:T(8,128)S(1)}, u32[]{:S(2)}, u32[]{:S(2)}) collective-permute-start(f32[136,128]{1,0:T(8,128)S(1)} %get-tuple-element.20.packed_ref), channel_id=1, source_target_pairs={{0,3},{1,2},{2,1},{3,0},{4,7},{5,6},{6,5},{7,4},{8,11},{9,10},{10,... | collective-permute-start | bytes 208904 | tf_op jit(solution)/shard_map/ppermute | solution.py:291
  4.3 4.3 %collective-permute-start = (f32[136,128]{1,0:T(8,128)S(1)}, f32[136,128]{1,0:T(8,128)S(1)}, u32[]{:S(2)}, u32[]{:S(2)}) collective-permute-start(f32[136,128]{1,0:T(8,128)S(1)} %get-tuple-element.20.packed_ref), channel_id=1, source_target_pairs={{0,2},{1,3},{2,0},{3,1},{4,6},{5,7},{6,4},{7,5},{8,10},{9,11},{10,... | collective-permute-start | bytes 208904 | tf_op jit(solution)/shard_map/ppermute | solution.py:289
  4.4 12.5 %collective-permute-start.4 = (s32[2,256]{1,0:T(2,128)S(1)}, s32[2,256]{1,0:T(2,128)S(1)}, u32[]{:S(2)}, u32[]{:S(2)}) collective-permute-start(s32[2,256]{1,0:T(2,128)S(1)} %get-tuple-element.29), channel_id=1, source_target_pairs={{0,4},{2,6},{4,0},{5,9},{6,2},{7,11},{8,12},{9,5},{10,14},{11,7},{... | collective-permute-start | bytes 6152 | tf_op jit(solution)/shard_map/ppermute | solution.py:288
  10.0 14.8 %all-to-all-start = ((f32[16,16,128]{2,1,0:T(8,128)}), f32[16,16,128]{2,1,0:T(8,128)S(1)}, u32[]{:S(2)}, u32[]{:S(2)}) async-start(f32[16,16,128]{2,1,0:T(8,128)} %bitcast.3), calls=%async_computation | async-start | bytes 262144 | tf_op jit(solution)/shard_map/all_to_all | solution.py:321
  17.2 6.5 %collective-permute-start.5 = (f32[32,256]{1,0:T(8,128)S(1)}, f32[32,256]{1,0:T(8,128)S(1)}, u32[]{:S(2)}, u32[]{:S(2)}) collective-permute-start(f32[32,256]{1,0:T(8,128)S(1)} %margins.1), channel_id=1, source_target_pairs={{0,4},{2,6},{4,0},{5,9},{6,2},{7,11},{8,12},{9,5},{10,14},{11,7},{... | collective-permute-start | bytes 98312 | tf_op jit(solution)/shard_map/ppermute | solution.py:333
  24.0 1.2 %collective-permute-start.6 = (f32[32,256]{1,0:T(8,128)S(1)}, f32[32,256]{1,0:T(8,128)S(1)}, u32[]{:S(2)}, u32[]{:S(2)}) collective-permute-start(f32[32,256]{1,0:T(8,128)S(1)} %get-tuple-element.33), channel_id=1, source_target_pairs={{0,1},{1,0},{2,3},{3,2},{4,5},{5,4},{6,7},{7,6},{8,9},{9,8},{10,11... | collective-permute-start | bytes 98312 | tf_op jit(solution)/shard_map/ppermute | solution.py:367
  24.7 1.2 %collective-permute-start.3 = (f32[2,16,128]{2,1,0:T(8,128)S(1)}, f32[2,16,128]{2,1,0:T(8,128)S(1)}, u32[]{:S(2)}, u32[]{:S(2)}) collective-permute-start(f32[2,16,128]{2,1,0:T(8,128)S(1)} %reduce.1.mine_ref), channel_id=1, source_target_pairs={{0,1},{1,0},{2,3},{3,2},{4,5},{5,4},{6,7},{7,6},{8,9},{9,8},{10,11... | collective-permute-start | bytes 49160 | tf_op jit(solution)/shard_map/ppermute | solution.py:387

commit v6 on v5

--- a/solution.py
+++ b/solution.py
@@ -130,8 +130,10 @@
             left = jnp.where(lane < width, part[:half], turned[half:])
             right = jnp.where(lane < width, turned[:half], part[half:])
             for copy in range(send_ref.shape[1]):
-                send_ref[to, copy] = left
-                send_ref[to + 1, copy] = right
+                for core in range(2):
+                    piece = slice(core * half // 2, (core + 1) * half // 2)
+                    send_ref[to, copy, core] = left[piece]
+                    send_ref[to + 1, copy, core] = right[piece]
 
 
 def margin_kernel(near_ref, far_ref, lists_ref, out_ref):
@@ -212,14 +214,15 @@
 
 
 def tail_kernel(width, mine_ref, other_ref, hot_ref, total_ref, out_ref):
-    chips, half, _ = mine_ref.shape
-    odd = lax.axis_index("blk") & 1
-    lane = lax.broadcasted_iota(jnp.int32, (half, LANES), 1)
+    odd = (lax.axis_index("blk") & 1) == 1
+    chunks = []
+    for k in range(mine_ref.shape[0]):
+        mine, other = mine_ref[k], other_ref[k]
+        pieces = [jnp.where(odd, other, mine), jnp.where(odd, mine, other)]
+        chunks.append(jnp.concatenate(pieces, axis=0))
+    lane = lax.broadcasted_iota(jnp.int32, chunks[0].shape, 1)
     top, bottom = [], []
-    for chip in range(chips):
-        mine, other = mine_ref[chip], other_ref[chip]
-        left = jnp.where(odd == 1, other, mine)
-        right = jnp.where(odd == 1, mine, other)
+    for left, right in zip(chunks[::2], chunks[1::2]):
         top.append(jnp.where(lane < width, left, pltpu.roll(right, width, 1)))
         bottom.append(jnp.where(lane < width, pltpu.roll(left, width, 1), right))
     coarse = jnp.concatenate([jnp.concatenate(top, axis=1), jnp.concatenate(bottom, axis=1)], axis=0)
@@ -307,7 +310,7 @@
     send, far = pl.pallas_call(
         functools.partial(coarse_kernel, width, rows, tiles),
         out_shape=(
-            jax.ShapeDtypeStruct((subs, chips, rows // 2, LANES), F32),
+            jax.ShapeDtypeStruct((subs, chips, 2, rows // 4, LANES), F32),
             jax.ShapeDtypeStruct((shards - 2, 3 * rows, cols), BF16),
         ),
         in_specs=[whole()] * 5,
@@ -316,10 +319,9 @@
         cost_estimate=weight(8 * 10**9),
         name="coarse",
     )(over_y, over_both, rhs, m_hi, m_low)
-    flat = send.reshape((subs * chips,) + send.shape[2:])
-    same_core = [[k for k in range(subs * shards) if k % 2 == core] for core in range(2)]
-    got = lax.all_to_all(flat, ("sub", "blk"), 0, 0, axis_index_groups=same_core, tiled=True)
-    got = got.reshape(send.shape)
+    flat = send.reshape((subs * shards,) + send.shape[3:])
+    got = lax.all_to_all(flat, ("sub", "blk"), 0, 0, tiled=True)
+    got = got.reshape((subs, shards) + flat.shape[1:])
 
     outgoing = pl.pallas_call(
         margin_kernel,

time: 27.1 us -> 26.5 us (0.978)
  starting transfers between devices: 17.9 us -> 17 us
  waiting for transfers between devices: 1.74 us -> 2.12 us
    all_to_all x1, starting transfers between devices: 6.96 us -> 5.94 us  [on_device(): got = lax.all_to_all(flat, ('sub', 'blk'), 0, 0, tiled=True)]
    all_to_all x1, waiting for transfers between devices: 0.73 us -> 1.31 us  [on_device(): got = lax.all_to_all(flat, ('sub', 'blk'), 0, 0, tiled=True)]
    ppermute x1, waiting for transfers between devices: 0.38 us -> 0.01 us  [on_device(): other = lax.ppermute(mine, 'blk', core_swap)]
  transfers between devices with their start and end apart: 8 -> 8, of which waited for: 3 -> 2; matrix products, arithmetic and copies ran while one was open for 0% -> 0% of each run, Pallas kernels for 19% -> 19%
where the time goes in v6:
time: 26.5 us; the launch traced here: 26.3 us
  starting transfers between devices  17 us (64%)
  Pallas kernels  7.06 us (27%)
  waiting for transfers between devices  2.12 us (8%)
    all_to_all x1, starting transfers between devices, on_device(): got = lax.all_to_all(flat, ('sub', 'blk'), 0, 0, tiled=True)  5.94 us
    ppermute x1, starting transfers between devices, on_device(): lists = lax.ppermute(lists, ('sub', 'blk'), neighbours)  3.85 us
    ppermute x1, starting transfers between devices, on_device(): halo = lax.ppermute(outgoing, ('sub', 'blk'), neighbours)  3.69 us
    pallas_call x1, Pallas kernels, on_device(): pl.pallas_call(functools.partial(own_kernel, margin), out_shape=(jax.Shap...  2.67 us
    ppermute x1, starting transfers between devices, on_device(): over_both = lax.ppermute(packed, 'blk', both_swap)  2.64 us
    all_to_all x1, waiting for transfers between devices, on_device(): got = lax.all_to_all(flat, ('sub', 'blk'), 0, 0, tiled=True)  1.31 us
    pallas_call x1, Pallas kernels, on_device(): pl.pallas_call(functools.partial(coarse_kernel, width, rows, tiles), out_...  1.3 us
    pallas_call x1, Pallas kernels, on_device(): pl.pallas_call(pack_kernel, out_shape=(jax.ShapeDtypeStruct(packed_shape,...  1.17 us
  transfers between devices with their start and end apart: 8, of which 2 were waited for; matrix products, arithmetic and copies ran while one was open for 0% of the time, Pallas kernels for 19%

profile of v6, /device:TPU:0, one launch (start us, length us, event | category | flops | bytes accessed | tf_op | source)
XLA Modules:
  0.0 26.3 jit_solution(16529242304480136051)
XLA Ops:
  0.0 1.2 %pack.1 = (f32[136,128]{1,0:T(8,128)S(1)}, s32[2,256]{1,0:T(2,128)S(1)}, f32[1024,128]{1,0:T(8,128)S(1)}) custom-call(f32[32,512]{1,0:T(8,128)} %residual_ref.1, s32[1,512]{1,0:T(1,128)} %bitcast.8, s32[2,256]{1,0:T(2,128)} %bitcast.7, s32[1,2]{1,0:T(1,128)} %counts_ref.1, f32[1024,128]{1,0:T(8,128)} %bitcast.6), custom_call_target="tpu_custom_call" | custom-call | tf_op jit(solution)/shard_map/pack/pallas_call | solution.py:272
  1.2 0.5 %collective-permute-start.2 = (f32[136,128]{1,0:T(8,128)S(1)}, f32[136,128]{1,0:T(8,128)S(1)}, u32[]{:S(2)}, u32[]{:S(2)}) collective-permute-start(f32[136,128]{1,0:T(8,128)S(1)} %get-tuple-element.20.packed_ref), channel_id=1, source_target_pairs={{0,1},{1,0},{2,3},{3,2},{4,5},{5,4},{6,7},{7,6},{8,9},{9,8},{10,11... | collective-permute-start | bytes 208904 | tf_op jit(solution)/shard_map/ppermute | solution.py:293
  1.7 2.6 %collective-permute-start.1 = (f32[136,128]{1,0:T(8,128)S(1)}, f32[136,128]{1,0:T(8,128)S(1)}, u32[]{:S(2)}, u32[]{:S(2)}) collective-permute-start(f32[136,128]{1,0:T(8,128)S(1)} %get-tuple-element.20.packed_ref), channel_id=1, source_target_pairs={{0,3},{1,2},{2,1},{3,0},{4,7},{5,6},{6,5},{7,4},{8,11},{9,10},{10,... | collective-permute-start | bytes 208904 | tf_op jit(solution)/shard_map/ppermute | solution.py:294
  4.3 0.0 collective-permute-start
  4.4 3.9 %collective-permute-start.4 = (s32[2,256]{1,0:T(2,128)S(1)}, s32[2,256]{1,0:T(2,128)S(1)}, u32[]{:S(2)}, u32[]{:S(2)}) collective-permute-start(s32[2,256]{1,0:T(2,128)S(1)} %get-tuple-element.29), channel_id=1, source_target_pairs={{0,4},{2,6},{4,0},{5,9},{6,2},{7,11},{8,12},{9,5},{10,14},{11,7},{... | collective-permute-start | bytes 6152 | tf_op jit(solution)/shard_map/ppermute | solution.py:291
  8.2 0.0 collective-permute-done.2.core_ref
  8.3 0.4 %near.1 = (f32[32,256]{1,0:T(8,128)S(1)}, bf16[2,96,512]{2,1,0:T(8,128)(2,1)S(1)}, bf16[256,512]{1,0:T(8,128)(2,1)S(1)}, bf16[256,512]{1,0:T(8,128)(2,1)S(1)}) custom-call(f32[136,128]{1,0:T(8,128)S(1)} %get-tuple-element.20.packed_ref, f32[136,128]{1,0:T(8,128)S(1)} %collective-permute-done.2.core_ref, f32[1024,128]{1,0:T(8,128)S(1)} %get-tuple-element.21.coarse_ref), custom_call_target="tpu_custom_call" | custom-call | flops 2000000000 | tf_op jit(solution)/shard_map/near/pallas_call | solution.py:296
  8.6 0.0 collective-permute-done.1.both_ref
  8.6 0.0 collective-permute-done.y_ref
  8.7 1.3 %coarse.1 = (f32[8,2,2,8,128]{4,3,2,1,0:T(8,128)}, bf16[2,96,512]{2,1,0:T(8,128)(2,1)S(1)}) custom-call(f32[136,128]{1,0:T(8,128)S(1)} %collective-permute-done.y_ref, f32[136,128]{1,0:T(8,128)S(1)} %collective-permute-done.1.both_ref, f32[32,256]{1,0:T(8,128)S(1)} %get-tuple-element.22.rhs_ref, bf16[256,512]{1,0:T(8,128)(2,1)S(1)} %get-tuple-element.23.hi_ref, ...), custom_call_target="tpu_custom_call" | custom-call | flops 8000000000 | tf_op jit(solution)/shard_map/coarse/pallas_call | solution.py:310
  10.0 5.9 %all-to-all-start = ((f32[32,8,128]{2,1,0:T(8,128)}), f32[32,8,128]{2,1,0:T(8,128)S(1)}, u32[]{:S(2)}, u32[]{:S(2)}) async-start(f32[32,8,128]{2,1,0:T(8,128)} %bitcast.3), calls=%async_computation | async-start | bytes 262144 | tf_op jit(solution)/shard_map/all_to_all | solution.py:323
  15.9 0.0 collective-permute-done.4.lists_ref
  15.9 0.3 %margins.1 = f32[32,256]{1,0:T(8,128)S(1)} custom-call(bf16[2,96,512]{2,1,0:T(8,128)(2,1)S(1)} %get-tuple-element.26.near_ref, bf16[2,96,512]{2,1,0:T(8,128)(2,1)S(1)} %get-tuple-element.27.far_ref, s32[2,256]{1,0:T(2,128)S(1)} %collective-permute-done.4.lists_ref), custom_call_target="tpu_custom_call" | custom-call | flops 4000000000 | tf_op jit(solution)/shard_map/margins/pallas_call | solution.py:326
  16.2 3.7 %collective-permute-start.5 = (f32[32,256]{1,0:T(8,128)S(1)}, f32[32,256]{1,0:T(8,128)S(1)}, u32[]{:S(2)}, u32[]{:S(2)}) collective-permute-start(f32[32,256]{1,0:T(8,128)S(1)} %margins.1), channel_id=1, source_target_pairs={{0,4},{2,6},{4,0},{5,9},{6,2},{7,11},{8,12},{9,5},{10,14},{11,7},{... | collective-permute-start | bytes 98312 | tf_op jit(solution)/shard_map/ppermute | solution.py:335
  19.9 2.7 %owned.1 = (f32[32,512]{1,0:T(8,128)S(1)}, bf16[2,256,512]{2,1,0:T(8,128)(2,1)S(1)}, bf16[2,256,512]{2,1,0:T(8,128)(2,1)S(1)}, bf16[256,512]{1,0:T(8,128)(2,1)S(1)}) custom-call(bf16[2,96,512]{2,1,0:T(8,128)(2,1)S(1)} %get-tuple-element.26.near_ref, bf16[2,96,512]{2,1,0:T(8,128)(2,1)S(1)} %get-tuple-element.27.far_ref, s32[1,512]{1,0:T(1,128)} %bitcast.9, ...), custom_call_target="tpu_custom_call" | custom-call | flops 40000000000 | tf_op jit(solution)/shard_map/owned/pallas_call | solution.py:337
  22.6 0.0 collective-permute-done.5.halo_ref
  22.6 0.2 mine.1
  22.8 0.0 collective-permute-start.6
  22.8 1.3 %all-to-all-done = f32[32,8,128]{2,1,0:T(8,128)S(1)} async-done(((f32[32,8,128]{2,1,0:T(8,128)}), f32[32,8,128]{2,1,0:T(8,128)S(1)}, u32[]{:S(2)}, u32[]{:S(2)}) %all-to-all-start) | async-done | bytes 131104 | tf_op jit(solution)/shard_map/all_to_all | solution.py:323
  24.1 0.3 %collective-permute-start.3 = (f32[4,8,128]{2,1,0:T(8,128)S(1)}, f32[4,8,128]{2,1,0:T(8,128)S(1)}, u32[]{:S(2)}, u32[]{:S(2)}) collective-permute-start(f32[4,8,128]{2,1,0:T(8,128)S(1)} %reduce.1.mine_ref), channel_id=1, source_target_pairs={{0,1},{1,0},{2,3},{3,2},{4,5},{5,4},{6,7},{7,6},{8,9},{9,8},{10,11... | collective-permute-start | bytes 49160 | tf_op jit(solution)/shard_map/ppermute | solution.py:389
  24.4 0.0 collective-permute-done.6.halo_ref
  24.4 0.2 other.1.total_ref
  24.6 0.8 %collective-permute-done.3.other_ref = f32[4,8,128]{2,1,0:T(8,128)S(1)} collective-permute-done((f32[4,8,128]{2,1,0:T(8,128)S(1)}, f32[4,8,128]{2,1,0:T(8,128)S(1)}, u32[]{:S(2)}, u32[]{:S(2)}) %collective-permute-start.3) | collective-permute-done | bytes 16416 | tf_op jit(solution)/shard_map/ppermute | solution.py:389
  25.4 0.9 %tail.1 = f32[32,512]{1,0:T(8,128)} custom-call(f32[4,8,128]{2,1,0:T(8,128)S(1)} %reduce.1.mine_ref, f32[4,8,128]{2,1,0:T(8,128)S(1)} %collective-permute-done.3.other_ref, bf16[256,512]{1,0:T(8,128)(2,1)S(1)} %get-tuple-element.28.hot_ref, f32[32,512]{1,0:T(8,128)S(1)} %other.1.total_ref), custom_call_target="tpu_custom_call" | custom-call | tf_op jit(solution)/shard_map/tail/pallas_call | solution.py:391
  (1 shorter events, 0.0 us)
Async XLA Ops:
  1.2 7.1 %collective-permute-start.2 = (f32[136,128]{1,0:T(8,128)S(1)}, f32[136,128]{1,0:T(8,128)S(1)}, u32[]{:S(2)}, u32[]{:S(2)}) collective-permute-start(f32[136,128]{1,0:T(8,128)S(1)} %get-tuple-element.20.packed_ref), channel_id=1, source_target_pairs={{0,1},{1,0},{2,3},{3,2},{4,5},{5,4},{6,7},{7,6},{8,9},{9,8},{10,11... | collective-permute-start | bytes 208904 | tf_op jit(solution)/shard_map/ppermute | solution.py:293
  1.7 6.9 %collective-permute-start.1 = (f32[136,128]{1,0:T(8,128)S(1)}, f32[136,128]{1,0:T(8,128)S(1)}, u32[]{:S(2)}, u32[]{:S(2)}) collective-permute-start(f32[136,128]{1,0:T(8,128)S(1)} %get-tuple-element.20.packed_ref), channel_id=1, source_target_pairs={{0,3},{1,2},{2,1},{3,0},{4,7},{5,6},{6,5},{7,4},{8,11},{9,10},{10,... | collective-permute-start | bytes 208904 | tf_op jit(solution)/shard_map/ppermute | solution.py:294
  4.3 4.3 %collective-permute-start = (f32[136,128]{1,0:T(8,128)S(1)}, f32[136,128]{1,0:T(8,128)S(1)}, u32[]{:S(2)}, u32[]{:S(2)}) collective-permute-start(f32[136,128]{1,0:T(8,128)S(1)} %get-tuple-element.20.packed_ref), channel_id=1, source_target_pairs={{0,2},{1,3},{2,0},{3,1},{4,6},{5,7},{6,4},{7,5},{8,10},{9,11},{10,... | collective-permute-start | bytes 208904 | tf_op jit(solution)/shard_map/ppermute | solution.py:292
  4.4 11.5 %collective-permute-start.4 = (s32[2,256]{1,0:T(2,128)S(1)}, s32[2,256]{1,0:T(2,128)S(1)}, u32[]{:S(2)}, u32[]{:S(2)}) collective-permute-start(s32[2,256]{1,0:T(2,128)S(1)} %get-tuple-element.29), channel_id=1, source_target_pairs={{0,4},{2,6},{4,0},{5,9},{6,2},{7,11},{8,12},{9,5},{10,14},{11,7},{... | collective-permute-start | bytes 6152 | tf_op jit(solution)/shard_map/ppermute | solution.py:291
  10.0 14.2 %all-to-all-start = ((f32[32,8,128]{2,1,0:T(8,128)}), f32[32,8,128]{2,1,0:T(8,128)S(1)}, u32[]{:S(2)}, u32[]{:S(2)}) async-start(f32[32,8,128]{2,1,0:T(8,128)} %bitcast.3), calls=%async_computation | async-start | bytes 262144 | tf_op jit(solution)/shard_map/all_to_all | solution.py:323
  16.2 6.4 %collective-permute-start.5 = (f32[32,256]{1,0:T(8,128)S(1)}, f32[32,256]{1,0:T(8,128)S(1)}, u32[]{:S(2)}, u32[]{:S(2)}) collective-permute-start(f32[32,256]{1,0:T(8,128)S(1)} %margins.1), channel_id=1, source_target_pairs={{0,4},{2,6},{4,0},{5,9},{6,2},{7,11},{8,12},{9,5},{10,14},{11,7},{... | collective-permute-start | bytes 98312 | tf_op jit(solution)/shard_map/ppermute | solution.py:335
  22.8 1.6 %collective-permute-start.6 = (f32[32,256]{1,0:T(8,128)S(1)}, f32[32,256]{1,0:T(8,128)S(1)}, u32[]{:S(2)}, u32[]{:S(2)}) collective-permute-start(f32[32,256]{1,0:T(8,128)S(1)} %get-tuple-element.33), channel_id=1, source_target_pairs={{0,1},{1,0},{2,3},{3,2},{4,5},{5,4},{6,7},{7,6},{8,9},{9,8},{10,11... | collective-permute-start | bytes 98312 | tf_op jit(solution)/shard_map/ppermute | solution.py:369
  24.1 1.2 %collective-permute-start.3 = (f32[4,8,128]{2,1,0:T(8,128)S(1)}, f32[4,8,128]{2,1,0:T(8,128)S(1)}, u32[]{:S(2)}, u32[]{:S(2)}) collective-permute-start(f32[4,8,128]{2,1,0:T(8,128)S(1)} %reduce.1.mine_ref), channel_id=1, source_target_pairs={{0,1},{1,0},{2,3},{3,2},{4,5},{5,4},{6,7},{7,6},{8,9},{9,8},{10,11... | collective-permute-start | bytes 49160 | tf_op jit(solution)/shard_map/ppermute | solution.py:389

commit v7 on v6

--- a/solution.py
+++ b/solution.py
@@ -89,23 +89,15 @@
     fetches[4].wait()
 
 
-def right_hand_side(rows, tiles, coarse_len, blocks, parts_ref):
+def near_kernel(rows, tiles, packed_ref, core_ref, coarse_ref, rhs_ref, hi_ref, low_ref):
+    coarse_len = hi_ref.shape[0]
     levels = lax.broadcasted_iota(jnp.int32, (coarse_len, tiles * LANES), 0)
     rhs = jnp.zeros((3 * rows, coarse_len), F32)
-    for k, ref in enumerate(blocks):
+    for ref in (packed_ref, core_ref):
         codes = [ref[pl.ds(tiles * rows + t, 1)] for t in range(tiles)]
         unknowns = jnp.concatenate(codes, axis=1).astype(jnp.int32)
-        parts = split3(block_rows(ref, rows, 0, tiles))
-        parts_ref[k] = parts
-        rhs = rhs + dot(parts, onehot(levels == unknowns), NT)
-    return fold3(rhs)
-
-
-def near_kernel(
-    rows, tiles, packed_ref, core_ref, coarse_ref, rhs_ref, parts_ref, hi_ref, low_ref
-):
-    coarse_len = hi_ref.shape[0]
-    rhs_ref[...] = right_hand_side(rows, tiles, coarse_len, (packed_ref, core_ref), parts_ref)
+        rhs = rhs + dot(split3(block_rows(ref, rows, 0, tiles)), onehot(levels == unknowns), NT)
+    rhs_ref[...] = fold3(rhs)
     stride = coarse_ref.shape[0] // coarse_len
     for tile in range(stride):
         at = slice(tile * LANES, (tile + 1) * LANES)
@@ -113,10 +105,11 @@
 
 
 def coarse_kernel(
-    width, rows, tiles, y_ref, both_ref, rhs_ref, hi_ref, low_ref, send_ref, parts_ref
+    width, rows, tiles, packed_ref, core_ref, rhs_ref, far_ref, hi_ref, low_ref, send_ref, parts_ref
 ):
-    coarse_len = hi_ref.shape[0]
-    rhs = rhs_ref[...] + right_hand_side(rows, tiles, coarse_len, (y_ref, both_ref), parts_ref)
+    for k, ref in enumerate((packed_ref, core_ref)):
+        parts_ref[k] = split3(block_rows(ref, rows, 0, tiles))
+    rhs = rhs_ref[...] + far_ref[...]
     half = rows // 2
     lane = lax.broadcasted_iota(jnp.int32, (half, LANES), 1)
     step = 2 * LANES
@@ -136,10 +129,12 @@
                     send_ref[to + 1, copy, core] = right[piece]
 
 
-def margin_kernel(near_ref, far_ref, lists_ref, out_ref):
+def margin_kernel(tiles, near_ref, y_ref, both_ref, lists_ref, out_ref, far_ref):
     half, rows, cols = near_ref.shape
     wanted = jnp.where(facing() == 1, lists_ref[1:2], lists_ref[0:1])
     local = lax.broadcasted_iota(jnp.int32, (cols, wanted.shape[1]), 0)
+    for k, ref in enumerate((y_ref, both_ref)):
+        far_ref[k] = split3(block_rows(ref, rows // 3, 0, tiles))
     total = jnp.zeros((rows, wanted.shape[1]), F32)
     for k in range(2 * half):
         part = near_ref[k] if k < half else far_ref[k - half]
@@ -289,49 +284,52 @@
         name="pack",
     )(in_hbm(residual), in_hbm(codes), in_hbm(lists), in_hbm(wanted_count), in_hbm(table))
     lists = lax.ppermute(lists, ("sub", "blk"), neighbours)
-    over_y = lax.ppermute(packed, "blk", far_swap)
     over_core = lax.ppermute(packed, "blk", core_swap)
-    over_both = lax.ppermute(packed, "blk", both_swap)
-
-    rhs, near, m_hi, m_low = pl.pallas_call(
+
+    rhs, m_hi, m_low = pl.pallas_call(
         functools.partial(near_kernel, rows, tiles),
         out_shape=(
             jax.ShapeDtypeStruct((rows, coarse_len), F32),
-            jax.ShapeDtypeStruct((2, 3 * rows, cols), BF16),
             jax.ShapeDtypeStruct((coarse_len, subs * width), BF16),
             jax.ShapeDtypeStruct((coarse_len, subs * width), BF16),
         ),
         in_specs=[whole()] * 3,
-        out_specs=(whole(),) * 4,
+        out_specs=(whole(),) * 3,
         compiler_params=limit(12),
         cost_estimate=weight(2 * 10**9),
         name="near",
     )(packed, over_core, table)
-    send, far = pl.pallas_call(
+    far_rhs = lax.ppermute(rhs, "blk", far_swap)
+    over_y = lax.ppermute(packed, "blk", far_swap)
+    over_both = lax.ppermute(packed, "blk", both_swap)
+    send, near = pl.pallas_call(
         functools.partial(coarse_kernel, width, rows, tiles),
         out_shape=(
             jax.ShapeDtypeStruct((subs, chips, 2, rows // 4, LANES), F32),
-            jax.ShapeDtypeStruct((shards - 2, 3 * rows, cols), BF16),
-        ),
-        in_specs=[whole()] * 5,
+            jax.ShapeDtypeStruct((2, 3 * rows, cols), BF16),
+        ),
+        in_specs=[whole()] * 6,
         out_specs=(whole(), whole()),
         compiler_params=limit(12),
         cost_estimate=weight(8 * 10**9),
         name="coarse",
-    )(over_y, over_both, rhs, m_hi, m_low)
+    )(packed, over_core, rhs, far_rhs, m_hi, m_low)
     flat = send.reshape((subs * shards,) + send.shape[3:])
     got = lax.all_to_all(flat, ("sub", "blk"), 0, 0, tiled=True)
     got = got.reshape((subs, shards) + flat.shape[1:])
 
-    outgoing = pl.pallas_call(
-        margin_kernel,
-        out_shape=jax.ShapeDtypeStruct((rows, margin), F32),
-        in_specs=[whole()] * 3,
-        out_specs=whole(),
+    outgoing, far = pl.pallas_call(
+        functools.partial(margin_kernel, tiles),
+        out_shape=(
+            jax.ShapeDtypeStruct((rows, margin), F32),
+            jax.ShapeDtypeStruct((shards - 2, 3 * rows, cols), BF16),
+        ),
+        in_specs=[whole()] * 4,
+        out_specs=(whole(), whole()),
         compiler_params=limit(8),
         cost_estimate=weight(4 * 10**9),
         name="margins",
-    )(near, far, lists)
+    )(near, over_y, over_both, lists)
     halo = lax.ppermute(outgoing, ("sub", "blk"), neighbours)
 
     owned, w_hi, w_low, hot = pl.pallas_call(

time: 26.5 us -> 26.4 us (level)
  waiting for transfers between devices: 2.12 us -> 2.96 us
  starting transfers between devices: 17 us -> 16.3 us
  Pallas kernels: 7.06 us -> 6.72 us
    ppermute x0 -> x1, starting transfers between devices: none -> 2.93 us  [on_device(): far_rhs = lax.ppermute(rhs, 'blk', far_swap)]
    ppermute x1, starting transfers between devices: 2.64 us -> 0.01 us  [on_device(): over_both = lax.ppermute(packed, 'blk', both_swap)]
    all_to_all x1, starting transfers between devices: 5.94 us -> 3.98 us  [on_device(): got = lax.all_to_all(flat, ('sub', 'blk'), 0, 0, tiled=True)]
    ppermute x1, starting transfers between devices: 0.04 us -> 1.5 us  [on_device(): over_y = lax.ppermute(packed, 'blk', far_swap)]
    ppermute x1, waiting for transfers between devices: 0.01 us -> 0.91 us  [on_device(): over_core = lax.ppermute(packed, 'blk', core_swap)]
    ppermute x1, starting transfers between devices: 3.85 us -> 3.39 us  [on_device(): lists = lax.ppermute(lists, ('sub', 'blk'), neighbours)]
    pallas_call x1, Pallas kernels: 1.3 us -> 0.95 us  [on_device(): pl.pallas_call(functools.partial(coarse_kernel, width, rows, tiles), out_...]
  transfers between devices with their start and end apart: 8 -> 9, of which waited for: 2 -> 3; matrix products, arithmetic and copies ran while one was open for 0% -> 0% of each run, Pallas kernels for 19% -> 17%
where the time goes in v7:
time: 26.4 us; the launch traced here: 26.1 us
  starting transfers between devices  16.3 us (62%)
  Pallas kernels  6.72 us (25%)
  waiting for transfers between devices  2.96 us (11%)
    all_to_all x1, starting transfers between devices, on_device(): got = lax.all_to_all(flat, ('sub', 'blk'), 0, 0, tiled=True)  3.98 us
    ppermute x1, starting transfers between devices, on_device(): halo = lax.ppermute(outgoing, ('sub', 'blk'), neighbours)  3.69 us
    ppermute x1, starting transfers between devices, on_device(): lists = lax.ppermute(lists, ('sub', 'blk'), neighbours)  3.39 us
    ppermute x1, starting transfers between devices, on_device(): far_rhs = lax.ppermute(rhs, 'blk', far_swap)  2.93 us
    pallas_call x1, Pallas kernels, on_device(): pl.pallas_call(functools.partial(own_kernel, margin), out_shape=(jax.Shap...  2.67 us
    ppermute x1, starting transfers between devices, on_device(): over_y = lax.ppermute(packed, 'blk', far_swap)  1.5 us
    all_to_all x1, waiting for transfers between devices, on_device(): got = lax.all_to_all(flat, ('sub', 'blk'), 0, 0, tiled=True)  1.26 us
    pallas_call x1, Pallas kernels, on_device(): pl.pallas_call(pack_kernel, out_shape=(jax.ShapeDtypeStruct(packed_shape,...  1.17 us
  transfers between devices with their start and end apart: 9, of which 3 were waited for; matrix products, arithmetic and copies ran while one was open for 0% of the time, Pallas kernels for 17%

profile of v7, /device:TPU:0, one launch (start us, length us, event | category | flops | bytes accessed | tf_op | source)
XLA Modules:
  0.0 26.1 jit_solution(17725982024577645716)
XLA Ops:
  0.0 1.2 %pack.1 = (f32[136,128]{1,0:T(8,128)S(1)}, s32[2,256]{1,0:T(2,128)S(1)}, f32[1024,128]{1,0:T(8,128)S(1)}) custom-call(f32[32,512]{1,0:T(8,128)} %residual_ref.1, s32[1,512]{1,0:T(1,128)} %bitcast.8, s32[2,256]{1,0:T(2,128)} %bitcast.7, s32[1,2]{1,0:T(1,128)} %counts_ref.1, f32[1024,128]{1,0:T(8,128)} %bitcast.6), custom_call_target="tpu_custom_call" | custom-call | tf_op jit(solution)/shard_map/pack/pallas_call | solution.py:267
  1.2 0.5 %collective-permute-start = (f32[136,128]{1,0:T(8,128)S(1)}, f32[136,128]{1,0:T(8,128)S(1)}, u32[]{:S(2)}, u32[]{:S(2)}) collective-permute-start(f32[136,128]{1,0:T(8,128)S(1)} %get-tuple-element.21.packed_ref), channel_id=1, source_target_pairs={{0,1},{1,0},{2,3},{3,2},{4,5},{5,4},{6,7},{7,6},{8,9},{9,8},{10,11... | collective-permute-start | bytes 208904 | tf_op jit(solution)/shard_map/ppermute | solution.py:287
  1.7 0.9 %collective-permute-done.core_ref = f32[136,128]{1,0:T(8,128)S(1)} collective-permute-done((f32[136,128]{1,0:T(8,128)S(1)}, f32[136,128]{1,0:T(8,128)S(1)}, u32[]{:S(2)}, u32[]{:S(2)}) %collective-permute-start) | collective-permute-done | bytes 69664 | tf_op jit(solution)/shard_map/ppermute | solution.py:287
  2.6 0.3 %near.1 = (f32[32,256]{1,0:T(8,128)S(1)}, bf16[256,512]{1,0:T(8,128)(2,1)S(1)}, bf16[256,512]{1,0:T(8,128)(2,1)S(1)}) custom-call(f32[136,128]{1,0:T(8,128)S(1)} %get-tuple-element.21.packed_ref, f32[136,128]{1,0:T(8,128)S(1)} %collective-permute-done.core_ref, f32[1024,128]{1,0:T(8,128)S(1)} %get-tuple-element.22.coarse_ref), custom_call_target="tpu_custom_call" | custom-call | flops 2000000000 | tf_op jit(solution)/shard_map/near/pallas_call | solution.py:289
  3.0 2.9 %collective-permute-start.1 = (f32[32,256]{1,0:T(8,128)S(1)}, f32[32,256]{1,0:T(8,128)S(1)}, u32[]{:S(2)}, u32[]{:S(2)}) collective-permute-start(f32[32,256]{1,0:T(8,128)S(1)} %get-tuple-element.23.rhs_ref), channel_id=1, source_target_pairs={{0,2},{1,3},{2,0},{3,1},{4,6},{5,7},{6,4},{7,5},{8,10},{9,11},{10,... | collective-permute-start | bytes 98312 | tf_op jit(solution)/shard_map/ppermute | solution.py:302
  5.9 0.0 collective-permute-start.4
  5.9 1.5 %collective-permute-start.3 = (f32[136,128]{1,0:T(8,128)S(1)}, f32[136,128]{1,0:T(8,128)S(1)}, u32[]{:S(2)}, u32[]{:S(2)}) collective-permute-start(f32[136,128]{1,0:T(8,128)S(1)} %get-tuple-element.21.packed_ref), channel_id=1, source_target_pairs={{0,2},{1,3},{2,0},{3,1},{4,6},{5,7},{6,4},{7,5},{8,10},{9,11},{10,... | collective-permute-start | bytes 208904 | tf_op jit(solution)/shard_map/ppermute | solution.py:303
  7.4 3.4 %collective-permute-start.5 = (s32[2,256]{1,0:T(2,128)S(1)}, s32[2,256]{1,0:T(2,128)S(1)}, u32[]{:S(2)}, u32[]{:S(2)}) collective-permute-start(s32[2,256]{1,0:T(2,128)S(1)} %get-tuple-element.28), channel_id=1, source_target_pairs={{0,4},{2,6},{4,0},{5,9},{6,2},{7,11},{8,12},{9,5},{10,14},{11,7},{... | collective-permute-start | bytes 6152 | tf_op jit(solution)/shard_map/ppermute | solution.py:286
  10.8 0.0 collective-permute-done.1.far_ref
  10.8 0.9 %coarse.1 = (f32[8,2,2,8,128]{4,3,2,1,0:T(8,128)}, bf16[2,96,512]{2,1,0:T(8,128)(2,1)S(1)}) custom-call(f32[136,128]{1,0:T(8,128)S(1)} %get-tuple-element.21.packed_ref, f32[136,128]{1,0:T(8,128)S(1)} %collective-permute-done.core_ref, f32[32,256]{1,0:T(8,128)S(1)} %get-tuple-element.23.rhs_ref, f32[32,256]{1,0:T(8,128)S(1)} %collective-permute-done.1.far_ref, ...), custom_call_target="tpu_custom_call" | custom-call | flops 8000000000 | tf_op jit(solution)/shard_map/coarse/pallas_call | solution.py:305
  11.8 4.0 %all-to-all-start = ((f32[32,8,128]{2,1,0:T(8,128)}), f32[32,8,128]{2,1,0:T(8,128)S(1)}, u32[]{:S(2)}, u32[]{:S(2)}) async-start(f32[32,8,128]{2,1,0:T(8,128)} %bitcast.3), calls=%async_computation | async-start | bytes 262144 | tf_op jit(solution)/shard_map/all_to_all | solution.py:318
  15.7 0.0 collective-permute-done.5.lists_ref
  15.8 0.0 collective-permute-done.4.both_ref
  15.8 0.0 collective-permute-done.3.y_ref
  15.8 0.3 %margins.1 = (f32[32,256]{1,0:T(8,128)S(1)}, bf16[2,96,512]{2,1,0:T(8,128)(2,1)S(1)}) custom-call(bf16[2,96,512]{2,1,0:T(8,128)(2,1)S(1)} %get-tuple-element.27.near_ref, f32[136,128]{1,0:T(8,128)S(1)} %collective-permute-done.3.y_ref, f32[136,128]{1,0:T(8,128)S(1)} %collective-permute-done.4.both_ref, s32[2,256]{1,0:T(2,128)S(1)} %collective-permute-done.5.lists_ref), custom_call_target="tpu_custom_call" | custom-call | flops 4000000000 | tf_op jit(solution)/shard_map/margins/pallas_call | solution.py:321
  16.1 3.7 %collective-permute-start.6 = (f32[32,256]{1,0:T(8,128)S(1)}, f32[32,256]{1,0:T(8,128)S(1)}, u32[]{:S(2)}, u32[]{:S(2)}) collective-permute-start(f32[32,256]{1,0:T(8,128)S(1)} %get-tuple-element.31), channel_id=1, source_target_pairs={{0,4},{2,6},{4,0},{5,9},{6,2},{7,11},{8,12},{9,5},{10,14},{11,7},{... | collective-permute-start | bytes 98312 | tf_op jit(solution)/shard_map/ppermute | solution.py:333
  19.8 2.7 %owned.1 = (f32[32,512]{1,0:T(8,128)S(1)}, bf16[2,256,512]{2,1,0:T(8,128)(2,1)S(1)}, bf16[2,256,512]{2,1,0:T(8,128)(2,1)S(1)}, bf16[256,512]{1,0:T(8,128)(2,1)S(1)}) custom-call(bf16[2,96,512]{2,1,0:T(8,128)(2,1)S(1)} %get-tuple-element.27.near_ref, bf16[2,96,512]{2,1,0:T(8,128)(2,1)S(1)} %get-tuple-element.29.far_ref, s32[1,512]{1,0:T(1,128)} %bitcast.9, ...), custom_call_target="tpu_custom_call" | custom-call | flops 40000000000 | tf_op jit(solution)/shard_map/owned/pallas_call | solution.py:335
  22.5 0.0 collective-permute-done.6.halo_ref
  22.5 0.2 mine.1
  22.7 0.0 collective-permute-start.7
  22.7 1.3 %all-to-all-done = f32[32,8,128]{2,1,0:T(8,128)S(1)} async-done(((f32[32,8,128]{2,1,0:T(8,128)}), f32[32,8,128]{2,1,0:T(8,128)S(1)}, u32[]{:S(2)}, u32[]{:S(2)}) %all-to-all-start) | async-done | bytes 131104 | tf_op jit(solution)/shard_map/all_to_all | solution.py:318
  24.0 0.3 %collective-permute-start.2 = (f32[4,8,128]{2,1,0:T(8,128)S(1)}, f32[4,8,128]{2,1,0:T(8,128)S(1)}, u32[]{:S(2)}, u32[]{:S(2)}) collective-permute-start(f32[4,8,128]{2,1,0:T(8,128)S(1)} %reduce.1.mine_ref), channel_id=1, source_target_pairs={{0,1},{1,0},{2,3},{3,2},{4,5},{5,4},{6,7},{7,6},{8,9},{9,8},{10,11... | collective-permute-start | bytes 49160 | tf_op jit(solution)/shard_map/ppermute | solution.py:387
  24.3 0.0 collective-permute-done.7.halo_ref
  24.3 0.2 other.1.total_ref
  24.5 0.8 %collective-permute-done.2.other_ref = f32[4,8,128]{2,1,0:T(8,128)S(1)} collective-permute-done((f32[4,8,128]{2,1,0:T(8,128)S(1)}, f32[4,8,128]{2,1,0:T(8,128)S(1)}, u32[]{:S(2)}, u32[]{:S(2)}) %collective-permute-start.2) | collective-permute-done | bytes 16416 | tf_op jit(solution)/shard_map/ppermute | solution.py:387
  25.2 0.9 %tail.1 = f32[32,512]{1,0:T(8,128)} custom-call(f32[4,8,128]{2,1,0:T(8,128)S(1)} %reduce.1.mine_ref, f32[4,8,128]{2,1,0:T(8,128)S(1)} %collective-permute-done.2.other_ref, bf16[256,512]{1,0:T(8,128)(2,1)S(1)} %get-tuple-element.30.hot_ref, f32[32,512]{1,0:T(8,128)S(1)} %other.1.total_ref), custom_call_target="tpu_custom_call" | custom-call | tf_op jit(solution)/shard_map/tail/pallas_call | solution.py:389
  (1 shorter events, 0.0 us)
Async XLA Ops:
  1.2 1.4 %collective-permute-start = (f32[136,128]{1,0:T(8,128)S(1)}, f32[136,128]{1,0:T(8,128)S(1)}, u32[]{:S(2)}, u32[]{:S(2)}) collective-permute-start(f32[136,128]{1,0:T(8,128)S(1)} %get-tuple-element.21.packed_ref), channel_id=1, source_target_pairs={{0,1},{1,0},{2,3},{3,2},{4,5},{5,4},{6,7},{7,6},{8,9},{9,8},{10,11... | collective-permute-start | bytes 208904 | tf_op jit(solution)/shard_map/ppermute | solution.py:287
  3.0 7.8 %collective-permute-start.1 = (f32[32,256]{1,0:T(8,128)S(1)}, f32[32,256]{1,0:T(8,128)S(1)}, u32[]{:S(2)}, u32[]{:S(2)}) collective-permute-start(f32[32,256]{1,0:T(8,128)S(1)} %get-tuple-element.23.rhs_ref), channel_id=1, source_target_pairs={{0,2},{1,3},{2,0},{3,1},{4,6},{5,7},{6,4},{7,5},{8,10},{9,11},{10,... | collective-permute-start | bytes 98312 | tf_op jit(solution)/shard_map/ppermute | solution.py:302
  5.9 9.9 %collective-permute-start.4 = (f32[136,128]{1,0:T(8,128)S(1)}, f32[136,128]{1,0:T(8,128)S(1)}, u32[]{:S(2)}, u32[]{:S(2)}) collective-permute-start(f32[136,128]{1,0:T(8,128)S(1)} %get-tuple-element.21.packed_ref), channel_id=1, source_target_pairs={{0,3},{1,2},{2,1},{3,0},{4,7},{5,6},{6,5},{7,4},{8,11},{9,10},{10,... | collective-permute-start | bytes 208904 | tf_op jit(solution)/shard_map/ppermute | solution.py:304
  5.9 9.9 %collective-permute-start.3 = (f32[136,128]{1,0:T(8,128)S(1)}, f32[136,128]{1,0:T(8,128)S(1)}, u32[]{:S(2)}, u32[]{:S(2)}) collective-permute-start(f32[136,128]{1,0:T(8,128)S(1)} %get-tuple-element.21.packed_ref), channel_id=1, source_target_pairs={{0,2},{1,3},{2,0},{3,1},{4,6},{5,7},{6,4},{7,5},{8,10},{9,11},{10,... | collective-permute-start | bytes 208904 | tf_op jit(solution)/shard_map/ppermute | solution.py:303
  7.4 8.3 %collective-permute-start.5 = (s32[2,256]{1,0:T(2,128)S(1)}, s32[2,256]{1,0:T(2,128)S(1)}, u32[]{:S(2)}, u32[]{:S(2)}) collective-permute-start(s32[2,256]{1,0:T(2,128)S(1)} %get-tuple-element.28), channel_id=1, source_target_pairs={{0,4},{2,6},{4,0},{5,9},{6,2},{7,11},{8,12},{9,5},{10,14},{11,7},{... | collective-permute-start | bytes 6152 | tf_op jit(solution)/shard_map/ppermute | solution.py:286
  11.8 12.2 %all-to-all-start = ((f32[32,8,128]{2,1,0:T(8,128)}), f32[32,8,128]{2,1,0:T(8,128)S(1)}, u32[]{:S(2)}, u32[]{:S(2)}) async-start(f32[32,8,128]{2,1,0:T(8,128)} %bitcast.3), calls=%async_computation | async-start | bytes 262144 | tf_op jit(solution)/shard_map/all_to_all | solution.py:318
  16.1 6.4 %collective-permute-start.6 = (f32[32,256]{1,0:T(8,128)S(1)}, f32[32,256]{1,0:T(8,128)S(1)}, u32[]{:S(2)}, u32[]{:S(2)}) collective-permute-start(f32[32,256]{1,0:T(8,128)S(1)} %get-tuple-element.31), channel_id=1, source_target_pairs={{0,4},{2,6},{4,0},{5,9},{6,2},{7,11},{8,12},{9,5},{10,14},{11,7},{... | collective-permute-start | bytes 98312 | tf_op jit(solution)/shard_map/ppermute | solution.py:333
  22.7 1.6 %collective-permute-start.7 = (f32[32,256]{1,0:T(8,128)S(1)}, f32[32,256]{1,0:T(8,128)S(1)}, u32[]{:S(2)}, u32[]{:S(2)}) collective-permute-start(f32[32,256]{1,0:T(8,128)S(1)} %get-tuple-element.35), channel_id=1, source_target_pairs={{0,1},{1,0},{2,3},{3,2},{4,5},{5,4},{6,7},{7,6},{8,9},{9,8},{10,11... | collective-permute-start | bytes 98312 | tf_op jit(solution)/shard_map/ppermute | solution.py:367
  24.0 1.2 %collective-permute-start.2 = (f32[4,8,128]{2,1,0:T(8,128)S(1)}, f32[4,8,128]{2,1,0:T(8,128)S(1)}, u32[]{:S(2)}, u32[]{:S(2)}) collective-permute-start(f32[4,8,128]{2,1,0:T(8,128)S(1)} %reduce.1.mine_ref), channel_id=1, source_target_pairs={{0,1},{1,0},{2,3},{3,2},{4,5},{5,4},{6,7},{7,6},{8,9},{9,8},{10,11... | collective-permute-start | bytes 49160 | tf_op jit(solution)/shard_map/ppermute | solution.py:387

commit v8 on v7

--- a/solution.py
+++ b/solution.py
@@ -89,14 +89,15 @@
     fetches[4].wait()
 
 
-def near_kernel(rows, tiles, packed_ref, core_ref, coarse_ref, rhs_ref, hi_ref, low_ref):
+def near_kernel(
+    rows, tiles, packed_ref, core_ref, core_agg_ref, coarse_ref, rhs_ref, hi_ref, low_ref
+):
     coarse_len = hi_ref.shape[0]
     levels = lax.broadcasted_iota(jnp.int32, (coarse_len, tiles * LANES), 0)
-    rhs = jnp.zeros((3 * rows, coarse_len), F32)
-    for ref in (packed_ref, core_ref):
-        codes = [ref[pl.ds(tiles * rows + t, 1)] for t in range(tiles)]
-        unknowns = jnp.concatenate(codes, axis=1).astype(jnp.int32)
-        rhs = rhs + dot(split3(block_rows(ref, rows, 0, tiles)), onehot(levels == unknowns), NT)
+    codes = [packed_ref[pl.ds(tiles * rows + t, 1)] for t in range(tiles)]
+    unknowns = jnp.concatenate(codes, axis=1).astype(jnp.int32)
+    rhs = dot(split3(block_rows(packed_ref, rows, 0, tiles)), onehot(levels == unknowns), NT)
+    rhs = rhs + dot(split3(core_ref[...]), onehot(levels == core_agg_ref[...]), NT)
     rhs_ref[...] = fold3(rhs)
     stride = coarse_ref.shape[0] // coarse_len
     for tile in range(stride):
@@ -107,8 +108,8 @@
 def coarse_kernel(
     width, rows, tiles, packed_ref, core_ref, rhs_ref, far_ref, hi_ref, low_ref, send_ref, parts_ref
 ):
-    for k, ref in enumerate((packed_ref, core_ref)):
-        parts_ref[k] = split3(block_rows(ref, rows, 0, tiles))
+    parts_ref[0] = split3(block_rows(packed_ref, rows, 0, tiles))
+    parts_ref[1] = split3(core_ref[...])
     rhs = rhs_ref[...] + far_ref[...]
     half = rows // 2
     lane = lax.broadcasted_iota(jnp.int32, (half, LANES), 1)
@@ -281,10 +282,12 @@
             pltpu.SemaphoreType.DMA((5,)),
         ],
         compiler_params=limit(4),
+        cost_estimate=weight(8 * 10**9),
         name="pack",
     )(in_hbm(residual), in_hbm(codes), in_hbm(lists), in_hbm(wanted_count), in_hbm(table))
     lists = lax.ppermute(lists, ("sub", "blk"), neighbours)
-    over_core = lax.ppermute(packed, "blk", core_swap)
+    over_core = lax.ppermute(residual, "blk", core_swap)
+    core_codes = lax.ppermute(aggregate, "blk", core_swap)[None]
 
     rhs, m_hi, m_low = pl.pallas_call(
         functools.partial(near_kernel, rows, tiles),
@@ -293,12 +296,12 @@
             jax.ShapeDtypeStruct((coarse_len, subs * width), BF16),
             jax.ShapeDtypeStruct((coarse_len, subs * width), BF16),
         ),
-        in_specs=[whole()] * 3,
+        in_specs=[whole()] * 4,
         out_specs=(whole(),) * 3,
         compiler_params=limit(12),
         cost_estimate=weight(2 * 10**9),
         name="near",
-    )(packed, over_core, table)
+    )(packed, over_core, core_codes, table)
     far_rhs = lax.ppermute(rhs, "blk", far_swap)
     over_y = lax.ppermute(packed, "blk", far_swap)
     over_both = lax.ppermute(packed, "blk", both_swap)

time: 26.4 us -> 25.7 us (0.973)
  waiting for transfers between devices: 2.96 us -> 2.28 us
    ppermute x1 -> x2, waiting for transfers between devices: 0.91 us -> 0.22 us  [the longest x1 0.22 us: on_device(): over_core = lax.ppermute(residual, 'blk', core_swap)]
  transfers between devices with their start and end apart: 9 -> 10, of which waited for: 3 -> 3; matrix products, arithmetic and copies ran while one was open for 0% -> 0% of each run, Pallas kernels for 17% -> 22%
where the time goes in v8:
time: 25.7 us; the launch traced here: 25.4 us
  starting transfers between devices  16.3 us (63%)
  Pallas kernels  6.71 us (26%)
  waiting for transfers between devices  2.28 us (9%)
    all_to_all x1, starting transfers between devices, on_device(): got = lax.all_to_all(flat, ('sub', 'blk'), 0, 0, tiled=True)  3.97 us
    ppermute x1, starting transfers between devices, on_device(): halo = lax.ppermute(outgoing, ('sub', 'blk'), neighbours)  3.69 us
    ppermute x1, starting transfers between devices, on_device(): lists = lax.ppermute(lists, ('sub', 'blk'), neighbours)  3.39 us
    ppermute x1, starting transfers between devices, on_device(): far_rhs = lax.ppermute(rhs, 'blk', far_swap)  2.83 us
    pallas_call x1, Pallas kernels, on_device(): pl.pallas_call(functools.partial(own_kernel, margin), out_shape=(jax.Shap...  2.67 us
    ppermute x1, starting transfers between devices, on_device(): over_y = lax.ppermute(packed, 'blk', far_swap)  1.61 us
    all_to_all x1, waiting for transfers between devices, on_device(): got = lax.all_to_all(flat, ('sub', 'blk'), 0, 0, tiled=True)  1.26 us
    pallas_call x1, Pallas kernels, on_device(): pl.pallas_call(pack_kernel, out_shape=(jax.ShapeDtypeStruct(packed_shape,...  1.17 us
  transfers between devices with their start and end apart: 10, of which 3 were waited for; matrix products, arithmetic and copies ran while one was open for 0% of the time, Pallas kernels for 22%

profile of v8, /device:TPU:0, one launch (start us, length us, event | category | flops | bytes accessed | tf_op | source)
XLA Modules:
  0.0 25.4 jit_solution(5618431682448501682)
XLA Ops:
  0.0 0.5 %collective-permute-start.1 = (s32[512]{0:T(512)}, s32[512]{0:T(512)S(1)}, u32[]{:S(2)}, u32[]{:S(2)}) collective-permute-start(s32[512]{0:T(512)} %param.11), channel_id=1, source_target_pairs={{0,1},{1,0},{2,3},{3,2},{4,5},{5,4},{6,7},{7,6},{8,9},{9,8},{10,11... | collective-permute-start | bytes 6152 | tf_op jit(solution)/shard_map/ppermute | solution.py:290
  0.5 0.1 collective-permute-start
  0.5 1.2 %pack.1 = (f32[136,128]{1,0:T(8,128)S(1)}, s32[2,256]{1,0:T(2,128)S(1)}, f32[1024,128]{1,0:T(8,128)S(1)}) custom-call(f32[32,512]{1,0:T(8,128)} %residual_ref.1, s32[1,512]{1,0:T(1,128)} %bitcast.10, s32[2,256]{1,0:T(2,128)} %bitcast.9, s32[1,2]{1,0:T(1,128)} %counts_ref.1, f32[1024,128]{1,0:T(8,128)} %bitcast.8), custom_call_target="tpu_custom_call" | custom-call | flops 8000000000 | tf_op jit(solution)/shard_map/pack/pallas_call | solution.py:268
  1.7 0.0 collective-permute-done.1
  1.7 0.2 collective-permute-done.core_ref
  1.9 0.3 %near.1 = (f32[32,256]{1,0:T(8,128)S(1)}, bf16[256,512]{1,0:T(8,128)(2,1)S(1)}, bf16[256,512]{1,0:T(8,128)(2,1)S(1)}) custom-call(f32[136,128]{1,0:T(8,128)S(1)} %get-tuple-element.21.packed_ref, f32[32,512]{1,0:T(8,128)S(1)} %collective-permute-done.core_ref, s32[1,512]{1,0:T(1,128)S(1)} %bitcast.7, f32[1024,128]{1,0:T(8,128)S(1)} %get-tuple-element.22.coarse_ref), custom_call_target="tpu_custom_call" | custom-call | flops 2000000000 | tf_op jit(solution)/shard_map/near/pallas_call | solution.py:292
  2.3 2.8 %collective-permute-start.2 = (f32[32,256]{1,0:T(8,128)S(1)}, f32[32,256]{1,0:T(8,128)S(1)}, u32[]{:S(2)}, u32[]{:S(2)}) collective-permute-start(f32[32,256]{1,0:T(8,128)S(1)} %get-tuple-element.23.rhs_ref), channel_id=1, source_target_pairs={{0,2},{1,3},{2,0},{3,1},{4,6},{5,7},{6,4},{7,5},{8,10},{9,11},{10,... | collective-permute-start | bytes 98312 | tf_op jit(solution)/shard_map/ppermute | solution.py:305
  5.1 0.0 collective-permute-start.5
  5.1 1.6 %collective-permute-start.4 = (f32[136,128]{1,0:T(8,128)S(1)}, f32[136,128]{1,0:T(8,128)S(1)}, u32[]{:S(2)}, u32[]{:S(2)}) collective-permute-start(f32[136,128]{1,0:T(8,128)S(1)} %get-tuple-element.21.packed_ref), channel_id=1, source_target_pairs={{0,2},{1,3},{2,0},{3,1},{4,6},{5,7},{6,4},{7,5},{8,10},{9,11},{10,... | collective-permute-start | bytes 208904 | tf_op jit(solution)/shard_map/ppermute | solution.py:306
  6.7 3.4 %collective-permute-start.6 = (s32[2,256]{1,0:T(2,128)S(1)}, s32[2,256]{1,0:T(2,128)S(1)}, u32[]{:S(2)}, u32[]{:S(2)}) collective-permute-start(s32[2,256]{1,0:T(2,128)S(1)} %get-tuple-element.28), channel_id=1, source_target_pairs={{0,4},{2,6},{4,0},{5,9},{6,2},{7,11},{8,12},{9,5},{10,14},{11,7},{... | collective-permute-start | bytes 6152 | tf_op jit(solution)/shard_map/ppermute | solution.py:288
  10.1 0.0 collective-permute-done.2.far_ref
  10.1 0.9 %coarse.1 = (f32[8,2,2,8,128]{4,3,2,1,0:T(8,128)}, bf16[2,96,512]{2,1,0:T(8,128)(2,1)S(1)}) custom-call(f32[136,128]{1,0:T(8,128)S(1)} %get-tuple-element.21.packed_ref, f32[32,512]{1,0:T(8,128)S(1)} %collective-permute-done.core_ref, f32[32,256]{1,0:T(8,128)S(1)} %get-tuple-element.23.rhs_ref, f32[32,256]{1,0:T(8,128)S(1)} %collective-permute-done.2.far_ref, ...), custom_call_target="tpu_custom_call" | custom-call | flops 8000000000 | tf_op jit(solution)/shard_map/coarse/pallas_call | solution.py:308
  11.1 4.0 %all-to-all-start = ((f32[32,8,128]{2,1,0:T(8,128)}), f32[32,8,128]{2,1,0:T(8,128)S(1)}, u32[]{:S(2)}, u32[]{:S(2)}) async-start(f32[32,8,128]{2,1,0:T(8,128)} %bitcast.4), calls=%async_computation | async-start | bytes 262144 | tf_op jit(solution)/shard_map/all_to_all | solution.py:321
  15.0 0.0 collective-permute-done.6.lists_ref
  15.1 0.0 collective-permute-done.5.both_ref
  15.1 0.0 collective-permute-done.4.y_ref
  15.1 0.3 %margins.1 = (f32[32,256]{1,0:T(8,128)S(1)}, bf16[2,96,512]{2,1,0:T(8,128)(2,1)S(1)}) custom-call(bf16[2,96,512]{2,1,0:T(8,128)(2,1)S(1)} %get-tuple-element.27.near_ref, f32[136,128]{1,0:T(8,128)S(1)} %collective-permute-done.4.y_ref, f32[136,128]{1,0:T(8,128)S(1)} %collective-permute-done.5.both_ref, s32[2,256]{1,0:T(2,128)S(1)} %collective-permute-done.6.lists_ref), custom_call_target="tpu_custom_call" | custom-call | flops 4000000000 | tf_op jit(solution)/shard_map/margins/pallas_call | solution.py:324
  15.4 3.7 %collective-permute-start.7 = (f32[32,256]{1,0:T(8,128)S(1)}, f32[32,256]{1,0:T(8,128)S(1)}, u32[]{:S(2)}, u32[]{:S(2)}) collective-permute-start(f32[32,256]{1,0:T(8,128)S(1)} %get-tuple-element.31), channel_id=1, source_target_pairs={{0,4},{2,6},{4,0},{5,9},{6,2},{7,11},{8,12},{9,5},{10,14},{11,7},{... | collective-permute-start | bytes 98312 | tf_op jit(solution)/shard_map/ppermute | solution.py:336
  19.1 2.7 %owned.1 = (f32[32,512]{1,0:T(8,128)S(1)}, bf16[2,256,512]{2,1,0:T(8,128)(2,1)S(1)}, bf16[2,256,512]{2,1,0:T(8,128)(2,1)S(1)}, bf16[256,512]{1,0:T(8,128)(2,1)S(1)}) custom-call(bf16[2,96,512]{2,1,0:T(8,128)(2,1)S(1)} %get-tuple-element.27.near_ref, bf16[2,96,512]{2,1,0:T(8,128)(2,1)S(1)} %get-tuple-element.29.far_ref, s32[1,512]{1,0:T(1,128)} %bitcast.11, ...), custom_call_target="tpu_custom_call" | custom-call | flops 40000000000 | tf_op jit(solution)/shard_map/owned/pallas_call | solution.py:338
  21.8 0.0 collective-permute-done.7.halo_ref
  21.8 0.2 mine.1
  22.0 0.0 collective-permute-start.8
  22.0 1.3 %all-to-all-done = f32[32,8,128]{2,1,0:T(8,128)S(1)} async-done(((f32[32,8,128]{2,1,0:T(8,128)}), f32[32,8,128]{2,1,0:T(8,128)S(1)}, u32[]{:S(2)}, u32[]{:S(2)}) %all-to-all-start) | async-done | bytes 131104 | tf_op jit(solution)/shard_map/all_to_all | solution.py:321
  23.3 0.3 %collective-permute-start.3 = (f32[4,8,128]{2,1,0:T(8,128)S(1)}, f32[4,8,128]{2,1,0:T(8,128)S(1)}, u32[]{:S(2)}, u32[]{:S(2)}) collective-permute-start(f32[4,8,128]{2,1,0:T(8,128)S(1)} %reduce.1.mine_ref), channel_id=1, source_target_pairs={{0,1},{1,0},{2,3},{3,2},{4,5},{5,4},{6,7},{7,6},{8,9},{9,8},{10,11... | collective-permute-start | bytes 49160 | tf_op jit(solution)/shard_map/ppermute | solution.py:390
  23.6 0.0 collective-permute-done.8.halo_ref
  23.6 0.2 other.1.total_ref
  23.8 0.8 %collective-permute-done.3.other_ref = f32[4,8,128]{2,1,0:T(8,128)S(1)} collective-permute-done((f32[4,8,128]{2,1,0:T(8,128)S(1)}, f32[4,8,128]{2,1,0:T(8,128)S(1)}, u32[]{:S(2)}, u32[]{:S(2)}) %collective-permute-start.3) | collective-permute-done | bytes 16416 | tf_op jit(solution)/shard_map/ppermute | solution.py:390
  24.5 0.9 %tail.1 = f32[32,512]{1,0:T(8,128)} custom-call(f32[4,8,128]{2,1,0:T(8,128)S(1)} %reduce.1.mine_ref, f32[4,8,128]{2,1,0:T(8,128)S(1)} %collective-permute-done.3.other_ref, bf16[256,512]{1,0:T(8,128)(2,1)S(1)} %get-tuple-element.30.hot_ref, f32[32,512]{1,0:T(8,128)S(1)} %other.1.total_ref), custom_call_target="tpu_custom_call" | custom-call | tf_op jit(solution)/shard_map/tail/pallas_call | solution.py:392
  (1 shorter events, 0.0 us)
Async XLA Ops:
  0.0 1.7 %collective-permute-start.1 = (s32[512]{0:T(512)}, s32[512]{0:T(512)S(1)}, u32[]{:S(2)}, u32[]{:S(2)}) collective-permute-start(s32[512]{0:T(512)} %param.11), channel_id=1, source_target_pairs={{0,1},{1,0},{2,3},{3,2},{4,5},{5,4},{6,7},{7,6},{8,9},{9,8},{10,11... | collective-permute-start | bytes 6152 | tf_op jit(solution)/shard_map/ppermute | solution.py:290
  0.5 1.5 %collective-permute-start = (f32[32,512]{1,0:T(8,128)}, f32[32,512]{1,0:T(8,128)S(1)}, u32[]{:S(2)}, u32[]{:S(2)}) collective-permute-start(f32[32,512]{1,0:T(8,128)} %residual_ref.1), channel_id=1, source_target_pairs={{0,1},{1,0},{2,3},{3,2},{4,5},{5,4},{6,7},{7,6},{8,9},{9,8},{10,11... | collective-permute-start | bytes 196616 | tf_op jit(solution)/shard_map/ppermute | solution.py:289
  2.3 7.8 %collective-permute-start.2 = (f32[32,256]{1,0:T(8,128)S(1)}, f32[32,256]{1,0:T(8,128)S(1)}, u32[]{:S(2)}, u32[]{:S(2)}) collective-permute-start(f32[32,256]{1,0:T(8,128)S(1)} %get-tuple-element.23.rhs_ref), channel_id=1, source_target_pairs={{0,2},{1,3},{2,0},{3,1},{4,6},{5,7},{6,4},{7,5},{8,10},{9,11},{10,... | collective-permute-start | bytes 98312 | tf_op jit(solution)/shard_map/ppermute | solution.py:305
  5.1 10.0 %collective-permute-start.5 = (f32[136,128]{1,0:T(8,128)S(1)}, f32[136,128]{1,0:T(8,128)S(1)}, u32[]{:S(2)}, u32[]{:S(2)}) collective-permute-start(f32[136,128]{1,0:T(8,128)S(1)} %get-tuple-element.21.packed_ref), channel_id=1, source_target_pairs={{0,3},{1,2},{2,1},{3,0},{4,7},{5,6},{6,5},{7,4},{8,11},{9,10},{10,... | collective-permute-start | bytes 208904 | tf_op jit(solution)/shard_map/ppermute | solution.py:307
  5.1 10.0 %collective-permute-start.4 = (f32[136,128]{1,0:T(8,128)S(1)}, f32[136,128]{1,0:T(8,128)S(1)}, u32[]{:S(2)}, u32[]{:S(2)}) collective-permute-start(f32[136,128]{1,0:T(8,128)S(1)} %get-tuple-element.21.packed_ref), channel_id=1, source_target_pairs={{0,2},{1,3},{2,0},{3,1},{4,6},{5,7},{6,4},{7,5},{8,10},{9,11},{10,... | collective-permute-start | bytes 208904 | tf_op jit(solution)/shard_map/ppermute | solution.py:306
  6.7 8.3 %collective-permute-start.6 = (s32[2,256]{1,0:T(2,128)S(1)}, s32[2,256]{1,0:T(2,128)S(1)}, u32[]{:S(2)}, u32[]{:S(2)}) collective-permute-start(s32[2,256]{1,0:T(2,128)S(1)} %get-tuple-element.28), channel_id=1, source_target_pairs={{0,4},{2,6},{4,0},{5,9},{6,2},{7,11},{8,12},{9,5},{10,14},{11,7},{... | collective-permute-start | bytes 6152 | tf_op jit(solution)/shard_map/ppermute | solution.py:288
  11.1 12.2 %all-to-all-start = ((f32[32,8,128]{2,1,0:T(8,128)}), f32[32,8,128]{2,1,0:T(8,128)S(1)}, u32[]{:S(2)}, u32[]{:S(2)}) async-start(f32[32,8,128]{2,1,0:T(8,128)} %bitcast.4), calls=%async_computation | async-start | bytes 262144 | tf_op jit(solution)/shard_map/all_to_all | solution.py:321
  15.4 6.4 %collective-permute-start.7 = (f32[32,256]{1,0:T(8,128)S(1)}, f32[32,256]{1,0:T(8,128)S(1)}, u32[]{:S(2)}, u32[]{:S(2)}) collective-permute-start(f32[32,256]{1,0:T(8,128)S(1)} %get-tuple-element.31), channel_id=1, source_target_pairs={{0,4},{2,6},{4,0},{5,9},{6,2},{7,11},{8,12},{9,5},{10,14},{11,7},{... | collective-permute-start | bytes 98312 | tf_op jit(solution)/shard_map/ppermute | solution.py:336
  22.0 1.6 %collective-permute-start.8 = (f32[32,256]{1,0:T(8,128)S(1)}, f32[32,256]{1,0:T(8,128)S(1)}, u32[]{:S(2)}, u32[]{:S(2)}) collective-permute-start(f32[32,256]{1,0:T(8,128)S(1)} %get-tuple-element.35), channel_id=1, source_target_pairs={{0,1},{1,0},{2,3},{3,2},{4,5},{5,4},{6,7},{7,6},{8,9},{9,8},{10,11... | collective-permute-start | bytes 98312 | tf_op jit(solution)/shard_map/ppermute | solution.py:370
  23.3 1.2 %collective-permute-start.3 = (f32[4,8,128]{2,1,0:T(8,128)S(1)}, f32[4,8,128]{2,1,0:T(8,128)S(1)}, u32[]{:S(2)}, u32[]{:S(2)}) collective-permute-start(f32[4,8,128]{2,1,0:T(8,128)S(1)} %reduce.1.mine_ref), channel_id=1, source_target_pairs={{0,1},{1,0},{2,3},{3,2},{4,5},{5,4},{6,7},{7,6},{8,9},{9,8},{10,11... | collective-permute-start | bytes 49160 | tf_op jit(solution)/shard_map/ppermute | solution.py:390

commit v9 on v8

--- a/solution.py
+++ b/solution.py
@@ -90,15 +90,17 @@
 
 
 def near_kernel(
-    rows, tiles, packed_ref, core_ref, core_agg_ref, coarse_ref, rhs_ref, hi_ref, low_ref
+    rows, tiles, packed_ref, core_ref, core_agg_ref, coarse_ref, joint_ref, hi_ref, low_ref
 ):
     coarse_len = hi_ref.shape[0]
     levels = lax.broadcasted_iota(jnp.int32, (coarse_len, tiles * LANES), 0)
     codes = [packed_ref[pl.ds(tiles * rows + t, 1)] for t in range(tiles)]
     unknowns = jnp.concatenate(codes, axis=1).astype(jnp.int32)
-    rhs = dot(split3(block_rows(packed_ref, rows, 0, tiles)), onehot(levels == unknowns), NT)
+    block = block_rows(packed_ref, rows, 0, tiles)
+    rhs = dot(split3(block), onehot(levels == unknowns), NT)
     rhs = rhs + dot(split3(core_ref[...]), onehot(levels == core_agg_ref[...]), NT)
-    rhs_ref[...] = fold3(rhs)
+    joint_ref[:, :coarse_len] = fold3(rhs)
+    joint_ref[:, coarse_len:] = block
     stride = coarse_ref.shape[0] // coarse_len
     for tile in range(stride):
         at = slice(tile * LANES, (tile + 1) * LANES)
@@ -106,11 +108,12 @@
 
 
 def coarse_kernel(
-    width, rows, tiles, packed_ref, core_ref, rhs_ref, far_ref, hi_ref, low_ref, send_ref, parts_ref
+    width, rows, tiles, packed_ref, core_ref, joint_ref, far_ref, hi_ref, low_ref, send_ref, parts_ref
 ):
     parts_ref[0] = split3(block_rows(packed_ref, rows, 0, tiles))
     parts_ref[1] = split3(core_ref[...])
-    rhs = rhs_ref[...] + far_ref[...]
+    coarse_len = hi_ref.shape[0]
+    rhs = joint_ref[:, :coarse_len] + far_ref[:, :coarse_len]
     half = rows // 2
     lane = lax.broadcasted_iota(jnp.int32, (half, LANES), 1)
     step = 2 * LANES
@@ -130,12 +133,12 @@
                     send_ref[to + 1, copy, core] = right[piece]
 
 
-def margin_kernel(tiles, near_ref, y_ref, both_ref, lists_ref, out_ref, far_ref):
+def margin_kernel(near_ref, y_ref, both_ref, lists_ref, out_ref, far_ref):
     half, rows, cols = near_ref.shape
     wanted = jnp.where(facing() == 1, lists_ref[1:2], lists_ref[0:1])
     local = lax.broadcasted_iota(jnp.int32, (cols, wanted.shape[1]), 0)
-    for k, ref in enumerate((y_ref, both_ref)):
-        far_ref[k] = split3(block_rows(ref, rows // 3, 0, tiles))
+    far_ref[0] = split3(y_ref[:, y_ref.shape[1] - cols :])
+    far_ref[1] = split3(both_ref[...])
     total = jnp.zeros((rows, wanted.shape[1]), F32)
     for k in range(2 * half):
         part = near_ref[k] if k < half else far_ref[k - half]
@@ -289,10 +292,10 @@
     over_core = lax.ppermute(residual, "blk", core_swap)
     core_codes = lax.ppermute(aggregate, "blk", core_swap)[None]
 
-    rhs, m_hi, m_low = pl.pallas_call(
+    joint, m_hi, m_low = pl.pallas_call(
         functools.partial(near_kernel, rows, tiles),
         out_shape=(
-            jax.ShapeDtypeStruct((rows, coarse_len), F32),
+            jax.ShapeDtypeStruct((rows, coarse_len + cols), F32),
             jax.ShapeDtypeStruct((coarse_len, subs * width), BF16),
             jax.ShapeDtypeStruct((coarse_len, subs * width), BF16),
         ),
@@ -302,9 +305,8 @@
         cost_estimate=weight(2 * 10**9),
         name="near",
     )(packed, over_core, core_codes, table)
-    far_rhs = lax.ppermute(rhs, "blk", far_swap)
-    over_y = lax.ppermute(packed, "blk", far_swap)
-    over_both = lax.ppermute(packed, "blk", both_swap)
+    over_y = lax.ppermute(joint, "blk", far_swap)
+    over_both = lax.ppermute(residual, "blk", both_swap)
     send, near = pl.pallas_call(
         functools.partial(coarse_kernel, width, rows, tiles),
         out_shape=(
@@ -316,13 +318,13 @@
         compiler_params=limit(12),
         cost_estimate=weight(8 * 10**9),
         name="coarse",
-    )(packed, over_core, rhs, far_rhs, m_hi, m_low)
+    )(packed, over_core, joint, over_y, m_hi, m_low)
     flat = send.reshape((subs * shards,) + send.shape[3:])
     got = lax.all_to_all(flat, ("sub", "blk"), 0, 0, tiled=True)
     got = got.reshape((subs, shards) + flat.shape[1:])
 
     outgoing, far = pl.pallas_call(
-        functools.partial(margin_kernel, tiles),
+        margin_kernel,
         out_shape=(
             jax.ShapeDtypeStruct((rows, margin), F32),
             jax.ShapeDtypeStruct((shards - 2, 3 * rows, cols), BF16),

time: 25.7 us -> 26.6 us (1.035)
  starting transfers between devices: 16.3 us -> 17.3 us
    all_to_all x1, starting transfers between devices: 3.97 us -> 6.46 us  [on_device(): got = lax.all_to_all(flat, ('sub', 'blk'), 0, 0, tiled=True)]
    ppermute x3 -> x2, starting transfers between devices: 4.44 us -> 2.87 us  [the longest x1 2.87 us: on_device(): over_y = lax.ppermute(joint, 'blk', far_swap)]
  transfers between devices with their start and end apart: 10 -> 9, of which waited for: 3 -> 3; matrix products, arithmetic and copies ran while one was open for 0% -> 0% of each run, Pallas kernels for 22% -> 21%
where the time goes in v9:
time: 26.6 us; the launch traced here: 26.4 us
  starting transfers between devices  17.3 us (65%)
  Pallas kernels  6.71 us (25%)
  waiting for transfers between devices  2.28 us (9%)
    all_to_all x1, starting transfers between devices, on_device(): got = lax.all_to_all(flat, ('sub', 'blk'), 0, 0, tiled=True)  6.46 us
    ppermute x1, starting transfers between devices, on_device(): halo = lax.ppermute(outgoing, ('sub', 'blk'), neighbours)  3.69 us
    ppermute x1, starting transfers between devices, on_device(): lists = lax.ppermute(lists, ('sub', 'blk'), neighbours)  3.44 us
    ppermute x1, starting transfers between devices, on_device(): over_y = lax.ppermute(joint, 'blk', far_swap)  2.87 us
    pallas_call x1, Pallas kernels, on_device(): pl.pallas_call(functools.partial(own_kernel, margin), out_shape=(jax.Shap...  2.67 us
    all_to_all x1, waiting for transfers between devices, on_device(): got = lax.all_to_all(flat, ('sub', 'blk'), 0, 0, tiled=True)  1.28 us
    pallas_call x1, Pallas kernels, on_device(): pl.pallas_call(pack_kernel, out_shape=(jax.ShapeDtypeStruct(packed_shape,...  1.17 us
    pallas_call x1, Pallas kernels, on_device(): pl.pallas_call(functools.partial(coarse_kernel, width, rows, tiles), out_...  0.94 us
  transfers between devices with their start and end apart: 9, of which 3 were waited for; matrix products, arithmetic and copies ran while one was open for 0% of the time, Pallas kernels for 21%

profile of v9, /device:TPU:0, one launch (start us, length us, event | category | flops | bytes accessed | tf_op | source)
XLA Modules:
  0.0 26.4 jit_solution(2527075404663815415)
XLA Ops:
  0.0 0.5 %collective-permute-start.1 = (s32[512]{0:T(512)}, s32[512]{0:T(512)S(1)}, u32[]{:S(2)}, u32[]{:S(2)}) collective-permute-start(s32[512]{0:T(512)} %param.11), channel_id=1, source_target_pairs={{0,1},{1,0},{2,3},{3,2},{4,5},{5,4},{6,7},{7,6},{8,9},{9,8},{10,11... | collective-permute-start | bytes 6152 | tf_op jit(solution)/shard_map/ppermute | solution.py:293
  0.5 0.1 collective-permute-start
  0.5 1.2 %pack.1 = (f32[136,128]{1,0:T(8,128)S(1)}, s32[2,256]{1,0:T(2,128)S(1)}, f32[1024,128]{1,0:T(8,128)S(1)}) custom-call(f32[32,512]{1,0:T(8,128)} %residual_ref.1, s32[1,512]{1,0:T(1,128)} %bitcast.10, s32[2,256]{1,0:T(2,128)} %bitcast.9, s32[1,2]{1,0:T(1,128)} %counts_ref.1, f32[1024,128]{1,0:T(8,128)} %bitcast.8), custom_call_target="tpu_custom_call" | custom-call | flops 8000000000 | tf_op jit(solution)/shard_map/pack/pallas_call | solution.py:271
  1.7 0.0 copy-start
  1.7 0.0 collective-permute-done.1
  1.7 0.2 collective-permute-done.core_ref
  1.9 0.3 %near.1 = (f32[32,768]{1,0:T(8,128)S(1)}, bf16[256,512]{1,0:T(8,128)(2,1)S(1)}, bf16[256,512]{1,0:T(8,128)(2,1)S(1)}) custom-call(f32[136,128]{1,0:T(8,128)S(1)} %get-tuple-element.21.packed_ref, f32[32,512]{1,0:T(8,128)S(1)} %collective-permute-done.core_ref, s32[1,512]{1,0:T(1,128)S(1)} %bitcast.7, f32[1024,128]{1,0:T(8,128)S(1)} %get-tuple-element.22.coarse_ref), custom_call_target="tpu_custom_call" | custom-call | flops 2000000000 | tf_op jit(solution)/shard_map/near/pallas_call | solution.py:295
  2.3 2.9 %collective-permute-start.2 = (f32[32,768]{1,0:T(8,128)S(1)}, f32[32,768]{1,0:T(8,128)S(1)}, u32[]{:S(2)}, u32[]{:S(2)}) collective-permute-start(f32[32,768]{1,0:T(8,128)S(1)} %get-tuple-element.23.joint_ref), channel_id=1, source_target_pairs={{0,2},{1,3},{2,0},{3,1},{4,6},{5,7},{6,4},{7,5},{8,10},{9,11},{10,... | collective-permute-start | bytes 294920 | tf_op jit(solution)/shard_map/ppermute | solution.py:308
  5.1 0.0 copy-done
  5.1 0.0 collective-permute-start.4
  5.1 3.4 %collective-permute-start.5 = (s32[2,256]{1,0:T(2,128)S(1)}, s32[2,256]{1,0:T(2,128)S(1)}, u32[]{:S(2)}, u32[]{:S(2)}) collective-permute-start(s32[2,256]{1,0:T(2,128)S(1)} %get-tuple-element.28), channel_id=1, source_target_pairs={{0,4},{2,6},{4,0},{5,9},{6,2},{7,11},{8,12},{9,5},{10,14},{11,7},{... | collective-permute-start | bytes 6152 | tf_op jit(solution)/shard_map/ppermute | solution.py:291
  8.6 0.0 collective-permute-done.2.far_ref.y_ref
  8.6 0.9 %coarse.1 = (f32[8,2,2,8,128]{4,3,2,1,0:T(8,128)}, bf16[2,96,512]{2,1,0:T(8,128)(2,1)S(1)}) custom-call(f32[136,128]{1,0:T(8,128)S(1)} %get-tuple-element.21.packed_ref, f32[32,512]{1,0:T(8,128)S(1)} %collective-permute-done.core_ref, f32[32,768]{1,0:T(8,128)S(1)} %get-tuple-element.23.joint_ref, f32[32,768]{1,0:T(8,128)S(1)} %collective-permute-done.2.far_ref.y_ref, ...), custom_call_target="tpu_custom_call" | custom-call | flops 8000000000 | tf_op jit(solution)/shard_map/coarse/pallas_call | solution.py:310
  9.6 6.5 %all-to-all-start = ((f32[32,8,128]{2,1,0:T(8,128)}), f32[32,8,128]{2,1,0:T(8,128)S(1)}, u32[]{:S(2)}, u32[]{:S(2)}) async-start(f32[32,8,128]{2,1,0:T(8,128)} %bitcast.4), calls=%async_computation | async-start | bytes 262144 | tf_op jit(solution)/shard_map/all_to_all | solution.py:323
  16.0 0.0 collective-permute-done.5.lists_ref
  16.0 0.0 collective-permute-done.4.both_ref
  16.0 0.3 %margins.1 = (f32[32,256]{1,0:T(8,128)S(1)}, bf16[2,96,512]{2,1,0:T(8,128)(2,1)S(1)}) custom-call(bf16[2,96,512]{2,1,0:T(8,128)(2,1)S(1)} %get-tuple-element.27.near_ref, f32[32,768]{1,0:T(8,128)S(1)} %collective-permute-done.2.far_ref.y_ref, f32[32,512]{1,0:T(8,128)S(1)} %collective-permute-done.4.both_ref, s32[2,256]{1,0:T(2,128)S(1)} %collective-permute-done.5.lists_ref), custom_call_target="tpu_custom_call" | custom-call | flops 4000000000 | tf_op jit(solution)/shard_map/margins/pallas_call | solution.py:326
  16.4 3.7 %collective-permute-start.6 = (f32[32,256]{1,0:T(8,128)S(1)}, f32[32,256]{1,0:T(8,128)S(1)}, u32[]{:S(2)}, u32[]{:S(2)}) collective-permute-start(f32[32,256]{1,0:T(8,128)S(1)} %get-tuple-element.31), channel_id=1, source_target_pairs={{0,4},{2,6},{4,0},{5,9},{6,2},{7,11},{8,12},{9,5},{10,14},{11,7},{... | collective-permute-start | bytes 98312 | tf_op jit(solution)/shard_map/ppermute | solution.py:338
  20.1 2.7 %owned.1 = (f32[32,512]{1,0:T(8,128)S(1)}, bf16[2,256,512]{2,1,0:T(8,128)(2,1)S(1)}, bf16[2,256,512]{2,1,0:T(8,128)(2,1)S(1)}, bf16[256,512]{1,0:T(8,128)(2,1)S(1)}) custom-call(bf16[2,96,512]{2,1,0:T(8,128)(2,1)S(1)} %get-tuple-element.27.near_ref, bf16[2,96,512]{2,1,0:T(8,128)(2,1)S(1)} %get-tuple-element.29.far_ref, s32[1,512]{1,0:T(1,128)} %bitcast.11, ...), custom_call_target="tpu_custom_call" | custom-call | flops 40000000000 | tf_op jit(solution)/shard_map/owned/pallas_call | solution.py:340
  22.7 0.0 collective-permute-done.6.halo_ref
  22.7 0.2 mine.1
  22.9 0.0 collective-permute-start.7
  23.0 1.3 %all-to-all-done = f32[32,8,128]{2,1,0:T(8,128)S(1)} async-done(((f32[32,8,128]{2,1,0:T(8,128)}), f32[32,8,128]{2,1,0:T(8,128)S(1)}, u32[]{:S(2)}, u32[]{:S(2)}) %all-to-all-start) | async-done | bytes 131104 | tf_op jit(solution)/shard_map/all_to_all | solution.py:323
  24.3 0.3 %collective-permute-start.3 = (f32[4,8,128]{2,1,0:T(8,128)S(1)}, f32[4,8,128]{2,1,0:T(8,128)S(1)}, u32[]{:S(2)}, u32[]{:S(2)}) collective-permute-start(f32[4,8,128]{2,1,0:T(8,128)S(1)} %reduce.1.mine_ref), channel_id=1, source_target_pairs={{0,1},{1,0},{2,3},{3,2},{4,5},{5,4},{6,7},{7,6},{8,9},{9,8},{10,11... | collective-permute-start | bytes 49160 | tf_op jit(solution)/shard_map/ppermute | solution.py:392
  24.5 0.0 collective-permute-done.7.halo_ref
  24.5 0.2 other.1.total_ref
  24.7 0.8 %collective-permute-done.3.other_ref = f32[4,8,128]{2,1,0:T(8,128)S(1)} collective-permute-done((f32[4,8,128]{2,1,0:T(8,128)S(1)}, f32[4,8,128]{2,1,0:T(8,128)S(1)}, u32[]{:S(2)}, u32[]{:S(2)}) %collective-permute-start.3) | collective-permute-done | bytes 16416 | tf_op jit(solution)/shard_map/ppermute | solution.py:392
  25.5 0.9 %tail.1 = f32[32,512]{1,0:T(8,128)} custom-call(f32[4,8,128]{2,1,0:T(8,128)S(1)} %reduce.1.mine_ref, f32[4,8,128]{2,1,0:T(8,128)S(1)} %collective-permute-done.3.other_ref, bf16[256,512]{1,0:T(8,128)(2,1)S(1)} %get-tuple-element.30.hot_ref, f32[32,512]{1,0:T(8,128)S(1)} %other.1.total_ref), custom_call_target="tpu_custom_call" | custom-call | tf_op jit(solution)/shard_map/tail/pallas_call | solution.py:394
  (1 shorter events, 0.0 us)
Async XLA Ops:
  0.0 1.7 %collective-permute-start.1 = (s32[512]{0:T(512)}, s32[512]{0:T(512)S(1)}, u32[]{:S(2)}, u32[]{:S(2)}) collective-permute-start(s32[512]{0:T(512)} %param.11), channel_id=1, source_target_pairs={{0,1},{1,0},{2,3},{3,2},{4,5},{5,4},{6,7},{7,6},{8,9},{9,8},{10,11... | collective-permute-start | bytes 6152 | tf_op jit(solution)/shard_map/ppermute | solution.py:293
  0.5 1.5 %collective-permute-start = (f32[32,512]{1,0:T(8,128)}, f32[32,512]{1,0:T(8,128)S(1)}, u32[]{:S(2)}, u32[]{:S(2)}) collective-permute-start(f32[32,512]{1,0:T(8,128)} %residual_ref.1), channel_id=1, source_target_pairs={{0,1},{1,0},{2,3},{3,2},{4,5},{5,4},{6,7},{7,6},{8,9},{9,8},{10,11... | collective-permute-start | bytes 196616 | tf_op jit(solution)/shard_map/ppermute | solution.py:292
  1.7 3.5 %copy-start = (f32[32,512]{1,0:T(8,128)S(1)}, f32[32,512]{1,0:T(8,128)}, u32[]{:S(2)}) copy-start(f32[32,512]{1,0:T(8,128)} %residual_ref.1) | copy-start | bytes 196612
  2.3 6.3 %collective-permute-start.2 = (f32[32,768]{1,0:T(8,128)S(1)}, f32[32,768]{1,0:T(8,128)S(1)}, u32[]{:S(2)}, u32[]{:S(2)}) collective-permute-start(f32[32,768]{1,0:T(8,128)S(1)} %get-tuple-element.23.joint_ref), channel_id=1, source_target_pairs={{0,2},{1,3},{2,0},{3,1},{4,6},{5,7},{6,4},{7,5},{8,10},{9,11},{10,... | collective-permute-start | bytes 294920 | tf_op jit(solution)/shard_map/ppermute | solution.py:308
  5.1 10.9 %collective-permute-start.4 = (f32[32,512]{1,0:T(8,128)S(1)}, f32[32,512]{1,0:T(8,128)S(1)}, u32[]{:S(2)}, u32[]{:S(2)}) collective-permute-start(f32[32,512]{1,0:T(8,128)S(1)} %copy-done), channel_id=1, source_target_pairs={{0,3},{1,2},{2,1},{3,0},{4,7},{5,6},{6,5},{7,4},{8,11},{9,10},{10,... | collective-permute-start | bytes 196616 | tf_op jit(solution)/shard_map/ppermute | solution.py:309
  5.1 10.9 %collective-permute-start.5 = (s32[2,256]{1,0:T(2,128)S(1)}, s32[2,256]{1,0:T(2,128)S(1)}, u32[]{:S(2)}, u32[]{:S(2)}) collective-permute-start(s32[2,256]{1,0:T(2,128)S(1)} %get-tuple-element.28), channel_id=1, source_target_pairs={{0,4},{2,6},{4,0},{5,9},{6,2},{7,11},{8,12},{9,5},{10,14},{11,7},{... | collective-permute-start | bytes 6152 | tf_op jit(solution)/shard_map/ppermute | solution.py:291
  9.6 14.7 %all-to-all-start = ((f32[32,8,128]{2,1,0:T(8,128)}), f32[32,8,128]{2,1,0:T(8,128)S(1)}, u32[]{:S(2)}, u32[]{:S(2)}) async-start(f32[32,8,128]{2,1,0:T(8,128)} %bitcast.4), calls=%async_computation | async-start | bytes 262144 | tf_op jit(solution)/shard_map/all_to_all | solution.py:323
  16.4 6.4 %collective-permute-start.6 = (f32[32,256]{1,0:T(8,128)S(1)}, f32[32,256]{1,0:T(8,128)S(1)}, u32[]{:S(2)}, u32[]{:S(2)}) collective-permute-start(f32[32,256]{1,0:T(8,128)S(1)} %get-tuple-element.31), channel_id=1, source_target_pairs={{0,4},{2,6},{4,0},{5,9},{6,2},{7,11},{8,12},{9,5},{10,14},{11,7},{... | collective-permute-start | bytes 98312 | tf_op jit(solution)/shard_map/ppermute | solution.py:338
  22.9 1.6 %collective-permute-start.7 = (f32[32,256]{1,0:T(8,128)S(1)}, f32[32,256]{1,0:T(8,128)S(1)}, u32[]{:S(2)}, u32[]{:S(2)}) collective-permute-start(f32[32,256]{1,0:T(8,128)S(1)} %get-tuple-element.35), channel_id=1, source_target_pairs={{0,1},{1,0},{2,3},{3,2},{4,5},{5,4},{6,7},{7,6},{8,9},{9,8},{10,11... | collective-permute-start | bytes 98312 | tf_op jit(solution)/shard_map/ppermute | solution.py:372
  24.3 1.2 %collective-permute-start.3 = (f32[4,8,128]{2,1,0:T(8,128)S(1)}, f32[4,8,128]{2,1,0:T(8,128)S(1)}, u32[]{:S(2)}, u32[]{:S(2)}) collective-permute-start(f32[4,8,128]{2,1,0:T(8,128)S(1)} %reduce.1.mine_ref), channel_id=1, source_target_pairs={{0,1},{1,0},{2,3},{3,2},{4,5},{5,4},{6,7},{7,6},{8,9},{9,8},{10,11... | collective-permute-start | bytes 49160 | tf_op jit(solution)/shard_map/ppermute | solution.py:392

commit v10 on v8

--- a/solution.py
+++ b/solution.py
@@ -106,7 +106,8 @@
 
 
 def coarse_kernel(
-    width, rows, tiles, packed_ref, core_ref, rhs_ref, far_ref, hi_ref, low_ref, send_ref, parts_ref
+    width, rows, tiles, sub_order, blk_order,
+    packed_ref, core_ref, rhs_ref, far_ref, hi_ref, low_ref, send_ref, parts_ref,
 ):
     parts_ref[0] = split3(block_rows(packed_ref, rows, 0, tiles))
     parts_ref[1] = split3(core_ref[...])
@@ -123,11 +124,12 @@
             turned = pltpu.roll(part, width, 1)
             left = jnp.where(lane < width, part[:half], turned[half:])
             right = jnp.where(lane < width, turned[:half], part[half:])
-            for copy in range(send_ref.shape[1]):
+            for copy in range(send_ref.shape[1] // 2):
                 for core in range(2):
                     piece = slice(core * half // 2, (core + 1) * half // 2)
-                    send_ref[to, copy, core] = left[piece]
-                    send_ref[to + 1, copy, core] = right[piece]
+                    at = blk_order.index(2 * copy + core)
+                    send_ref[sub_order.index(to), at] = left[piece]
+                    send_ref[sub_order.index(to + 1), at] = right[piece]
 
 
 def margin_kernel(tiles, near_ref, y_ref, both_ref, lists_ref, out_ref, far_ref):
@@ -202,11 +204,12 @@
     out_ref[...] = total_ref[...] + dot_halves(halo_ref[...], hi_ref[side], low_ref[side])
 
 
-def reduce_kernel(got_ref, out_ref):
+def reduce_kernel(blk_order, got_ref, out_ref):
     total = got_ref[0]
     for sub in range(1, got_ref.shape[0]):
         total = total + got_ref[sub]
-    out_ref[...] = total
+    for k, b in enumerate(blk_order):
+        out_ref[b] = total[k]
 
 
 def tail_kernel(width, mine_ref, other_ref, hot_ref, total_ref, out_ref):
@@ -249,8 +252,10 @@
     margin = wanted_rows.shape[2]
     coarse_len = coarse_inverse.shape[0]
     width = coarse_len // shards
-    chips = shards // 2
     packed_rows = -(-(rows * tiles + tiles) // 8) * 8
+    lead = (subs // 2 + 1) % subs
+    sub_order = [(lead + k) % subs for k in range(subs)]
+    blk_order = [b ^ 2 for b in range(shards)]
     core_swap = [(b, b ^ 1) for b in range(shards)]
     far_swap = [(b, b ^ 2) for b in range(shards)]
     both_swap = [(b, b ^ 3) for b in range(shards)]
@@ -306,9 +311,9 @@
     over_y = lax.ppermute(packed, "blk", far_swap)
     over_both = lax.ppermute(packed, "blk", both_swap)
     send, near = pl.pallas_call(
-        functools.partial(coarse_kernel, width, rows, tiles),
-        out_shape=(
-            jax.ShapeDtypeStruct((subs, chips, 2, rows // 4, LANES), F32),
+        functools.partial(coarse_kernel, width, rows, tiles, sub_order, blk_order),
+        out_shape=(
+            jax.ShapeDtypeStruct((subs, shards, rows // 4, LANES), F32),
             jax.ShapeDtypeStruct((2, 3 * rows, cols), BF16),
         ),
         in_specs=[whole()] * 6,
@@ -317,8 +322,9 @@
         cost_estimate=weight(8 * 10**9),
         name="coarse",
     )(packed, over_core, rhs, far_rhs, m_hi, m_low)
-    flat = send.reshape((subs * shards,) + send.shape[3:])
-    got = lax.all_to_all(flat, ("sub", "blk"), 0, 0, tiled=True)
+    flat = send.reshape((subs * shards,) + send.shape[2:])
+    members = [sub * shards + b for sub in sub_order for b in blk_order]
+    got = lax.all_to_all(flat, ("sub", "blk"), 0, 0, axis_index_groups=[members], tiled=True)
     got = got.reshape((subs, shards) + flat.shape[1:])
 
     outgoing, far = pl.pallas_call(
@@ -379,7 +385,7 @@
     )(other, w_hi, w_low, fine)
 
     sums = pl.pallas_call(
-        reduce_kernel,
+        functools.partial(reduce_kernel, blk_order),
         out_shape=jax.ShapeDtypeStruct(got.shape[1:], F32),
         in_specs=[whole()],
         out_specs=whole(),

time: 25.7 us -> 25.1 us (0.977)
  waiting for transfers between devices: 2.28 us -> 1.5 us
    all_to_all x1, waiting for transfers between devices: 1.26 us -> 0.62 us  [on_device(): lax.all_to_all(flat, ('sub', 'blk'), 0, 0, axis_index_groups=[members], t...]
  transfers between devices with their start and end apart: 10 -> 10, of which waited for: 3 -> 4; matrix products, arithmetic and copies ran while one was open for 0% -> 0% of each run, Pallas kernels for 22% -> 22%
where the time goes in v10:
time: 25.1 us; the launch traced here: 24.8 us
  starting transfers between devices  16.5 us (66%)
  Pallas kernels  6.71 us (27%)
  waiting for transfers between devices  1.5 us (6%)
    all_to_all x1, starting transfers between devices, on_device(): lax.all_to_all(flat, ('sub', 'blk'), 0, 0, axis_index_groups=[members], t...  3.97 us
    ppermute x1, starting transfers between devices, on_device(): halo = lax.ppermute(outgoing, ('sub', 'blk'), neighbours)  3.69 us
    ppermute x1, starting transfers between devices, on_device(): lists = lax.ppermute(lists, ('sub', 'blk'), neighbours)  3.39 us
    ppermute x1, starting transfers between devices, on_device(): far_rhs = lax.ppermute(rhs, 'blk', far_swap)  2.83 us
    pallas_call x1, Pallas kernels, on_device(): pl.pallas_call(functools.partial(own_kernel, margin), out_shape=(jax.Shap...  2.67 us
    ppermute x1, starting transfers between devices, on_device(): over_y = lax.ppermute(packed, 'blk', far_swap)  1.61 us
    pallas_call x1, Pallas kernels, on_device(): pl.pallas_call(pack_kernel, out_shape=(jax.ShapeDtypeStruct(packed_shape,...  1.17 us
    pallas_call x1, Pallas kernels, on_device(): pl.pallas_call(functools.partial(coarse_kernel, width, rows, tiles, sub_o...  0.94 us
  transfers between devices with their start and end apart: 10, of which 4 were waited for; matrix products, arithmetic and copies ran while one was open for 0% of the time, Pallas kernels for 22%

profile of v10, /device:TPU:0, one launch (start us, length us, event | category | flops | bytes accessed | tf_op | source)
XLA Modules:
  0.0 24.8 jit_solution(4885374473965869729)
XLA Ops:
  0.0 0.5 %collective-permute-start.1 = (s32[512]{0:T(512)}, s32[512]{0:T(512)S(1)}, u32[]{:S(2)}, u32[]{:S(2)}) collective-permute-start(s32[512]{0:T(512)} %param.11), channel_id=1, source_target_pairs={{0,1},{1,0},{2,3},{3,2},{4,5},{5,4},{6,7},{7,6},{8,9},{9,8},{10,11... | collective-permute-start | bytes 6152 | tf_op jit(solution)/shard_map/ppermute | solution.py:295
  0.5 0.1 collective-permute-start
  0.5 1.2 %pack.1 = (f32[136,128]{1,0:T(8,128)S(1)}, s32[2,256]{1,0:T(2,128)S(1)}, f32[1024,128]{1,0:T(8,128)S(1)}) custom-call(f32[32,512]{1,0:T(8,128)} %residual_ref.1, s32[1,512]{1,0:T(1,128)} %bitcast.10, s32[2,256]{1,0:T(2,128)} %bitcast.9, s32[1,2]{1,0:T(1,128)} %counts_ref.1, f32[1024,128]{1,0:T(8,128)} %bitcast.8), custom_call_target="tpu_custom_call" | custom-call | flops 8000000000 | tf_op jit(solution)/shard_map/pack/pallas_call | solution.py:273
  1.7 0.0 collective-permute-done.1
  1.7 0.2 collective-permute-done.core_ref
  1.9 0.3 %near.1 = (f32[32,256]{1,0:T(8,128)S(1)}, bf16[256,512]{1,0:T(8,128)(2,1)S(1)}, bf16[256,512]{1,0:T(8,128)(2,1)S(1)}) custom-call(f32[136,128]{1,0:T(8,128)S(1)} %get-tuple-element.21.packed_ref, f32[32,512]{1,0:T(8,128)S(1)} %collective-permute-done.core_ref, s32[1,512]{1,0:T(1,128)S(1)} %bitcast.7, f32[1024,128]{1,0:T(8,128)S(1)} %get-tuple-element.22.coarse_ref), custom_call_target="tpu_custom_call" | custom-call | flops 2000000000 | tf_op jit(solution)/shard_map/near/pallas_call | solution.py:297
  2.3 2.8 %collective-permute-start.2 = (f32[32,256]{1,0:T(8,128)S(1)}, f32[32,256]{1,0:T(8,128)S(1)}, u32[]{:S(2)}, u32[]{:S(2)}) collective-permute-start(f32[32,256]{1,0:T(8,128)S(1)} %get-tuple-element.23.rhs_ref), channel_id=1, source_target_pairs={{0,2},{1,3},{2,0},{3,1},{4,6},{5,7},{6,4},{7,5},{8,10},{9,11},{10,... | collective-permute-start | bytes 98312 | tf_op jit(solution)/shard_map/ppermute | solution.py:310
  5.1 0.0 collective-permute-start.5
  5.1 1.6 %collective-permute-start.4 = (f32[136,128]{1,0:T(8,128)S(1)}, f32[136,128]{1,0:T(8,128)S(1)}, u32[]{:S(2)}, u32[]{:S(2)}) collective-permute-start(f32[136,128]{1,0:T(8,128)S(1)} %get-tuple-element.21.packed_ref), channel_id=1, source_target_pairs={{0,2},{1,3},{2,0},{3,1},{4,6},{5,7},{6,4},{7,5},{8,10},{9,11},{10,... | collective-permute-start | bytes 208904 | tf_op jit(solution)/shard_map/ppermute | solution.py:311
  6.7 3.4 %collective-permute-start.6 = (s32[2,256]{1,0:T(2,128)S(1)}, s32[2,256]{1,0:T(2,128)S(1)}, u32[]{:S(2)}, u32[]{:S(2)}) collective-permute-start(s32[2,256]{1,0:T(2,128)S(1)} %get-tuple-element.28), channel_id=1, source_target_pairs={{0,4},{2,6},{4,0},{5,9},{6,2},{7,11},{8,12},{9,5},{10,14},{11,7},{... | collective-permute-start | bytes 6152 | tf_op jit(solution)/shard_map/ppermute | solution.py:293
  10.1 0.0 collective-permute-done.2.far_ref
  10.1 0.9 %coarse.1 = (f32[8,4,8,128]{3,2,1,0:T(8,128)}, bf16[2,96,512]{2,1,0:T(8,128)(2,1)S(1)}) custom-call(f32[136,128]{1,0:T(8,128)S(1)} %get-tuple-element.21.packed_ref, f32[32,512]{1,0:T(8,128)S(1)} %collective-permute-done.core_ref, f32[32,256]{1,0:T(8,128)S(1)} %get-tuple-element.23.rhs_ref, f32[32,256]{1,0:T(8,128)S(1)} %collective-permute-done.2.far_ref, ...), custom_call_target="tpu_custom_call" | custom-call | flops 8000000000 | tf_op jit(solution)/shard_map/coarse/pallas_call | solution.py:313
  11.1 4.0 %all-to-all-start = ((f32[32,8,128]{2,1,0:T(8,128)}), f32[32,8,128]{2,1,0:T(8,128)S(1)}, u32[]{:S(2)}, u32[]{:S(2)}) async-start(f32[32,8,128]{2,1,0:T(8,128)} %bitcast.4), calls=%async_computation | async-start | bytes 262144 | tf_op jit(solution)/shard_map/all_to_all | solution.py:327
  15.0 0.0 collective-permute-done.6.lists_ref
  15.1 0.0 collective-permute-done.5.both_ref
  15.1 0.0 collective-permute-done.4.y_ref
  15.1 0.3 %margins.1 = (f32[32,256]{1,0:T(8,128)S(1)}, bf16[2,96,512]{2,1,0:T(8,128)(2,1)S(1)}) custom-call(bf16[2,96,512]{2,1,0:T(8,128)(2,1)S(1)} %get-tuple-element.27.near_ref, f32[136,128]{1,0:T(8,128)S(1)} %collective-permute-done.4.y_ref, f32[136,128]{1,0:T(8,128)S(1)} %collective-permute-done.5.both_ref, s32[2,256]{1,0:T(2,128)S(1)} %collective-permute-done.6.lists_ref), custom_call_target="tpu_custom_call" | custom-call | flops 4000000000 | tf_op jit(solution)/shard_map/margins/pallas_call | solution.py:330
  15.4 3.7 %collective-permute-start.7 = (f32[32,256]{1,0:T(8,128)S(1)}, f32[32,256]{1,0:T(8,128)S(1)}, u32[]{:S(2)}, u32[]{:S(2)}) collective-permute-start(f32[32,256]{1,0:T(8,128)S(1)} %get-tuple-element.31), channel_id=1, source_target_pairs={{0,4},{2,6},{4,0},{5,9},{6,2},{7,11},{8,12},{9,5},{10,14},{11,7},{... | collective-permute-start | bytes 98312 | tf_op jit(solution)/shard_map/ppermute | solution.py:342
  19.1 2.7 %owned.1 = (f32[32,512]{1,0:T(8,128)S(1)}, bf16[2,256,512]{2,1,0:T(8,128)(2,1)S(1)}, bf16[2,256,512]{2,1,0:T(8,128)(2,1)S(1)}, bf16[256,512]{1,0:T(8,128)(2,1)S(1)}) custom-call(bf16[2,96,512]{2,1,0:T(8,128)(2,1)S(1)} %get-tuple-element.27.near_ref, bf16[2,96,512]{2,1,0:T(8,128)(2,1)S(1)} %get-tuple-element.29.far_ref, s32[1,512]{1,0:T(1,128)} %bitcast.11, ...), custom_call_target="tpu_custom_call" | custom-call | flops 40000000000 | tf_op jit(solution)/shard_map/owned/pallas_call | solution.py:344
  21.8 0.0 collective-permute-done.7.halo_ref
  21.8 0.2 mine.1
  22.0 0.0 collective-permute-start.8
  22.0 0.6 %all-to-all-done = f32[32,8,128]{2,1,0:T(8,128)S(1)} async-done(((f32[32,8,128]{2,1,0:T(8,128)}), f32[32,8,128]{2,1,0:T(8,128)S(1)}, u32[]{:S(2)}, u32[]{:S(2)}) %all-to-all-start) | async-done | bytes 131104 | tf_op jit(solution)/shard_map/all_to_all | solution.py:327
  22.6 0.5 %collective-permute-start.3 = (f32[4,8,128]{2,1,0:T(8,128)S(1)}, f32[4,8,128]{2,1,0:T(8,128)S(1)}, u32[]{:S(2)}, u32[]{:S(2)}) collective-permute-start(f32[4,8,128]{2,1,0:T(8,128)S(1)} %reduce.1.mine_ref), channel_id=1, source_target_pairs={{0,1},{1,0},{2,3},{3,2},{4,5},{5,4},{6,7},{7,6},{8,9},{9,8},{10,11... | collective-permute-start | bytes 49160 | tf_op jit(solution)/shard_map/ppermute | solution.py:396
  23.1 0.1 collective-permute-done.8.halo_ref
  23.2 0.2 other.1.total_ref
  23.4 0.6 %collective-permute-done.3.other_ref = f32[4,8,128]{2,1,0:T(8,128)S(1)} collective-permute-done((f32[4,8,128]{2,1,0:T(8,128)S(1)}, f32[4,8,128]{2,1,0:T(8,128)S(1)}, u32[]{:S(2)}, u32[]{:S(2)}) %collective-permute-start.3) | collective-permute-done | bytes 16416 | tf_op jit(solution)/shard_map/ppermute | solution.py:396
  24.0 0.9 %tail.1 = f32[32,512]{1,0:T(8,128)} custom-call(f32[4,8,128]{2,1,0:T(8,128)S(1)} %reduce.1.mine_ref, f32[4,8,128]{2,1,0:T(8,128)S(1)} %collective-permute-done.3.other_ref, bf16[256,512]{1,0:T(8,128)(2,1)S(1)} %get-tuple-element.30.hot_ref, f32[32,512]{1,0:T(8,128)S(1)} %other.1.total_ref), custom_call_target="tpu_custom_call" | custom-call | tf_op jit(solution)/shard_map/tail/pallas_call | solution.py:398
  (1 shorter events, 0.0 us)
Async XLA Ops:
  0.0 1.7 %collective-permute-start.1 = (s32[512]{0:T(512)}, s32[512]{0:T(512)S(1)}, u32[]{:S(2)}, u32[]{:S(2)}) collective-permute-start(s32[512]{0:T(512)} %param.11), channel_id=1, source_target_pairs={{0,1},{1,0},{2,3},{3,2},{4,5},{5,4},{6,7},{7,6},{8,9},{9,8},{10,11... | collective-permute-start | bytes 6152 | tf_op jit(solution)/shard_map/ppermute | solution.py:295
  0.5 1.5 %collective-permute-start = (f32[32,512]{1,0:T(8,128)}, f32[32,512]{1,0:T(8,128)S(1)}, u32[]{:S(2)}, u32[]{:S(2)}) collective-permute-start(f32[32,512]{1,0:T(8,128)} %residual_ref.1), channel_id=1, source_target_pairs={{0,1},{1,0},{2,3},{3,2},{4,5},{5,4},{6,7},{7,6},{8,9},{9,8},{10,11... | collective-permute-start | bytes 196616 | tf_op jit(solution)/shard_map/ppermute | solution.py:294
  2.3 7.8 %collective-permute-start.2 = (f32[32,256]{1,0:T(8,128)S(1)}, f32[32,256]{1,0:T(8,128)S(1)}, u32[]{:S(2)}, u32[]{:S(2)}) collective-permute-start(f32[32,256]{1,0:T(8,128)S(1)} %get-tuple-element.23.rhs_ref), channel_id=1, source_target_pairs={{0,2},{1,3},{2,0},{3,1},{4,6},{5,7},{6,4},{7,5},{8,10},{9,11},{10,... | collective-permute-start | bytes 98312 | tf_op jit(solution)/shard_map/ppermute | solution.py:310
  5.1 10.0 %collective-permute-start.5 = (f32[136,128]{1,0:T(8,128)S(1)}, f32[136,128]{1,0:T(8,128)S(1)}, u32[]{:S(2)}, u32[]{:S(2)}) collective-permute-start(f32[136,128]{1,0:T(8,128)S(1)} %get-tuple-element.21.packed_ref), channel_id=1, source_target_pairs={{0,3},{1,2},{2,1},{3,0},{4,7},{5,6},{6,5},{7,4},{8,11},{9,10},{10,... | collective-permute-start | bytes 208904 | tf_op jit(solution)/shard_map/ppermute | solution.py:312
  5.1 10.0 %collective-permute-start.4 = (f32[136,128]{1,0:T(8,128)S(1)}, f32[136,128]{1,0:T(8,128)S(1)}, u32[]{:S(2)}, u32[]{:S(2)}) collective-permute-start(f32[136,128]{1,0:T(8,128)S(1)} %get-tuple-element.21.packed_ref), channel_id=1, source_target_pairs={{0,2},{1,3},{2,0},{3,1},{4,6},{5,7},{6,4},{7,5},{8,10},{9,11},{10,... | collective-permute-start | bytes 208904 | tf_op jit(solution)/shard_map/ppermute | solution.py:311
  6.7 8.3 %collective-permute-start.6 = (s32[2,256]{1,0:T(2,128)S(1)}, s32[2,256]{1,0:T(2,128)S(1)}, u32[]{:S(2)}, u32[]{:S(2)}) collective-permute-start(s32[2,256]{1,0:T(2,128)S(1)} %get-tuple-element.28), channel_id=1, source_target_pairs={{0,4},{2,6},{4,0},{5,9},{6,2},{7,11},{8,12},{9,5},{10,14},{11,7},{... | collective-permute-start | bytes 6152 | tf_op jit(solution)/shard_map/ppermute | solution.py:293
  11.1 11.6 %all-to-all-start = ((f32[32,8,128]{2,1,0:T(8,128)}), f32[32,8,128]{2,1,0:T(8,128)S(1)}, u32[]{:S(2)}, u32[]{:S(2)}) async-start(f32[32,8,128]{2,1,0:T(8,128)} %bitcast.4), calls=%async_computation | async-start | bytes 262144 | tf_op jit(solution)/shard_map/all_to_all | solution.py:327
  15.4 6.4 %collective-permute-start.7 = (f32[32,256]{1,0:T(8,128)S(1)}, f32[32,256]{1,0:T(8,128)S(1)}, u32[]{:S(2)}, u32[]{:S(2)}) collective-permute-start(f32[32,256]{1,0:T(8,128)S(1)} %get-tuple-element.31), channel_id=1, source_target_pairs={{0,4},{2,6},{4,0},{5,9},{6,2},{7,11},{8,12},{9,5},{10,14},{11,7},{... | collective-permute-start | bytes 98312 | tf_op jit(solution)/shard_map/ppermute | solution.py:342
  22.0 1.2 %collective-permute-start.8 = (f32[32,256]{1,0:T(8,128)S(1)}, f32[32,256]{1,0:T(8,128)S(1)}, u32[]{:S(2)}, u32[]{:S(2)}) collective-permute-start(f32[32,256]{1,0:T(8,128)S(1)} %get-tuple-element.35), channel_id=1, source_target_pairs={{0,1},{1,0},{2,3},{3,2},{4,5},{5,4},{6,7},{7,6},{8,9},{9,8},{10,11... | collective-permute-start | bytes 98312 | tf_op jit(solution)/shard_map/ppermute | solution.py:376
  22.6 1.3 %collective-permute-start.3 = (f32[4,8,128]{2,1,0:T(8,128)S(1)}, f32[4,8,128]{2,1,0:T(8,128)S(1)}, u32[]{:S(2)}, u32[]{:S(2)}) collective-permute-start(f32[4,8,128]{2,1,0:T(8,128)S(1)} %reduce.1.mine_ref), channel_id=1, source_target_pairs={{0,1},{1,0},{2,3},{3,2},{4,5},{5,4},{6,7},{7,6},{8,9},{9,8},{10,11... | collective-permute-start | bytes 49160 | tf_op jit(solution)/shard_map/ppermute | solution.py:396

commit v11 on v10

--- a/solution.py
+++ b/solution.py
@@ -253,7 +253,7 @@
     coarse_len = coarse_inverse.shape[0]
     width = coarse_len // shards
     packed_rows = -(-(rows * tiles + tiles) // 8) * 8
-    lead = (subs // 2 + 1) % subs
+    lead = subs - 1
     sub_order = [(lead + k) % subs for k in range(subs)]
     blk_order = [b ^ 2 for b in range(shards)]
     core_swap = [(b, b ^ 1) for b in range(shards)]

time: 25.1 us -> 25.1 us (level)
  no operation moved by 1% of the time
where the time goes in v11:
time: 25.1 us; the launch traced here: 24.8 us
  starting transfers between devices  16.5 us (66%)
  Pallas kernels  6.71 us (27%)
  waiting for transfers between devices  1.5 us (6%)
    all_to_all x1, starting transfers between devices, on_device(): lax.all_to_all(flat, ('sub', 'blk'), 0, 0, axis_index_groups=[members], t...  3.97 us
    ppermute x1, starting transfers between devices, on_device(): halo = lax.ppermute(outgoing, ('sub', 'blk'), neighbours)  3.69 us
    ppermute x1, starting transfers between devices, on_device(): lists = lax.ppermute(lists, ('sub', 'blk'), neighbours)  3.39 us
    ppermute x1, starting transfers between devices, on_device(): far_rhs = lax.ppermute(rhs, 'blk', far_swap)  2.83 us
    pallas_call x1, Pallas kernels, on_device(): pl.pallas_call(functools.partial(own_kernel, margin), out_shape=(jax.Shap...  2.67 us
    ppermute x1, starting transfers between devices, on_device(): over_y = lax.ppermute(packed, 'blk', far_swap)  1.61 us
    pallas_call x1, Pallas kernels, on_device(): pl.pallas_call(pack_kernel, out_shape=(jax.ShapeDtypeStruct(packed_shape,...  1.17 us
    pallas_call x1, Pallas kernels, on_device(): pl.pallas_call(functools.partial(coarse_kernel, width, rows, tiles, sub_o...  0.94 us
  transfers between devices with their start and end apart: 10, of which 4 were waited for; matrix products, arithmetic and copies ran while one was open for 0% of the time, Pallas kernels for 22%

profile of v11, /device:TPU:0, one launch (start us, length us, event | category | flops | bytes accessed | tf_op | source)
XLA Modules:
  0.0 24.8 jit_solution(18040239293532284385)
XLA Ops:
  0.0 0.5 %collective-permute-start.1 = (s32[512]{0:T(512)}, s32[512]{0:T(512)S(1)}, u32[]{:S(2)}, u32[]{:S(2)}) collective-permute-start(s32[512]{0:T(512)} %param.11), channel_id=1, source_target_pairs={{0,1},{1,0},{2,3},{3,2},{4,5},{5,4},{6,7},{7,6},{8,9},{9,8},{10,11... | collective-permute-start | bytes 6152 | tf_op jit(solution)/shard_map/ppermute | solution.py:295
  0.5 0.1 collective-permute-start
  0.5 1.2 %pack.1 = (f32[136,128]{1,0:T(8,128)S(1)}, s32[2,256]{1,0:T(2,128)S(1)}, f32[1024,128]{1,0:T(8,128)S(1)}) custom-call(f32[32,512]{1,0:T(8,128)} %residual_ref.1, s32[1,512]{1,0:T(1,128)} %bitcast.10, s32[2,256]{1,0:T(2,128)} %bitcast.9, s32[1,2]{1,0:T(1,128)} %counts_ref.1, f32[1024,128]{1,0:T(8,128)} %bitcast.8), custom_call_target="tpu_custom_call" | custom-call | flops 8000000000 | tf_op jit(solution)/shard_map/pack/pallas_call | solution.py:273
  1.7 0.0 collective-permute-done.1
  1.7 0.2 collective-permute-done.core_ref
  1.9 0.3 %near.1 = (f32[32,256]{1,0:T(8,128)S(1)}, bf16[256,512]{1,0:T(8,128)(2,1)S(1)}, bf16[256,512]{1,0:T(8,128)(2,1)S(1)}) custom-call(f32[136,128]{1,0:T(8,128)S(1)} %get-tuple-element.21.packed_ref, f32[32,512]{1,0:T(8,128)S(1)} %collective-permute-done.core_ref, s32[1,512]{1,0:T(1,128)S(1)} %bitcast.7, f32[1024,128]{1,0:T(8,128)S(1)} %get-tuple-element.22.coarse_ref), custom_call_target="tpu_custom_call" | custom-call | flops 2000000000 | tf_op jit(solution)/shard_map/near/pallas_call | solution.py:297
  2.3 2.8 %collective-permute-start.2 = (f32[32,256]{1,0:T(8,128)S(1)}, f32[32,256]{1,0:T(8,128)S(1)}, u32[]{:S(2)}, u32[]{:S(2)}) collective-permute-start(f32[32,256]{1,0:T(8,128)S(1)} %get-tuple-element.23.rhs_ref), channel_id=1, source_target_pairs={{0,2},{1,3},{2,0},{3,1},{4,6},{5,7},{6,4},{7,5},{8,10},{9,11},{10,... | collective-permute-start | bytes 98312 | tf_op jit(solution)/shard_map/ppermute | solution.py:310
  5.1 0.0 collective-permute-start.5
  5.1 1.6 %collective-permute-start.4 = (f32[136,128]{1,0:T(8,128)S(1)}, f32[136,128]{1,0:T(8,128)S(1)}, u32[]{:S(2)}, u32[]{:S(2)}) collective-permute-start(f32[136,128]{1,0:T(8,128)S(1)} %get-tuple-element.21.packed_ref), channel_id=1, source_target_pairs={{0,2},{1,3},{2,0},{3,1},{4,6},{5,7},{6,4},{7,5},{8,10},{9,11},{10,... | collective-permute-start | bytes 208904 | tf_op jit(solution)/shard_map/ppermute | solution.py:311
  6.7 3.4 %collective-permute-start.6 = (s32[2,256]{1,0:T(2,128)S(1)}, s32[2,256]{1,0:T(2,128)S(1)}, u32[]{:S(2)}, u32[]{:S(2)}) collective-permute-start(s32[2,256]{1,0:T(2,128)S(1)} %get-tuple-element.28), channel_id=1, source_target_pairs={{0,4},{2,6},{4,0},{5,9},{6,2},{7,11},{8,12},{9,5},{10,14},{11,7},{... | collective-permute-start | bytes 6152 | tf_op jit(solution)/shard_map/ppermute | solution.py:293
  10.1 0.0 collective-permute-done.2.far_ref
  10.1 0.9 %coarse.1 = (f32[8,4,8,128]{3,2,1,0:T(8,128)}, bf16[2,96,512]{2,1,0:T(8,128)(2,1)S(1)}) custom-call(f32[136,128]{1,0:T(8,128)S(1)} %get-tuple-element.21.packed_ref, f32[32,512]{1,0:T(8,128)S(1)} %collective-permute-done.core_ref, f32[32,256]{1,0:T(8,128)S(1)} %get-tuple-element.23.rhs_ref, f32[32,256]{1,0:T(8,128)S(1)} %collective-permute-done.2.far_ref, ...), custom_call_target="tpu_custom_call" | custom-call | flops 8000000000 | tf_op jit(solution)/shard_map/coarse/pallas_call | solution.py:313
  11.1 4.0 %all-to-all-start = ((f32[32,8,128]{2,1,0:T(8,128)}), f32[32,8,128]{2,1,0:T(8,128)S(1)}, u32[]{:S(2)}, u32[]{:S(2)}) async-start(f32[32,8,128]{2,1,0:T(8,128)} %bitcast.4), calls=%async_computation | async-start | bytes 262144 | tf_op jit(solution)/shard_map/all_to_all | solution.py:327
  15.0 0.0 collective-permute-done.6.lists_ref
  15.1 0.0 collective-permute-done.5.both_ref
  15.1 0.0 collective-permute-done.4.y_ref
  15.1 0.3 %margins.1 = (f32[32,256]{1,0:T(8,128)S(1)}, bf16[2,96,512]{2,1,0:T(8,128)(2,1)S(1)}) custom-call(bf16[2,96,512]{2,1,0:T(8,128)(2,1)S(1)} %get-tuple-element.27.near_ref, f32[136,128]{1,0:T(8,128)S(1)} %collective-permute-done.4.y_ref, f32[136,128]{1,0:T(8,128)S(1)} %collective-permute-done.5.both_ref, s32[2,256]{1,0:T(2,128)S(1)} %collective-permute-done.6.lists_ref), custom_call_target="tpu_custom_call" | custom-call | flops 4000000000 | tf_op jit(solution)/shard_map/margins/pallas_call | solution.py:330
  15.4 3.7 %collective-permute-start.7 = (f32[32,256]{1,0:T(8,128)S(1)}, f32[32,256]{1,0:T(8,128)S(1)}, u32[]{:S(2)}, u32[]{:S(2)}) collective-permute-start(f32[32,256]{1,0:T(8,128)S(1)} %get-tuple-element.31), channel_id=1, source_target_pairs={{0,4},{2,6},{4,0},{5,9},{6,2},{7,11},{8,12},{9,5},{10,14},{11,7},{... | collective-permute-start | bytes 98312 | tf_op jit(solution)/shard_map/ppermute | solution.py:342
  19.1 2.7 %owned.1 = (f32[32,512]{1,0:T(8,128)S(1)}, bf16[2,256,512]{2,1,0:T(8,128)(2,1)S(1)}, bf16[2,256,512]{2,1,0:T(8,128)(2,1)S(1)}, bf16[256,512]{1,0:T(8,128)(2,1)S(1)}) custom-call(bf16[2,96,512]{2,1,0:T(8,128)(2,1)S(1)} %get-tuple-element.27.near_ref, bf16[2,96,512]{2,1,0:T(8,128)(2,1)S(1)} %get-tuple-element.29.far_ref, s32[1,512]{1,0:T(1,128)} %bitcast.11, ...), custom_call_target="tpu_custom_call" | custom-call | flops 40000000000 | tf_op jit(solution)/shard_map/owned/pallas_call | solution.py:344
  21.8 0.0 collective-permute-done.7.halo_ref
  21.8 0.2 mine.1
  22.0 0.0 collective-permute-start.8
  22.0 0.6 %all-to-all-done = f32[32,8,128]{2,1,0:T(8,128)S(1)} async-done(((f32[32,8,128]{2,1,0:T(8,128)}), f32[32,8,128]{2,1,0:T(8,128)S(1)}, u32[]{:S(2)}, u32[]{:S(2)}) %all-to-all-start) | async-done | bytes 131104 | tf_op jit(solution)/shard_map/all_to_all | solution.py:327
  22.6 0.5 %collective-permute-start.3 = (f32[4,8,128]{2,1,0:T(8,128)S(1)}, f32[4,8,128]{2,1,0:T(8,128)S(1)}, u32[]{:S(2)}, u32[]{:S(2)}) collective-permute-start(f32[4,8,128]{2,1,0:T(8,128)S(1)} %reduce.1.mine_ref), channel_id=1, source_target_pairs={{0,1},{1,0},{2,3},{3,2},{4,5},{5,4},{6,7},{7,6},{8,9},{9,8},{10,11... | collective-permute-start | bytes 49160 | tf_op jit(solution)/shard_map/ppermute | solution.py:396
  23.1 0.1 collective-permute-done.8.halo_ref
  23.2 0.2 other.1.total_ref
  23.4 0.6 %collective-permute-done.3.other_ref = f32[4,8,128]{2,1,0:T(8,128)S(1)} collective-permute-done((f32[4,8,128]{2,1,0:T(8,128)S(1)}, f32[4,8,128]{2,1,0:T(8,128)S(1)}, u32[]{:S(2)}, u32[]{:S(2)}) %collective-permute-start.3) | collective-permute-done | bytes 16416 | tf_op jit(solution)/shard_map/ppermute | solution.py:396
  24.0 0.9 %tail.1 = f32[32,512]{1,0:T(8,128)} custom-call(f32[4,8,128]{2,1,0:T(8,128)S(1)} %reduce.1.mine_ref, f32[4,8,128]{2,1,0:T(8,128)S(1)} %collective-permute-done.3.other_ref, bf16[256,512]{1,0:T(8,128)(2,1)S(1)} %get-tuple-element.30.hot_ref, f32[32,512]{1,0:T(8,128)S(1)} %other.1.total_ref), custom_call_target="tpu_custom_call" | custom-call | tf_op jit(solution)/shard_map/tail/pallas_call | solution.py:398
  (1 shorter events, 0.0 us)
Async XLA Ops:
  0.0 1.7 %collective-permute-start.1 = (s32[512]{0:T(512)}, s32[512]{0:T(512)S(1)}, u32[]{:S(2)}, u32[]{:S(2)}) collective-permute-start(s32[512]{0:T(512)} %param.11), channel_id=1, source_target_pairs={{0,1},{1,0},{2,3},{3,2},{4,5},{5,4},{6,7},{7,6},{8,9},{9,8},{10,11... | collective-permute-start | bytes 6152 | tf_op jit(solution)/shard_map/ppermute | solution.py:295
  0.5 1.5 %collective-permute-start = (f32[32,512]{1,0:T(8,128)}, f32[32,512]{1,0:T(8,128)S(1)}, u32[]{:S(2)}, u32[]{:S(2)}) collective-permute-start(f32[32,512]{1,0:T(8,128)} %residual_ref.1), channel_id=1, source_target_pairs={{0,1},{1,0},{2,3},{3,2},{4,5},{5,4},{6,7},{7,6},{8,9},{9,8},{10,11... | collective-permute-start | bytes 196616 | tf_op jit(solution)/shard_map/ppermute | solution.py:294
  2.3 7.8 %collective-permute-start.2 = (f32[32,256]{1,0:T(8,128)S(1)}, f32[32,256]{1,0:T(8,128)S(1)}, u32[]{:S(2)}, u32[]{:S(2)}) collective-permute-start(f32[32,256]{1,0:T(8,128)S(1)} %get-tuple-element.23.rhs_ref), channel_id=1, source_target_pairs={{0,2},{1,3},{2,0},{3,1},{4,6},{5,7},{6,4},{7,5},{8,10},{9,11},{10,... | collective-permute-start | bytes 98312 | tf_op jit(solution)/shard_map/ppermute | solution.py:310
  5.1 10.0 %collective-permute-start.5 = (f32[136,128]{1,0:T(8,128)S(1)}, f32[136,128]{1,0:T(8,128)S(1)}, u32[]{:S(2)}, u32[]{:S(2)}) collective-permute-start(f32[136,128]{1,0:T(8,128)S(1)} %get-tuple-element.21.packed_ref), channel_id=1, source_target_pairs={{0,3},{1,2},{2,1},{3,0},{4,7},{5,6},{6,5},{7,4},{8,11},{9,10},{10,... | collective-permute-start | bytes 208904 | tf_op jit(solution)/shard_map/ppermute | solution.py:312
  5.1 10.0 %collective-permute-start.4 = (f32[136,128]{1,0:T(8,128)S(1)}, f32[136,128]{1,0:T(8,128)S(1)}, u32[]{:S(2)}, u32[]{:S(2)}) collective-permute-start(f32[136,128]{1,0:T(8,128)S(1)} %get-tuple-element.21.packed_ref), channel_id=1, source_target_pairs={{0,2},{1,3},{2,0},{3,1},{4,6},{5,7},{6,4},{7,5},{8,10},{9,11},{10,... | collective-permute-start | bytes 208904 | tf_op jit(solution)/shard_map/ppermute | solution.py:311
  6.7 8.3 %collective-permute-start.6 = (s32[2,256]{1,0:T(2,128)S(1)}, s32[2,256]{1,0:T(2,128)S(1)}, u32[]{:S(2)}, u32[]{:S(2)}) collective-permute-start(s32[2,256]{1,0:T(2,128)S(1)} %get-tuple-element.28), channel_id=1, source_target_pairs={{0,4},{2,6},{4,0},{5,9},{6,2},{7,11},{8,12},{9,5},{10,14},{11,7},{... | collective-permute-start | bytes 6152 | tf_op jit(solution)/shard_map/ppermute | solution.py:293
  11.1 11.6 %all-to-all-start = ((f32[32,8,128]{2,1,0:T(8,128)}), f32[32,8,128]{2,1,0:T(8,128)S(1)}, u32[]{:S(2)}, u32[]{:S(2)}) async-start(f32[32,8,128]{2,1,0:T(8,128)} %bitcast.4), calls=%async_computation | async-start | bytes 262144 | tf_op jit(solution)/shard_map/all_to_all | solution.py:327
  15.4 6.4 %collective-permute-start.7 = (f32[32,256]{1,0:T(8,128)S(1)}, f32[32,256]{1,0:T(8,128)S(1)}, u32[]{:S(2)}, u32[]{:S(2)}) collective-permute-start(f32[32,256]{1,0:T(8,128)S(1)} %get-tuple-element.31), channel_id=1, source_target_pairs={{0,4},{2,6},{4,0},{5,9},{6,2},{7,11},{8,12},{9,5},{10,14},{11,7},{... | collective-permute-start | bytes 98312 | tf_op jit(solution)/shard_map/ppermute | solution.py:342
  22.0 1.2 %collective-permute-start.8 = (f32[32,256]{1,0:T(8,128)S(1)}, f32[32,256]{1,0:T(8,128)S(1)}, u32[]{:S(2)}, u32[]{:S(2)}) collective-permute-start(f32[32,256]{1,0:T(8,128)S(1)} %get-tuple-element.35), channel_id=1, source_target_pairs={{0,1},{1,0},{2,3},{3,2},{4,5},{5,4},{6,7},{7,6},{8,9},{9,8},{10,11... | collective-permute-start | bytes 98312 | tf_op jit(solution)/shard_map/ppermute | solution.py:376
  22.6 1.3 %collective-permute-start.3 = (f32[4,8,128]{2,1,0:T(8,128)S(1)}, f32[4,8,128]{2,1,0:T(8,128)S(1)}, u32[]{:S(2)}, u32[]{:S(2)}) collective-permute-start(f32[4,8,128]{2,1,0:T(8,128)S(1)} %reduce.1.mine_ref), channel_id=1, source_target_pairs={{0,1},{1,0},{2,3},{3,2},{4,5},{5,4},{6,7},{7,6},{8,9},{9,8},{10,11... | collective-permute-start | bytes 49160 | tf_op jit(solution)/shard_map/ppermute | solution.py:396

commit v12 on v10

--- a/solution.py
+++ b/solution.py
@@ -107,10 +107,9 @@
 
 def coarse_kernel(
     width, rows, tiles, sub_order, blk_order,
-    packed_ref, core_ref, rhs_ref, far_ref, hi_ref, low_ref, send_ref, parts_ref,
+    rhs_ref, far_ref, hi_ref, low_ref, send_ref, order_ref,
 ):
-    parts_ref[0] = split3(block_rows(packed_ref, rows, 0, tiles))
-    parts_ref[1] = split3(core_ref[...])
+    order_ref[...] = jnp.zeros(order_ref.shape, F32)
     rhs = rhs_ref[...] + far_ref[...]
     half = rows // 2
     lane = lax.broadcasted_iota(jnp.int32, (half, LANES), 1)
@@ -132,10 +131,14 @@
                     send_ref[sub_order.index(to + 1), at] = right[piece]
 
 
-def margin_kernel(tiles, near_ref, y_ref, both_ref, lists_ref, out_ref, far_ref):
+def margin_kernel(
+    tiles, packed_ref, core_ref, y_ref, both_ref, lists_ref, order_ref, out_ref, near_ref, far_ref
+):
     half, rows, cols = near_ref.shape
     wanted = jnp.where(facing() == 1, lists_ref[1:2], lists_ref[0:1])
     local = lax.broadcasted_iota(jnp.int32, (cols, wanted.shape[1]), 0)
+    near_ref[0] = split3(block_rows(packed_ref, rows // 3, 0, tiles))
+    near_ref[1] = split3(core_ref[...])
     for k, ref in enumerate((y_ref, both_ref)):
         far_ref[k] = split3(block_rows(ref, rows // 3, 0, tiles))
     total = jnp.zeros((rows, wanted.shape[1]), F32)
@@ -212,7 +215,7 @@
         out_ref[b] = total[k]
 
 
-def tail_kernel(width, mine_ref, other_ref, hot_ref, total_ref, out_ref):
+def tail_kernel(width, mine_ref, other_ref, hot_ref, total_ref, out_ref, out_buf, sems):
     odd = (lax.axis_index("blk") & 1) == 1
     chunks = []
     for k in range(mine_ref.shape[0]):
@@ -225,7 +228,17 @@
         top.append(jnp.where(lane < width, left, pltpu.roll(right, width, 1)))
         bottom.append(jnp.where(lane < width, pltpu.roll(left, width, 1), right))
     coarse = jnp.concatenate([jnp.concatenate(top, axis=1), jnp.concatenate(bottom, axis=1)], axis=0)
-    out_ref[...] = total_ref[...] + fold3(dot(split3(coarse), hot_ref[...]))
+    parts = split3(coarse)
+    step = out_buf.shape[1] // 2
+    sends = []
+    for k in range(2):
+        at = slice(k * step, (k + 1) * step)
+        out_buf[:, at] = total_ref[:, at] + fold3(dot(parts, hot_ref[:, at]))
+        there = pl.ds(k * step, step)
+        sends.append(pltpu.make_async_copy(out_buf.at[:, there], out_ref.at[:, there], sems.at[k]))
+        sends[k].start()
+    for send in sends:
+        send.wait()
 
 
 def whole(space=pltpu.VMEM):
@@ -310,35 +323,36 @@
     far_rhs = lax.ppermute(rhs, "blk", far_swap)
     over_y = lax.ppermute(packed, "blk", far_swap)
     over_both = lax.ppermute(packed, "blk", both_swap)
-    send, near = pl.pallas_call(
+    send, order = pl.pallas_call(
         functools.partial(coarse_kernel, width, rows, tiles, sub_order, blk_order),
         out_shape=(
             jax.ShapeDtypeStruct((subs, shards, rows // 4, LANES), F32),
-            jax.ShapeDtypeStruct((2, 3 * rows, cols), BF16),
-        ),
-        in_specs=[whole()] * 6,
+            jax.ShapeDtypeStruct((8, LANES), F32),
+        ),
+        in_specs=[whole()] * 4,
         out_specs=(whole(), whole()),
         compiler_params=limit(12),
         cost_estimate=weight(8 * 10**9),
         name="coarse",
-    )(packed, over_core, rhs, far_rhs, m_hi, m_low)
+    )(rhs, far_rhs, m_hi, m_low)
     flat = send.reshape((subs * shards,) + send.shape[2:])
     members = [sub * shards + b for sub in sub_order for b in blk_order]
     got = lax.all_to_all(flat, ("sub", "blk"), 0, 0, axis_index_groups=[members], tiled=True)
     got = got.reshape((subs, shards) + flat.shape[1:])
 
-    outgoing, far = pl.pallas_call(
+    outgoing, near, far = pl.pallas_call(
         functools.partial(margin_kernel, tiles),
         out_shape=(
             jax.ShapeDtypeStruct((rows, margin), F32),
+            jax.ShapeDtypeStruct((2, 3 * rows, cols), BF16),
             jax.ShapeDtypeStruct((shards - 2, 3 * rows, cols), BF16),
         ),
-        in_specs=[whole()] * 4,
-        out_specs=(whole(), whole()),
+        in_specs=[whole()] * 6,
+        out_specs=(whole(),) * 3,
         compiler_params=limit(8),
         cost_estimate=weight(4 * 10**9),
         name="margins",
-    )(near, over_y, over_both, lists)
+    )(packed, over_core, over_y, over_both, lists, order)
     halo = lax.ppermute(outgoing, ("sub", "blk"), neighbours)
 
     owned, w_hi, w_low, hot = pl.pallas_call(
@@ -399,7 +413,8 @@
         functools.partial(tail_kernel, width),
         out_shape=jax.ShapeDtypeStruct((rows, cols), F32),
         in_specs=[whole()] * 4,
-        out_specs=whole(),
+        out_specs=whole(pl.ANY),
+        scratch_shapes=[pltpu.VMEM((rows, cols), F32), pltpu.SemaphoreType.DMA((2,))],
         compiler_params=limit(12),
         name="tail",
     )(sums, other_sums, hot, fine)

time: 25.1 us -> 25.1 us (level)
  no operation moved by 1% of the time
where the time goes in v12:
time: 25.1 us; the launch traced here: 24.8 us
  starting transfers between devices  16.5 us (66%)
  Pallas kernels  6.79 us (27%)
  waiting for transfers between devices  1.42 us (6%)
    all_to_all x1, starting transfers between devices, on_device(): lax.all_to_all(flat, ('sub', 'blk'), 0, 0, axis_index_groups=[members], t...  3.97 us
    ppermute x1, starting transfers between devices, on_device(): halo = lax.ppermute(outgoing, ('sub', 'blk'), neighbours)  3.7 us
    ppermute x1, starting transfers between devices, on_device(): lists = lax.ppermute(lists, ('sub', 'blk'), neighbours)  3.39 us
    ppermute x1, starting transfers between devices, on_device(): far_rhs = lax.ppermute(rhs, 'blk', far_swap)  2.83 us
    pallas_call x1, Pallas kernels, on_device(): pl.pallas_call(functools.partial(own_kernel, margin), out_shape=(jax.Shap...  2.67 us
    ppermute x1, starting transfers between devices, on_device(): over_y = lax.ppermute(packed, 'blk', far_swap)  1.61 us
    pallas_call x1, Pallas kernels, on_device(): pl.pallas_call(pack_kernel, out_shape=(jax.ShapeDtypeStruct(packed_shape,...  1.17 us
    pallas_call x1, Pallas kernels, on_device(): pl.pallas_call(functools.partial(coarse_kernel, width, rows, tiles, sub_o...  0.94 us
  transfers between devices with their start and end apart: 10, of which 4 were waited for; matrix products, arithmetic and copies ran while one was open for 0% of the time, Pallas kernels for 22%

profile of v12, /device:TPU:0, one launch (start us, length us, event | category | flops | bytes accessed | tf_op | source)
XLA Modules:
  0.0 24.8 jit_solution(5016299479771340129)
XLA Ops:
  0.0 0.5 %collective-permute-start.1 = (s32[512]{0:T(512)}, s32[512]{0:T(512)S(1)}, u32[]{:S(2)}, u32[]{:S(2)}) collective-permute-start(s32[512]{0:T(512)} %param.11), channel_id=1, source_target_pairs={{0,1},{1,0},{2,3},{3,2},{4,5},{5,4},{6,7},{7,6},{8,9},{9,8},{10,11... | collective-permute-start | bytes 6152 | tf_op jit(solution)/shard_map/ppermute | solution.py:308
  0.5 0.1 collective-permute-start
  0.5 1.2 %pack.1 = (f32[136,128]{1,0:T(8,128)S(1)}, s32[2,256]{1,0:T(2,128)S(1)}, f32[1024,128]{1,0:T(8,128)S(1)}) custom-call(f32[32,512]{1,0:T(8,128)} %residual_ref.1, s32[1,512]{1,0:T(1,128)} %bitcast.10, s32[2,256]{1,0:T(2,128)} %bitcast.9, s32[1,2]{1,0:T(1,128)} %counts_ref.1, f32[1024,128]{1,0:T(8,128)} %bitcast.8), custom_call_target="tpu_custom_call" | custom-call | flops 8000000000 | tf_op jit(solution)/shard_map/pack/pallas_call | solution.py:286
  1.7 0.0 collective-permute-done.1
  1.7 0.2 collective-permute-done.core_ref
  1.9 0.3 %near.1 = (f32[32,256]{1,0:T(8,128)S(1)}, bf16[256,512]{1,0:T(8,128)(2,1)S(1)}, bf16[256,512]{1,0:T(8,128)(2,1)S(1)}) custom-call(f32[136,128]{1,0:T(8,128)S(1)} %get-tuple-element.22.packed_ref, f32[32,512]{1,0:T(8,128)S(1)} %collective-permute-done.core_ref, s32[1,512]{1,0:T(1,128)S(1)} %bitcast.7, f32[1024,128]{1,0:T(8,128)S(1)} %get-tuple-element.23.coarse_ref), custom_call_target="tpu_custom_call" | custom-call | flops 2000000000 | tf_op jit(solution)/shard_map/near/pallas_call | solution.py:310
  2.3 2.8 %collective-permute-start.2 = (f32[32,256]{1,0:T(8,128)S(1)}, f32[32,256]{1,0:T(8,128)S(1)}, u32[]{:S(2)}, u32[]{:S(2)}) collective-permute-start(f32[32,256]{1,0:T(8,128)S(1)} %get-tuple-element.24.rhs_ref), channel_id=1, source_target_pairs={{0,2},{1,3},{2,0},{3,1},{4,6},{5,7},{6,4},{7,5},{8,10},{9,11},{10,... | collective-permute-start | bytes 98312 | tf_op jit(solution)/shard_map/ppermute | solution.py:323
  5.1 0.0 collective-permute-start.5
  5.1 1.6 %collective-permute-start.4 = (f32[136,128]{1,0:T(8,128)S(1)}, f32[136,128]{1,0:T(8,128)S(1)}, u32[]{:S(2)}, u32[]{:S(2)}) collective-permute-start(f32[136,128]{1,0:T(8,128)S(1)} %get-tuple-element.22.packed_ref), channel_id=1, source_target_pairs={{0,2},{1,3},{2,0},{3,1},{4,6},{5,7},{6,4},{7,5},{8,10},{9,11},{10,... | collective-permute-start | bytes 208904 | tf_op jit(solution)/shard_map/ppermute | solution.py:324
  6.7 3.4 %collective-permute-start.6 = (s32[2,256]{1,0:T(2,128)S(1)}, s32[2,256]{1,0:T(2,128)S(1)}, u32[]{:S(2)}, u32[]{:S(2)}) collective-permute-start(s32[2,256]{1,0:T(2,128)S(1)} %get-tuple-element.28), channel_id=1, source_target_pairs={{0,4},{2,6},{4,0},{5,9},{6,2},{7,11},{8,12},{9,5},{10,14},{11,7},{... | collective-permute-start | bytes 6152 | tf_op jit(solution)/shard_map/ppermute | solution.py:306
  10.1 0.0 collective-permute-done.2.far_ref
  10.1 0.9 %coarse.1 = (f32[8,4,8,128]{3,2,1,0:T(8,128)}, f32[8,128]{1,0:T(8,128)S(1)}) custom-call(f32[32,256]{1,0:T(8,128)S(1)} %get-tuple-element.24.rhs_ref, f32[32,256]{1,0:T(8,128)S(1)} %collective-permute-done.2.far_ref, bf16[256,512]{1,0:T(8,128)(2,1)S(1)} %get-tuple-element.25.hi_ref, bf16[256,512]{1,0:T(8,128)(2,1)S(1)} %get-tuple-element.26.low_ref), custom_call_target="tpu_custom_call" | custom-call | flops 8000000000 | tf_op jit(solution)/shard_map/coarse/pallas_call | solution.py:326
  11.1 4.0 %all-to-all-start = ((f32[32,8,128]{2,1,0:T(8,128)}), f32[32,8,128]{2,1,0:T(8,128)S(1)}, u32[]{:S(2)}, u32[]{:S(2)}) async-start(f32[32,8,128]{2,1,0:T(8,128)} %bitcast.4), calls=%async_computation | async-start | bytes 262144 | tf_op jit(solution)/shard_map/all_to_all | solution.py:340
  15.0 0.0 collective-permute-done.6.lists_ref
  15.0 0.0 collective-permute-done.5.both_ref
  15.1 0.0 collective-permute-done.4.y_ref
  15.1 0.4 %margins.1 = (f32[32,256]{1,0:T(8,128)S(1)}, bf16[2,96,512]{2,1,0:T(8,128)(2,1)S(1)}, bf16[2,96,512]{2,1,0:T(8,128)(2,1)S(1)}) custom-call(f32[136,128]{1,0:T(8,128)S(1)} %get-tuple-element.22.packed_ref, f32[32,512]{1,0:T(8,128)S(1)} %collective-permute-done.core_ref, f32[136,128]{1,0:T(8,128)S(1)} %collective-permute-done.4.y_ref, ...), custom_call_target="tpu_custom_call" | custom-call | flops 4000000000 | tf_op jit(solution)/shard_map/margins/pallas_call | solution.py:343
  15.5 3.7 %collective-permute-start.7 = (f32[32,256]{1,0:T(8,128)S(1)}, f32[32,256]{1,0:T(8,128)S(1)}, u32[]{:S(2)}, u32[]{:S(2)}) collective-permute-start(f32[32,256]{1,0:T(8,128)S(1)} %get-tuple-element.33), channel_id=1, source_target_pairs={{0,4},{2,6},{4,0},{5,9},{6,2},{7,11},{8,12},{9,5},{10,14},{11,7},{... | collective-permute-start | bytes 98312 | tf_op jit(solution)/shard_map/ppermute | solution.py:356
  19.2 2.7 %owned.1 = (f32[32,512]{1,0:T(8,128)S(1)}, bf16[2,256,512]{2,1,0:T(8,128)(2,1)S(1)}, bf16[2,256,512]{2,1,0:T(8,128)(2,1)S(1)}, bf16[256,512]{1,0:T(8,128)(2,1)S(1)}) custom-call(bf16[2,96,512]{2,1,0:T(8,128)(2,1)S(1)} %get-tuple-element.30.near_ref, bf16[2,96,512]{2,1,0:T(8,128)(2,1)S(1)} %get-tuple-element.31.far_ref, s32[1,512]{1,0:T(1,128)} %bitcast.11, ...), custom_call_target="tpu_custom_call" | custom-call | flops 40000000000 | tf_op jit(solution)/shard_map/owned/pallas_call | solution.py:358
  21.8 0.0 collective-permute-done.7.halo_ref
  21.9 0.2 mine.1
  22.1 0.0 collective-permute-start.8
  22.1 0.5 %all-to-all-done = f32[32,8,128]{2,1,0:T(8,128)S(1)} async-done(((f32[32,8,128]{2,1,0:T(8,128)}), f32[32,8,128]{2,1,0:T(8,128)S(1)}, u32[]{:S(2)}, u32[]{:S(2)}) %all-to-all-start) | async-done | bytes 131104 | tf_op jit(solution)/shard_map/all_to_all | solution.py:340
  22.6 0.5 %collective-permute-start.3 = (f32[4,8,128]{2,1,0:T(8,128)S(1)}, f32[4,8,128]{2,1,0:T(8,128)S(1)}, u32[]{:S(2)}, u32[]{:S(2)}) collective-permute-start(f32[4,8,128]{2,1,0:T(8,128)S(1)} %reduce.1.mine_ref), channel_id=1, source_target_pairs={{0,1},{1,0},{2,3},{3,2},{4,5},{5,4},{6,7},{7,6},{8,9},{9,8},{10,11... | collective-permute-start | bytes 49160 | tf_op jit(solution)/shard_map/ppermute | solution.py:410
  23.1 0.2 collective-permute-done.8.halo_ref
  23.3 0.2 other.1.total_ref
  23.5 0.5 %collective-permute-done.3.other_ref = f32[4,8,128]{2,1,0:T(8,128)S(1)} collective-permute-done((f32[4,8,128]{2,1,0:T(8,128)S(1)}, f32[4,8,128]{2,1,0:T(8,128)S(1)}, u32[]{:S(2)}, u32[]{:S(2)}) %collective-permute-start.3) | collective-permute-done | bytes 16416 | tf_op jit(solution)/shard_map/ppermute | solution.py:410
  23.9 0.9 %tail.1 = f32[32,512]{1,0:T(8,128)} custom-call(f32[4,8,128]{2,1,0:T(8,128)S(1)} %reduce.1.mine_ref, f32[4,8,128]{2,1,0:T(8,128)S(1)} %collective-permute-done.3.other_ref, bf16[256,512]{1,0:T(8,128)(2,1)S(1)} %get-tuple-element.32.hot_ref, f32[32,512]{1,0:T(8,128)S(1)} %other.1.total_ref), custom_call_target="tpu_custom_call" | custom-call | tf_op jit(solution)/shard_map/tail/pallas_call | solution.py:412
  (1 shorter events, 0.0 us)
Async XLA Ops:
  0.0 1.7 %collective-permute-start.1 = (s32[512]{0:T(512)}, s32[512]{0:T(512)S(1)}, u32[]{:S(2)}, u32[]{:S(2)}) collective-permute-start(s32[512]{0:T(512)} %param.11), channel_id=1, source_target_pairs={{0,1},{1,0},{2,3},{3,2},{4,5},{5,4},{6,7},{7,6},{8,9},{9,8},{10,11... | collective-permute-start | bytes 6152 | tf_op jit(solution)/shard_map/ppermute | solution.py:308
  0.5 1.5 %collective-permute-start = (f32[32,512]{1,0:T(8,128)}, f32[32,512]{1,0:T(8,128)S(1)}, u32[]{:S(2)}, u32[]{:S(2)}) collective-permute-start(f32[32,512]{1,0:T(8,128)} %residual_ref.1), channel_id=1, source_target_pairs={{0,1},{1,0},{2,3},{3,2},{4,5},{5,4},{6,7},{7,6},{8,9},{9,8},{10,11... | collective-permute-start | bytes 196616 | tf_op jit(solution)/shard_map/ppermute | solution.py:307
  2.3 7.8 %collective-permute-start.2 = (f32[32,256]{1,0:T(8,128)S(1)}, f32[32,256]{1,0:T(8,128)S(1)}, u32[]{:S(2)}, u32[]{:S(2)}) collective-permute-start(f32[32,256]{1,0:T(8,128)S(1)} %get-tuple-element.24.rhs_ref), channel_id=1, source_target_pairs={{0,2},{1,3},{2,0},{3,1},{4,6},{5,7},{6,4},{7,5},{8,10},{9,11},{10,... | collective-permute-start | bytes 98312 | tf_op jit(solution)/shard_map/ppermute | solution.py:323
  5.1 9.9 %collective-permute-start.5 = (f32[136,128]{1,0:T(8,128)S(1)}, f32[136,128]{1,0:T(8,128)S(1)}, u32[]{:S(2)}, u32[]{:S(2)}) collective-permute-start(f32[136,128]{1,0:T(8,128)S(1)} %get-tuple-element.22.packed_ref), channel_id=1, source_target_pairs={{0,3},{1,2},{2,1},{3,0},{4,7},{5,6},{6,5},{7,4},{8,11},{9,10},{10,... | collective-permute-start | bytes 208904 | tf_op jit(solution)/shard_map/ppermute | solution.py:325
  5.1 10.0 %collective-permute-start.4 = (f32[136,128]{1,0:T(8,128)S(1)}, f32[136,128]{1,0:T(8,128)S(1)}, u32[]{:S(2)}, u32[]{:S(2)}) collective-permute-start(f32[136,128]{1,0:T(8,128)S(1)} %get-tuple-element.22.packed_ref), channel_id=1, source_target_pairs={{0,2},{1,3},{2,0},{3,1},{4,6},{5,7},{6,4},{7,5},{8,10},{9,11},{10,... | collective-permute-start | bytes 208904 | tf_op jit(solution)/shard_map/ppermute | solution.py:324
  6.7 8.3 %collective-permute-start.6 = (s32[2,256]{1,0:T(2,128)S(1)}, s32[2,256]{1,0:T(2,128)S(1)}, u32[]{:S(2)}, u32[]{:S(2)}) collective-permute-start(s32[2,256]{1,0:T(2,128)S(1)} %get-tuple-element.28), channel_id=1, source_target_pairs={{0,4},{2,6},{4,0},{5,9},{6,2},{7,11},{8,12},{9,5},{10,14},{11,7},{... | collective-permute-start | bytes 6152 | tf_op jit(solution)/shard_map/ppermute | solution.py:306
  11.1 11.6 %all-to-all-start = ((f32[32,8,128]{2,1,0:T(8,128)}), f32[32,8,128]{2,1,0:T(8,128)S(1)}, u32[]{:S(2)}, u32[]{:S(2)}) async-start(f32[32,8,128]{2,1,0:T(8,128)} %bitcast.4), calls=%async_computation | async-start | bytes 262144 | tf_op jit(solution)/shard_map/all_to_all | solution.py:340
  15.5 6.4 %collective-permute-start.7 = (f32[32,256]{1,0:T(8,128)S(1)}, f32[32,256]{1,0:T(8,128)S(1)}, u32[]{:S(2)}, u32[]{:S(2)}) collective-permute-start(f32[32,256]{1,0:T(8,128)S(1)} %get-tuple-element.33), channel_id=1, source_target_pairs={{0,4},{2,6},{4,0},{5,9},{6,2},{7,11},{8,12},{9,5},{10,14},{11,7},{... | collective-permute-start | bytes 98312 | tf_op jit(solution)/shard_map/ppermute | solution.py:356
  22.1 1.2 %collective-permute-start.8 = (f32[32,256]{1,0:T(8,128)S(1)}, f32[32,256]{1,0:T(8,128)S(1)}, u32[]{:S(2)}, u32[]{:S(2)}) collective-permute-start(f32[32,256]{1,0:T(8,128)S(1)} %get-tuple-element.37), channel_id=1, source_target_pairs={{0,1},{1,0},{2,3},{3,2},{4,5},{5,4},{6,7},{7,6},{8,9},{9,8},{10,11... | collective-permute-start | bytes 98312 | tf_op jit(solution)/shard_map/ppermute | solution.py:390
  22.6 1.3 %collective-permute-start.3 = (f32[4,8,128]{2,1,0:T(8,128)S(1)}, f32[4,8,128]{2,1,0:T(8,128)S(1)}, u32[]{:S(2)}, u32[]{:S(2)}) collective-permute-start(f32[4,8,128]{2,1,0:T(8,128)S(1)} %reduce.1.mine_ref), channel_id=1, source_target_pairs={{0,1},{1,0},{2,3},{3,2},{4,5},{5,4},{6,7},{7,6},{8,9},{9,8},{10,11... | collective-permute-start | bytes 49160 | tf_op jit(solution)/shard_map/ppermute | solution.py:410

commit v13 on v10

--- a/solution.py
+++ b/solution.py
@@ -62,12 +62,12 @@
 
 
 def pack_kernel(
-    residual_ref, agg_ref, lists_ref, counts_ref, coarse_ref,
-    out_ref, lists_out, coarse_out,
+    residual_ref, agg_ref, lists_ref, counts_ref,
+    out_ref, lists_out,
     residual_buf, agg_buf, lists_buf, counts_buf, sems,
 ):
-    sources = (residual_ref, agg_ref, lists_ref, counts_ref, coarse_ref)
-    targets = (residual_buf, agg_buf, lists_buf, counts_buf, coarse_out)
+    sources = (residual_ref, agg_ref, lists_ref, counts_ref)
+    targets = (residual_buf, agg_buf, lists_buf, counts_buf)
     fetches = [pltpu.make_async_copy(a, b, sems.at[k]) for k, (a, b) in enumerate(zip(sources, targets))]
     for fetch in fetches:
         fetch.start()
@@ -86,7 +86,6 @@
     for side in range(2):
         used = slots < counts_buf[:, side : side + 1]
         lists_out[side : side + 1] = jnp.where(used, lists_buf[side : side + 1], -1)
-    fetches[4].wait()
 
 
 def near_kernel(
@@ -270,26 +269,25 @@
     table = coarse_inverse.reshape(-1, LANES)
     packed_shape = (packed_rows, LANES)
 
-    packed, lists, table = pl.pallas_call(
+    packed, lists = pl.pallas_call(
         pack_kernel,
         out_shape=(
             jax.ShapeDtypeStruct(packed_shape, F32),
             jax.ShapeDtypeStruct(lists.shape, jnp.int32),
-            jax.ShapeDtypeStruct(table.shape, F32),
-        ),
-        in_specs=[whole(pl.ANY)] * 5,
-        out_specs=(whole(),) * 3,
+        ),
+        in_specs=[whole(pl.ANY)] * 4,
+        out_specs=(whole(), whole()),
         scratch_shapes=[
             pltpu.VMEM(residual.shape, F32),
             pltpu.VMEM(codes.shape, jnp.int32),
             pltpu.VMEM(lists.shape, jnp.int32),
             pltpu.VMEM(wanted_count.shape, jnp.int32),
-            pltpu.SemaphoreType.DMA((5,)),
+            pltpu.SemaphoreType.DMA((4,)),
         ],
         compiler_params=limit(4),
         cost_estimate=weight(8 * 10**9),
         name="pack",
-    )(in_hbm(residual), in_hbm(codes), in_hbm(lists), in_hbm(wanted_count), in_hbm(table))
+    )(in_hbm(residual), in_hbm(codes), in_hbm(lists), in_hbm(wanted_count))
     lists = lax.ppermute(lists, ("sub", "blk"), neighbours)
     over_core = lax.ppermute(residual, "blk", core_swap)
     core_codes = lax.ppermute(aggregate, "blk", core_swap)[None]

time: 25.1 us -> 25.1 us (level)
  no operation moved by 1% of the time
where the time goes in v13:
time: 25.1 us; the launch traced here: 24.8 us
  starting transfers between devices  16.5 us (66%)
  Pallas kernels  6.56 us (26%)
  waiting for transfers between devices  1.65 us (7%)
    all_to_all x1, starting transfers between devices, on_device(): lax.all_to_all(flat, ('sub', 'blk'), 0, 0, axis_index_groups=[members], t...  3.97 us
    ppermute x1, starting transfers between devices, on_device(): halo = lax.ppermute(outgoing, ('sub', 'blk'), neighbours)  3.69 us
    ppermute x1, starting transfers between devices, on_device(): lists = lax.ppermute(lists, ('sub', 'blk'), neighbours)  3.39 us
    ppermute x1, starting transfers between devices, on_device(): far_rhs = lax.ppermute(rhs, 'blk', far_swap)  2.74 us
    pallas_call x1, Pallas kernels, on_device(): pl.pallas_call(functools.partial(own_kernel, margin), out_shape=(jax.Shap...  2.67 us
    ppermute x1, starting transfers between devices, on_device(): over_y = lax.ppermute(packed, 'blk', far_swap)  1.65 us
    pallas_call x1, Pallas kernels, on_device(): pl.pallas_call(pack_kernel, out_shape=(jax.ShapeDtypeStruct(packed_shape,...  1.02 us
    pallas_call x1, Pallas kernels, on_device(): pl.pallas_call(functools.partial(coarse_kernel, width, rows, tiles, sub_o...  0.94 us
  transfers between devices with their start and end apart: 10, of which 4 were waited for; matrix products, arithmetic and copies ran while one was open for 0% of the time, Pallas kernels for 22%

profile of v13, /device:TPU:0, one launch (start us, length us, event | category | flops | bytes accessed | tf_op | source)
XLA Modules:
  0.0 24.8 jit_solution(8343703771078493721)
XLA Ops:
  0.0 0.5 %collective-permute-start.1 = (s32[512]{0:T(512)}, s32[512]{0:T(512)S(1)}, u32[]{:S(2)}, u32[]{:S(2)}) collective-permute-start(s32[512]{0:T(512)} %param.11), channel_id=1, source_target_pairs={{0,1},{1,0},{2,3},{3,2},{4,5},{5,4},{6,7},{7,6},{8,9},{9,8},{10,11... | collective-permute-start | bytes 6152 | tf_op jit(solution)/shard_map/ppermute | solution.py:293
  0.5 0.1 collective-permute-start
  0.5 0.0 copy-start
  0.5 1.0 %pack.1 = (f32[136,128]{1,0:T(8,128)S(1)}, s32[2,256]{1,0:T(2,128)S(1)}) custom-call(f32[32,512]{1,0:T(8,128)} %residual_ref.1, s32[1,512]{1,0:T(1,128)} %bitcast.10, s32[2,256]{1,0:T(2,128)} %bitcast.9, s32[1,2]{1,0:T(1,128)} %counts_ref.1), custom_call_target="tpu_custom_call" | custom-call | flops 8000000000 | tf_op jit(solution)/shard_map/pack/pallas_call | solution.py:272
  1.5 0.0 collective-permute-done.1
  1.6 0.4 %collective-permute-done.core_ref = f32[32,512]{1,0:T(8,128)S(1)} collective-permute-done((f32[32,512]{1,0:T(8,128)}, f32[32,512]{1,0:T(8,128)S(1)}, u32[]{:S(2)}, u32[]{:S(2)}) %collective-permute-start) | collective-permute-done | bytes 65568 | tf_op jit(solution)/shard_map/ppermute | solution.py:292
  1.9 0.0 copy-done
  1.9 0.3 %near.1 = (f32[32,256]{1,0:T(8,128)S(1)}, bf16[256,512]{1,0:T(8,128)(2,1)S(1)}, bf16[256,512]{1,0:T(8,128)(2,1)S(1)}) custom-call(f32[136,128]{1,0:T(8,128)S(1)} %get-tuple-element.20.packed_ref, f32[32,512]{1,0:T(8,128)S(1)} %collective-permute-done.core_ref, s32[1,512]{1,0:T(1,128)S(1)} %bitcast.8, f32[1024,128]{1,0:T(8,128)S(1)} %bitcast.7), custom_call_target="tpu_custom_call" | custom-call | flops 2000000000 | tf_op jit(solution)/shard_map/near/pallas_call | solution.py:295
  2.3 2.7 %collective-permute-start.2 = (f32[32,256]{1,0:T(8,128)S(1)}, f32[32,256]{1,0:T(8,128)S(1)}, u32[]{:S(2)}, u32[]{:S(2)}) collective-permute-start(f32[32,256]{1,0:T(8,128)S(1)} %get-tuple-element.21.rhs_ref), channel_id=1, source_target_pairs={{0,2},{1,3},{2,0},{3,1},{4,6},{5,7},{6,4},{7,5},{8,10},{9,11},{10,... | collective-permute-start | bytes 98312 | tf_op jit(solution)/shard_map/ppermute | solution.py:308
  5.0 0.0 collective-permute-start.5
  5.1 1.7 %collective-permute-start.4 = (f32[136,128]{1,0:T(8,128)S(1)}, f32[136,128]{1,0:T(8,128)S(1)}, u32[]{:S(2)}, u32[]{:S(2)}) collective-permute-start(f32[136,128]{1,0:T(8,128)S(1)} %get-tuple-element.20.packed_ref), channel_id=1, source_target_pairs={{0,2},{1,3},{2,0},{3,1},{4,6},{5,7},{6,4},{7,5},{8,10},{9,11},{10,... | collective-permute-start | bytes 208904 | tf_op jit(solution)/shard_map/ppermute | solution.py:309
  6.7 3.4 %collective-permute-start.6 = (s32[2,256]{1,0:T(2,128)S(1)}, s32[2,256]{1,0:T(2,128)S(1)}, u32[]{:S(2)}, u32[]{:S(2)}) collective-permute-start(s32[2,256]{1,0:T(2,128)S(1)} %get-tuple-element.26), channel_id=1, source_target_pairs={{0,4},{2,6},{4,0},{5,9},{6,2},{7,11},{8,12},{9,5},{10,14},{11,7},{... | collective-permute-start | bytes 6152 | tf_op jit(solution)/shard_map/ppermute | solution.py:291
  10.1 0.0 collective-permute-done.2.far_ref
  10.1 0.9 %coarse.1 = (f32[8,4,8,128]{3,2,1,0:T(8,128)}, bf16[2,96,512]{2,1,0:T(8,128)(2,1)S(1)}) custom-call(f32[136,128]{1,0:T(8,128)S(1)} %get-tuple-element.20.packed_ref, f32[32,512]{1,0:T(8,128)S(1)} %collective-permute-done.core_ref, f32[32,256]{1,0:T(8,128)S(1)} %get-tuple-element.21.rhs_ref, f32[32,256]{1,0:T(8,128)S(1)} %collective-permute-done.2.far_ref, ...), custom_call_target="tpu_custom_call" | custom-call | flops 8000000000 | tf_op jit(solution)/shard_map/coarse/pallas_call | solution.py:311
  11.1 4.0 %all-to-all-start = ((f32[32,8,128]{2,1,0:T(8,128)}), f32[32,8,128]{2,1,0:T(8,128)S(1)}, u32[]{:S(2)}, u32[]{:S(2)}) async-start(f32[32,8,128]{2,1,0:T(8,128)} %bitcast.4), calls=%async_computation | async-start | bytes 262144 | tf_op jit(solution)/shard_map/all_to_all | solution.py:325
  15.0 0.0 collective-permute-done.6.lists_ref
  15.1 0.0 collective-permute-done.5.both_ref
  15.1 0.0 collective-permute-done.4.y_ref
  15.1 0.3 %margins.1 = (f32[32,256]{1,0:T(8,128)S(1)}, bf16[2,96,512]{2,1,0:T(8,128)(2,1)S(1)}) custom-call(bf16[2,96,512]{2,1,0:T(8,128)(2,1)S(1)} %get-tuple-element.25.near_ref, f32[136,128]{1,0:T(8,128)S(1)} %collective-permute-done.4.y_ref, f32[136,128]{1,0:T(8,128)S(1)} %collective-permute-done.5.both_ref, s32[2,256]{1,0:T(2,128)S(1)} %collective-permute-done.6.lists_ref), custom_call_target="tpu_custom_call" | custom-call | flops 4000000000 | tf_op jit(solution)/shard_map/margins/pallas_call | solution.py:328
  15.4 3.7 %collective-permute-start.7 = (f32[32,256]{1,0:T(8,128)S(1)}, f32[32,256]{1,0:T(8,128)S(1)}, u32[]{:S(2)}, u32[]{:S(2)}) collective-permute-start(f32[32,256]{1,0:T(8,128)S(1)} %get-tuple-element.29), channel_id=1, source_target_pairs={{0,4},{2,6},{4,0},{5,9},{6,2},{7,11},{8,12},{9,5},{10,14},{11,7},{... | collective-permute-start | bytes 98312 | tf_op jit(solution)/shard_map/ppermute | solution.py:340
  19.1 2.7 %owned.1 = (f32[32,512]{1,0:T(8,128)S(1)}, bf16[2,256,512]{2,1,0:T(8,128)(2,1)S(1)}, bf16[2,256,512]{2,1,0:T(8,128)(2,1)S(1)}, bf16[256,512]{1,0:T(8,128)(2,1)S(1)}) custom-call(bf16[2,96,512]{2,1,0:T(8,128)(2,1)S(1)} %get-tuple-element.25.near_ref, bf16[2,96,512]{2,1,0:T(8,128)(2,1)S(1)} %get-tuple-element.27.far_ref, s32[1,512]{1,0:T(1,128)} %bitcast.11, ...), custom_call_target="tpu_custom_call" | custom-call | flops 40000000000 | tf_op jit(solution)/shard_map/owned/pallas_call | solution.py:342
  21.8 0.0 collective-permute-done.7.halo_ref
  21.8 0.2 mine.1
  22.0 0.0 collective-permute-start.8
  22.0 0.6 %all-to-all-done = f32[32,8,128]{2,1,0:T(8,128)S(1)} async-done(((f32[32,8,128]{2,1,0:T(8,128)}), f32[32,8,128]{2,1,0:T(8,128)S(1)}, u32[]{:S(2)}, u32[]{:S(2)}) %all-to-all-start) | async-done | bytes 131104 | tf_op jit(solution)/shard_map/all_to_all | solution.py:325
  22.6 0.5 %collective-permute-start.3 = (f32[4,8,128]{2,1,0:T(8,128)S(1)}, f32[4,8,128]{2,1,0:T(8,128)S(1)}, u32[]{:S(2)}, u32[]{:S(2)}) collective-permute-start(f32[4,8,128]{2,1,0:T(8,128)S(1)} %reduce.1.mine_ref), channel_id=1, source_target_pairs={{0,1},{1,0},{2,3},{3,2},{4,5},{5,4},{6,7},{7,6},{8,9},{9,8},{10,11... | collective-permute-start | bytes 49160 | tf_op jit(solution)/shard_map/ppermute | solution.py:394
  23.1 0.1 collective-permute-done.8.halo_ref
  23.2 0.2 other.1.total_ref
  23.4 0.6 %collective-permute-done.3.other_ref = f32[4,8,128]{2,1,0:T(8,128)S(1)} collective-permute-done((f32[4,8,128]{2,1,0:T(8,128)S(1)}, f32[4,8,128]{2,1,0:T(8,128)S(1)}, u32[]{:S(2)}, u32[]{:S(2)}) %collective-permute-start.3) | collective-permute-done | bytes 16416 | tf_op jit(solution)/shard_map/ppermute | solution.py:394
  24.0 0.9 %tail.1 = f32[32,512]{1,0:T(8,128)} custom-call(f32[4,8,128]{2,1,0:T(8,128)S(1)} %reduce.1.mine_ref, f32[4,8,128]{2,1,0:T(8,128)S(1)} %collective-permute-done.3.other_ref, bf16[256,512]{1,0:T(8,128)(2,1)S(1)} %get-tuple-element.28.hot_ref, f32[32,512]{1,0:T(8,128)S(1)} %other.1.total_ref), custom_call_target="tpu_custom_call" | custom-call | tf_op jit(solution)/shard_map/tail/pallas_call | solution.py:396
  (1 shorter events, 0.0 us)
Async XLA Ops:
  0.0 1.5 %collective-permute-start.1 = (s32[512]{0:T(512)}, s32[512]{0:T(512)S(1)}, u32[]{:S(2)}, u32[]{:S(2)}) collective-permute-start(s32[512]{0:T(512)} %param.11), channel_id=1, source_target_pairs={{0,1},{1,0},{2,3},{3,2},{4,5},{5,4},{6,7},{7,6},{8,9},{9,8},{10,11... | collective-permute-start | bytes 6152 | tf_op jit(solution)/shard_map/ppermute | solution.py:293
  0.5 1.5 %collective-permute-start = (f32[32,512]{1,0:T(8,128)}, f32[32,512]{1,0:T(8,128)S(1)}, u32[]{:S(2)}, u32[]{:S(2)}) collective-permute-start(f32[32,512]{1,0:T(8,128)} %residual_ref.1), channel_id=1, source_target_pairs={{0,1},{1,0},{2,3},{3,2},{4,5},{5,4},{6,7},{7,6},{8,9},{9,8},{10,11... | collective-permute-start | bytes 196616 | tf_op jit(solution)/shard_map/ppermute | solution.py:292
  0.5 1.4 %copy-start = (f32[256,1,512]{2,1,0:T(1,128)S(1)}, f32[256,1,512]{2,1,0:T(1,128)}, u32[]{:S(2)}) copy-start(f32[256,1,512]{2,1,0:T(1,128)} %param.8) | copy-start | bytes 1572868
  2.3 7.8 %collective-permute-start.2 = (f32[32,256]{1,0:T(8,128)S(1)}, f32[32,256]{1,0:T(8,128)S(1)}, u32[]{:S(2)}, u32[]{:S(2)}) collective-permute-start(f32[32,256]{1,0:T(8,128)S(1)} %get-tuple-element.21.rhs_ref), channel_id=1, source_target_pairs={{0,2},{1,3},{2,0},{3,1},{4,6},{5,7},{6,4},{7,5},{8,10},{9,11},{10,... | collective-permute-start | bytes 98312 | tf_op jit(solution)/shard_map/ppermute | solution.py:308
  5.0 10.0 %collective-permute-start.5 = (f32[136,128]{1,0:T(8,128)S(1)}, f32[136,128]{1,0:T(8,128)S(1)}, u32[]{:S(2)}, u32[]{:S(2)}) collective-permute-start(f32[136,128]{1,0:T(8,128)S(1)} %get-tuple-element.20.packed_ref), channel_id=1, source_target_pairs={{0,3},{1,2},{2,1},{3,0},{4,7},{5,6},{6,5},{7,4},{8,11},{9,10},{10,... | collective-permute-start | bytes 208904 | tf_op jit(solution)/shard_map/ppermute | solution.py:310
  5.1 10.0 %collective-permute-start.4 = (f32[136,128]{1,0:T(8,128)S(1)}, f32[136,128]{1,0:T(8,128)S(1)}, u32[]{:S(2)}, u32[]{:S(2)}) collective-permute-start(f32[136,128]{1,0:T(8,128)S(1)} %get-tuple-element.20.packed_ref), channel_id=1, source_target_pairs={{0,2},{1,3},{2,0},{3,1},{4,6},{5,7},{6,4},{7,5},{8,10},{9,11},{10,... | collective-permute-start | bytes 208904 | tf_op jit(solution)/shard_map/ppermute | solution.py:309
  6.7 8.3 %collective-permute-start.6 = (s32[2,256]{1,0:T(2,128)S(1)}, s32[2,256]{1,0:T(2,128)S(1)}, u32[]{:S(2)}, u32[]{:S(2)}) collective-permute-start(s32[2,256]{1,0:T(2,128)S(1)} %get-tuple-element.26), channel_id=1, source_target_pairs={{0,4},{2,6},{4,0},{5,9},{6,2},{7,11},{8,12},{9,5},{10,14},{11,7},{... | collective-permute-start | bytes 6152 | tf_op jit(solution)/shard_map/ppermute | solution.py:291
  11.1 11.6 %all-to-all-start = ((f32[32,8,128]{2,1,0:T(8,128)}), f32[32,8,128]{2,1,0:T(8,128)S(1)}, u32[]{:S(2)}, u32[]{:S(2)}) async-start(f32[32,8,128]{2,1,0:T(8,128)} %bitcast.4), calls=%async_computation | async-start | bytes 262144 | tf_op jit(solution)/shard_map/all_to_all | solution.py:325
  15.4 6.4 %collective-permute-start.7 = (f32[32,256]{1,0:T(8,128)S(1)}, f32[32,256]{1,0:T(8,128)S(1)}, u32[]{:S(2)}, u32[]{:S(2)}) collective-permute-start(f32[32,256]{1,0:T(8,128)S(1)} %get-tuple-element.29), channel_id=1, source_target_pairs={{0,4},{2,6},{4,0},{5,9},{6,2},{7,11},{8,12},{9,5},{10,14},{11,7},{... | collective-permute-start | bytes 98312 | tf_op jit(solution)/shard_map/ppermute | solution.py:340
  22.0 1.2 %collective-permute-start.8 = (f32[32,256]{1,0:T(8,128)S(1)}, f32[32,256]{1,0:T(8,128)S(1)}, u32[]{:S(2)}, u32[]{:S(2)}) collective-permute-start(f32[32,256]{1,0:T(8,128)S(1)} %get-tuple-element.33), channel_id=1, source_target_pairs={{0,1},{1,0},{2,3},{3,2},{4,5},{5,4},{6,7},{7,6},{8,9},{9,8},{10,11... | collective-permute-start | bytes 98312 | tf_op jit(solution)/shard_map/ppermute | solution.py:374
  22.6 1.3 %collective-permute-start.3 = (f32[4,8,128]{2,1,0:T(8,128)S(1)}, f32[4,8,128]{2,1,0:T(8,128)S(1)}, u32[]{:S(2)}, u32[]{:S(2)}) collective-permute-start(f32[4,8,128]{2,1,0:T(8,128)S(1)} %reduce.1.mine_ref), channel_id=1, source_target_pairs={{0,1},{1,0},{2,3},{3,2},{4,5},{5,4},{6,7},{7,6},{8,9},{9,8},{10,11... | collective-permute-start | bytes 49160 | tf_op jit(solution)/shard_map/ppermute | solution.py:394

commit v14 on v10

--- a/solution.py
+++ b/solution.py
@@ -254,7 +254,7 @@
     width = coarse_len // shards
     packed_rows = -(-(rows * tiles + tiles) // 8) * 8
     lead = (subs // 2 + 1) % subs
-    sub_order = [(lead + k) % subs for k in range(subs)]
+    sub_order = [(lead - k) % subs for k in range(subs)]
     blk_order = [b ^ 2 for b in range(shards)]
     core_swap = [(b, b ^ 1) for b in range(shards)]
     far_swap = [(b, b ^ 2) for b in range(shards)]

time: 25.1 us -> 25.3 us (level)
  waiting for transfers between devices: 1.5 us -> 1.83 us
    all_to_all x1, waiting for transfers between devices: 0.62 us -> 0.95 us  [on_device(): lax.all_to_all(flat, ('sub', 'blk'), 0, 0, axis_index_groups=[members], t...]
  transfers between devices with their start and end apart: 10 -> 10, of which waited for: 4 -> 3; matrix products, arithmetic and copies ran while one was open for 0% -> 0% of each run, Pallas kernels for 22% -> 22%
where the time goes in v14:
time: 25.3 us; the launch traced here: 25.1 us
  starting transfers between devices  16.4 us (65%)
  Pallas kernels  6.71 us (27%)
  waiting for transfers between devices  1.83 us (7%)
    all_to_all x1, starting transfers between devices, on_device(): lax.all_to_all(flat, ('sub', 'blk'), 0, 0, axis_index_groups=[members], t...  3.97 us
    ppermute x1, starting transfers between devices, on_device(): halo = lax.ppermute(outgoing, ('sub', 'blk'), neighbours)  3.69 us
    ppermute x1, starting transfers between devices, on_device(): lists = lax.ppermute(lists, ('sub', 'blk'), neighbours)  3.39 us
    ppermute x1, starting transfers between devices, on_device(): far_rhs = lax.ppermute(rhs, 'blk', far_swap)  2.83 us
    pallas_call x1, Pallas kernels, on_device(): pl.pallas_call(functools.partial(own_kernel, margin), out_shape=(jax.Shap...  2.67 us
    ppermute x1, starting transfers between devices, on_device(): over_y = lax.ppermute(packed, 'blk', far_swap)  1.61 us
    pallas_call x1, Pallas kernels, on_device(): pl.pallas_call(pack_kernel, out_shape=(jax.ShapeDtypeStruct(packed_shape,...  1.17 us
    all_to_all x1, waiting for transfers between devices, on_device(): lax.all_to_all(flat, ('sub', 'blk'), 0, 0, axis_index_groups=[members], t...  0.95 us
  transfers between devices with their start and end apart: 10, of which 3 were waited for; matrix products, arithmetic and copies ran while one was open for 0% of the time, Pallas kernels for 22%

profile of v14, /device:TPU:0, one launch (start us, length us, event | category | flops | bytes accessed | tf_op | source)
XLA Modules:
  0.0 25.1 jit_solution(14121949389454335633)
XLA Ops:
  0.0 0.5 %collective-permute-start.1 = (s32[512]{0:T(512)}, s32[512]{0:T(512)S(1)}, u32[]{:S(2)}, u32[]{:S(2)}) collective-permute-start(s32[512]{0:T(512)} %param.11), channel_id=1, source_target_pairs={{0,1},{1,0},{2,3},{3,2},{4,5},{5,4},{6,7},{7,6},{8,9},{9,8},{10,11... | collective-permute-start | bytes 6152 | tf_op jit(solution)/shard_map/ppermute | solution.py:295
  0.5 0.1 collective-permute-start
  0.5 1.2 %pack.1 = (f32[136,128]{1,0:T(8,128)S(1)}, s32[2,256]{1,0:T(2,128)S(1)}, f32[1024,128]{1,0:T(8,128)S(1)}) custom-call(f32[32,512]{1,0:T(8,128)} %residual_ref.1, s32[1,512]{1,0:T(1,128)} %bitcast.10, s32[2,256]{1,0:T(2,128)} %bitcast.9, s32[1,2]{1,0:T(1,128)} %counts_ref.1, f32[1024,128]{1,0:T(8,128)} %bitcast.8), custom_call_target="tpu_custom_call" | custom-call | flops 8000000000 | tf_op jit(solution)/shard_map/pack/pallas_call | solution.py:273
  1.7 0.0 collective-permute-done.1
  1.7 0.2 collective-permute-done.core_ref
  1.9 0.3 %near.1 = (f32[32,256]{1,0:T(8,128)S(1)}, bf16[256,512]{1,0:T(8,128)(2,1)S(1)}, bf16[256,512]{1,0:T(8,128)(2,1)S(1)}) custom-call(f32[136,128]{1,0:T(8,128)S(1)} %get-tuple-element.21.packed_ref, f32[32,512]{1,0:T(8,128)S(1)} %collective-permute-done.core_ref, s32[1,512]{1,0:T(1,128)S(1)} %bitcast.7, f32[1024,128]{1,0:T(8,128)S(1)} %get-tuple-element.22.coarse_ref), custom_call_target="tpu_custom_call" | custom-call | flops 2000000000 | tf_op jit(solution)/shard_map/near/pallas_call | solution.py:297
  2.3 2.8 %collective-permute-start.2 = (f32[32,256]{1,0:T(8,128)S(1)}, f32[32,256]{1,0:T(8,128)S(1)}, u32[]{:S(2)}, u32[]{:S(2)}) collective-permute-start(f32[32,256]{1,0:T(8,128)S(1)} %get-tuple-element.23.rhs_ref), channel_id=1, source_target_pairs={{0,2},{1,3},{2,0},{3,1},{4,6},{5,7},{6,4},{7,5},{8,10},{9,11},{10,... | collective-permute-start | bytes 98312 | tf_op jit(solution)/shard_map/ppermute | solution.py:310
  5.1 0.0 collective-permute-start.5
  5.1 1.6 %collective-permute-start.4 = (f32[136,128]{1,0:T(8,128)S(1)}, f32[136,128]{1,0:T(8,128)S(1)}, u32[]{:S(2)}, u32[]{:S(2)}) collective-permute-start(f32[136,128]{1,0:T(8,128)S(1)} %get-tuple-element.21.packed_ref), channel_id=1, source_target_pairs={{0,2},{1,3},{2,0},{3,1},{4,6},{5,7},{6,4},{7,5},{8,10},{9,11},{10,... | collective-permute-start | bytes 208904 | tf_op jit(solution)/shard_map/ppermute | solution.py:311
  6.7 3.4 %collective-permute-start.6 = (s32[2,256]{1,0:T(2,128)S(1)}, s32[2,256]{1,0:T(2,128)S(1)}, u32[]{:S(2)}, u32[]{:S(2)}) collective-permute-start(s32[2,256]{1,0:T(2,128)S(1)} %get-tuple-element.28), channel_id=1, source_target_pairs={{0,4},{2,6},{4,0},{5,9},{6,2},{7,11},{8,12},{9,5},{10,14},{11,7},{... | collective-permute-start | bytes 6152 | tf_op jit(solution)/shard_map/ppermute | solution.py:293
  10.1 0.0 collective-permute-done.2.far_ref
  10.1 0.9 %coarse.1 = (f32[8,4,8,128]{3,2,1,0:T(8,128)}, bf16[2,96,512]{2,1,0:T(8,128)(2,1)S(1)}) custom-call(f32[136,128]{1,0:T(8,128)S(1)} %get-tuple-element.21.packed_ref, f32[32,512]{1,0:T(8,128)S(1)} %collective-permute-done.core_ref, f32[32,256]{1,0:T(8,128)S(1)} %get-tuple-element.23.rhs_ref, f32[32,256]{1,0:T(8,128)S(1)} %collective-permute-done.2.far_ref, ...), custom_call_target="tpu_custom_call" | custom-call | flops 8000000000 | tf_op jit(solution)/shard_map/coarse/pallas_call | solution.py:313
  11.1 4.0 %all-to-all-start = ((f32[32,8,128]{2,1,0:T(8,128)}), f32[32,8,128]{2,1,0:T(8,128)S(1)}, u32[]{:S(2)}, u32[]{:S(2)}) async-start(f32[32,8,128]{2,1,0:T(8,128)} %bitcast.4), calls=%async_computation | async-start | bytes 262144 | tf_op jit(solution)/shard_map/all_to_all | solution.py:327
  15.0 0.0 collective-permute-done.6.lists_ref
  15.1 0.0 collective-permute-done.5.both_ref
  15.1 0.0 collective-permute-done.4.y_ref
  15.1 0.3 %margins.1 = (f32[32,256]{1,0:T(8,128)S(1)}, bf16[2,96,512]{2,1,0:T(8,128)(2,1)S(1)}) custom-call(bf16[2,96,512]{2,1,0:T(8,128)(2,1)S(1)} %get-tuple-element.27.near_ref, f32[136,128]{1,0:T(8,128)S(1)} %collective-permute-done.4.y_ref, f32[136,128]{1,0:T(8,128)S(1)} %collective-permute-done.5.both_ref, s32[2,256]{1,0:T(2,128)S(1)} %collective-permute-done.6.lists_ref), custom_call_target="tpu_custom_call" | custom-call | flops 4000000000 | tf_op jit(solution)/shard_map/margins/pallas_call | solution.py:330
  15.4 3.7 %collective-permute-start.7 = (f32[32,256]{1,0:T(8,128)S(1)}, f32[32,256]{1,0:T(8,128)S(1)}, u32[]{:S(2)}, u32[]{:S(2)}) collective-permute-start(f32[32,256]{1,0:T(8,128)S(1)} %get-tuple-element.31), channel_id=1, source_target_pairs={{0,4},{2,6},{4,0},{5,9},{6,2},{7,11},{8,12},{9,5},{10,14},{11,7},{... | collective-permute-start | bytes 98312 | tf_op jit(solution)/shard_map/ppermute | solution.py:342
  19.1 2.7 %owned.1 = (f32[32,512]{1,0:T(8,128)S(1)}, bf16[2,256,512]{2,1,0:T(8,128)(2,1)S(1)}, bf16[2,256,512]{2,1,0:T(8,128)(2,1)S(1)}, bf16[256,512]{1,0:T(8,128)(2,1)S(1)}) custom-call(bf16[2,96,512]{2,1,0:T(8,128)(2,1)S(1)} %get-tuple-element.27.near_ref, bf16[2,96,512]{2,1,0:T(8,128)(2,1)S(1)} %get-tuple-element.29.far_ref, s32[1,512]{1,0:T(1,128)} %bitcast.11, ...), custom_call_target="tpu_custom_call" | custom-call | flops 40000000000 | tf_op jit(solution)/shard_map/owned/pallas_call | solution.py:344
  21.8 0.0 collective-permute-done.7.halo_ref
  21.8 0.2 mine.1
  22.0 0.0 collective-permute-start.8
  22.0 0.9 %all-to-all-done = f32[32,8,128]{2,1,0:T(8,128)S(1)} async-done(((f32[32,8,128]{2,1,0:T(8,128)}), f32[32,8,128]{2,1,0:T(8,128)S(1)}, u32[]{:S(2)}, u32[]{:S(2)}) %all-to-all-start) | async-done | bytes 131104 | tf_op jit(solution)/shard_map/all_to_all | solution.py:327
  23.0 0.4 %collective-permute-start.3 = (f32[4,8,128]{2,1,0:T(8,128)S(1)}, f32[4,8,128]{2,1,0:T(8,128)S(1)}, u32[]{:S(2)}, u32[]{:S(2)}) collective-permute-start(f32[4,8,128]{2,1,0:T(8,128)S(1)} %reduce.1.mine_ref), channel_id=1, source_target_pairs={{0,1},{1,0},{2,3},{3,2},{4,5},{5,4},{6,7},{7,6},{8,9},{9,8},{10,11... | collective-permute-start | bytes 49160 | tf_op jit(solution)/shard_map/ppermute | solution.py:396
  23.4 0.0 collective-permute-done.8.halo_ref
  23.4 0.2 other.1.total_ref
  23.6 0.6 %collective-permute-done.3.other_ref = f32[4,8,128]{2,1,0:T(8,128)S(1)} collective-permute-done((f32[4,8,128]{2,1,0:T(8,128)S(1)}, f32[4,8,128]{2,1,0:T(8,128)S(1)}, u32[]{:S(2)}, u32[]{:S(2)}) %collective-permute-start.3) | collective-permute-done | bytes 16416 | tf_op jit(solution)/shard_map/ppermute | solution.py:396
  24.2 0.9 %tail.1 = f32[32,512]{1,0:T(8,128)} custom-call(f32[4,8,128]{2,1,0:T(8,128)S(1)} %reduce.1.mine_ref, f32[4,8,128]{2,1,0:T(8,128)S(1)} %collective-permute-done.3.other_ref, bf16[256,512]{1,0:T(8,128)(2,1)S(1)} %get-tuple-element.30.hot_ref, f32[32,512]{1,0:T(8,128)S(1)} %other.1.total_ref), custom_call_target="tpu_custom_call" | custom-call | tf_op jit(solution)/shard_map/tail/pallas_call | solution.py:398
  (1 shorter events, 0.0 us)
Async XLA Ops:
  0.0 1.7 %collective-permute-start.1 = (s32[512]{0:T(512)}, s32[512]{0:T(512)S(1)}, u32[]{:S(2)}, u32[]{:S(2)}) collective-permute-start(s32[512]{0:T(512)} %param.11), channel_id=1, source_target_pairs={{0,1},{1,0},{2,3},{3,2},{4,5},{5,4},{6,7},{7,6},{8,9},{9,8},{10,11... | collective-permute-start | bytes 6152 | tf_op jit(solution)/shard_map/ppermute | solution.py:295
  0.5 1.5 %collective-permute-start = (f32[32,512]{1,0:T(8,128)}, f32[32,512]{1,0:T(8,128)S(1)}, u32[]{:S(2)}, u32[]{:S(2)}) collective-permute-start(f32[32,512]{1,0:T(8,128)} %residual_ref.1), channel_id=1, source_target_pairs={{0,1},{1,0},{2,3},{3,2},{4,5},{5,4},{6,7},{7,6},{8,9},{9,8},{10,11... | collective-permute-start | bytes 196616 | tf_op jit(solution)/shard_map/ppermute | solution.py:294
  2.3 7.8 %collective-permute-start.2 = (f32[32,256]{1,0:T(8,128)S(1)}, f32[32,256]{1,0:T(8,128)S(1)}, u32[]{:S(2)}, u32[]{:S(2)}) collective-permute-start(f32[32,256]{1,0:T(8,128)S(1)} %get-tuple-element.23.rhs_ref), channel_id=1, source_target_pairs={{0,2},{1,3},{2,0},{3,1},{4,6},{5,7},{6,4},{7,5},{8,10},{9,11},{10,... | collective-permute-start | bytes 98312 | tf_op jit(solution)/shard_map/ppermute | solution.py:310
  5.1 10.0 %collective-permute-start.5 = (f32[136,128]{1,0:T(8,128)S(1)}, f32[136,128]{1,0:T(8,128)S(1)}, u32[]{:S(2)}, u32[]{:S(2)}) collective-permute-start(f32[136,128]{1,0:T(8,128)S(1)} %get-tuple-element.21.packed_ref), channel_id=1, source_target_pairs={{0,3},{1,2},{2,1},{3,0},{4,7},{5,6},{6,5},{7,4},{8,11},{9,10},{10,... | collective-permute-start | bytes 208904 | tf_op jit(solution)/shard_map/ppermute | solution.py:312
  5.1 10.0 %collective-permute-start.4 = (f32[136,128]{1,0:T(8,128)S(1)}, f32[136,128]{1,0:T(8,128)S(1)}, u32[]{:S(2)}, u32[]{:S(2)}) collective-permute-start(f32[136,128]{1,0:T(8,128)S(1)} %get-tuple-element.21.packed_ref), channel_id=1, source_target_pairs={{0,2},{1,3},{2,0},{3,1},{4,6},{5,7},{6,4},{7,5},{8,10},{9,11},{10,... | collective-permute-start | bytes 208904 | tf_op jit(solution)/shard_map/ppermute | solution.py:311
  6.7 8.3 %collective-permute-start.6 = (s32[2,256]{1,0:T(2,128)S(1)}, s32[2,256]{1,0:T(2,128)S(1)}, u32[]{:S(2)}, u32[]{:S(2)}) collective-permute-start(s32[2,256]{1,0:T(2,128)S(1)} %get-tuple-element.28), channel_id=1, source_target_pairs={{0,4},{2,6},{4,0},{5,9},{6,2},{7,11},{8,12},{9,5},{10,14},{11,7},{... | collective-permute-start | bytes 6152 | tf_op jit(solution)/shard_map/ppermute | solution.py:293
  11.1 11.9 %all-to-all-start = ((f32[32,8,128]{2,1,0:T(8,128)}), f32[32,8,128]{2,1,0:T(8,128)S(1)}, u32[]{:S(2)}, u32[]{:S(2)}) async-start(f32[32,8,128]{2,1,0:T(8,128)} %bitcast.4), calls=%async_computation | async-start | bytes 262144 | tf_op jit(solution)/shard_map/all_to_all | solution.py:327
  15.4 6.4 %collective-permute-start.7 = (f32[32,256]{1,0:T(8,128)S(1)}, f32[32,256]{1,0:T(8,128)S(1)}, u32[]{:S(2)}, u32[]{:S(2)}) collective-permute-start(f32[32,256]{1,0:T(8,128)S(1)} %get-tuple-element.31), channel_id=1, source_target_pairs={{0,4},{2,6},{4,0},{5,9},{6,2},{7,11},{8,12},{9,5},{10,14},{11,7},{... | collective-permute-start | bytes 98312 | tf_op jit(solution)/shard_map/ppermute | solution.py:342
  22.0 1.4 %collective-permute-start.8 = (f32[32,256]{1,0:T(8,128)S(1)}, f32[32,256]{1,0:T(8,128)S(1)}, u32[]{:S(2)}, u32[]{:S(2)}) collective-permute-start(f32[32,256]{1,0:T(8,128)S(1)} %get-tuple-element.35), channel_id=1, source_target_pairs={{0,1},{1,0},{2,3},{3,2},{4,5},{5,4},{6,7},{7,6},{8,9},{9,8},{10,11... | collective-permute-start | bytes 98312 | tf_op jit(solution)/shard_map/ppermute | solution.py:376
  23.0 1.3 %collective-permute-start.3 = (f32[4,8,128]{2,1,0:T(8,128)S(1)}, f32[4,8,128]{2,1,0:T(8,128)S(1)}, u32[]{:S(2)}, u32[]{:S(2)}) collective-permute-start(f32[4,8,128]{2,1,0:T(8,128)S(1)} %reduce.1.mine_ref), channel_id=1, source_target_pairs={{0,1},{1,0},{2,3},{3,2},{4,5},{5,4},{6,7},{7,6},{8,9},{9,8},{10,11... | collective-permute-start | bytes 49160 | tf_op jit(solution)/shard_map/ppermute | solution.py:396

commit v15 on v10

--- a/solution.py
+++ b/solution.py
@@ -255,7 +255,7 @@
     packed_rows = -(-(rows * tiles + tiles) // 8) * 8
     lead = (subs // 2 + 1) % subs
     sub_order = [(lead + k) % subs for k in range(subs)]
-    blk_order = [b ^ 2 for b in range(shards)]
+    blk_order = [b ^ 3 for b in range(shards)]
     core_swap = [(b, b ^ 1) for b in range(shards)]
     far_swap = [(b, b ^ 2) for b in range(shards)]
     both_swap = [(b, b ^ 3) for b in range(shards)]

time: 25.1 us -> 25.2 us (level)
  transfers between devices with their start and end apart: 10 -> 10, of which waited for: 4 -> 3; matrix products, arithmetic and copies ran while one was open for 0% -> 0% of each run, Pallas kernels for 22% -> 22%
where the time goes in v15:
time: 25.2 us; the launch traced here: 25 us
  starting transfers between devices  16.7 us (66%)
  Pallas kernels  6.71 us (27%)
  waiting for transfers between devices  1.46 us (6%)
    all_to_all x1, starting transfers between devices, on_device(): lax.all_to_all(flat, ('sub', 'blk'), 0, 0, axis_index_groups=[members], t...  3.97 us
    ppermute x1, starting transfers between devices, on_device(): halo = lax.ppermute(outgoing, ('sub', 'blk'), neighbours)  3.69 us
    ppermute x1, starting transfers between devices, on_device(): lists = lax.ppermute(lists, ('sub', 'blk'), neighbours)  3.39 us
    ppermute x1, starting transfers between devices, on_device(): far_rhs = lax.ppermute(rhs, 'blk', far_swap)  2.83 us
    pallas_call x1, Pallas kernels, on_device(): pl.pallas_call(functools.partial(own_kernel, margin), out_shape=(jax.Shap...  2.67 us
    ppermute x1, starting transfers between devices, on_device(): over_y = lax.ppermute(packed, 'blk', far_swap)  1.61 us
    pallas_call x1, Pallas kernels, on_device(): pl.pallas_call(pack_kernel, out_shape=(jax.ShapeDtypeStruct(packed_shape,...  1.17 us
    pallas_call x1, Pallas kernels, on_device(): pl.pallas_call(functools.partial(coarse_kernel, width, rows, tiles, sub_o...  0.94 us
  transfers between devices with their start and end apart: 10, of which 3 were waited for; matrix products, arithmetic and copies ran while one was open for 0% of the time, Pallas kernels for 22%

profile of v15, /device:TPU:0, one launch (start us, length us, event | category | flops | bytes accessed | tf_op | source)
XLA Modules:
  0.0 25.0 jit_solution(10553612476624033960)
XLA Ops:
  0.0 0.5 %collective-permute-start.1 = (s32[512]{0:T(512)}, s32[512]{0:T(512)S(1)}, u32[]{:S(2)}, u32[]{:S(2)}) collective-permute-start(s32[512]{0:T(512)} %param.11), channel_id=1, source_target_pairs={{0,1},{1,0},{2,3},{3,2},{4,5},{5,4},{6,7},{7,6},{8,9},{9,8},{10,11... | collective-permute-start | bytes 6152 | tf_op jit(solution)/shard_map/ppermute | solution.py:295
  0.5 0.1 collective-permute-start
  0.5 1.2 %pack.1 = (f32[136,128]{1,0:T(8,128)S(1)}, s32[2,256]{1,0:T(2,128)S(1)}, f32[1024,128]{1,0:T(8,128)S(1)}) custom-call(f32[32,512]{1,0:T(8,128)} %residual_ref.1, s32[1,512]{1,0:T(1,128)} %bitcast.10, s32[2,256]{1,0:T(2,128)} %bitcast.9, s32[1,2]{1,0:T(1,128)} %counts_ref.1, f32[1024,128]{1,0:T(8,128)} %bitcast.8), custom_call_target="tpu_custom_call" | custom-call | flops 8000000000 | tf_op jit(solution)/shard_map/pack/pallas_call | solution.py:273
  1.7 0.0 collective-permute-done.1
  1.7 0.2 collective-permute-done.core_ref
  1.9 0.3 %near.1 = (f32[32,256]{1,0:T(8,128)S(1)}, bf16[256,512]{1,0:T(8,128)(2,1)S(1)}, bf16[256,512]{1,0:T(8,128)(2,1)S(1)}) custom-call(f32[136,128]{1,0:T(8,128)S(1)} %get-tuple-element.21.packed_ref, f32[32,512]{1,0:T(8,128)S(1)} %collective-permute-done.core_ref, s32[1,512]{1,0:T(1,128)S(1)} %bitcast.7, f32[1024,128]{1,0:T(8,128)S(1)} %get-tuple-element.22.coarse_ref), custom_call_target="tpu_custom_call" | custom-call | flops 2000000000 | tf_op jit(solution)/shard_map/near/pallas_call | solution.py:297
  2.3 2.8 %collective-permute-start.2 = (f32[32,256]{1,0:T(8,128)S(1)}, f32[32,256]{1,0:T(8,128)S(1)}, u32[]{:S(2)}, u32[]{:S(2)}) collective-permute-start(f32[32,256]{1,0:T(8,128)S(1)} %get-tuple-element.23.rhs_ref), channel_id=1, source_target_pairs={{0,2},{1,3},{2,0},{3,1},{4,6},{5,7},{6,4},{7,5},{8,10},{9,11},{10,... | collective-permute-start | bytes 98312 | tf_op jit(solution)/shard_map/ppermute | solution.py:310
  5.1 0.0 collective-permute-start.5
  5.1 1.6 %collective-permute-start.4 = (f32[136,128]{1,0:T(8,128)S(1)}, f32[136,128]{1,0:T(8,128)S(1)}, u32[]{:S(2)}, u32[]{:S(2)}) collective-permute-start(f32[136,128]{1,0:T(8,128)S(1)} %get-tuple-element.21.packed_ref), channel_id=1, source_target_pairs={{0,2},{1,3},{2,0},{3,1},{4,6},{5,7},{6,4},{7,5},{8,10},{9,11},{10,... | collective-permute-start | bytes 208904 | tf_op jit(solution)/shard_map/ppermute | solution.py:311
  6.7 3.4 %collective-permute-start.6 = (s32[2,256]{1,0:T(2,128)S(1)}, s32[2,256]{1,0:T(2,128)S(1)}, u32[]{:S(2)}, u32[]{:S(2)}) collective-permute-start(s32[2,256]{1,0:T(2,128)S(1)} %get-tuple-element.28), channel_id=1, source_target_pairs={{0,4},{2,6},{4,0},{5,9},{6,2},{7,11},{8,12},{9,5},{10,14},{11,7},{... | collective-permute-start | bytes 6152 | tf_op jit(solution)/shard_map/ppermute | solution.py:293
  10.1 0.0 collective-permute-done.2.far_ref
  10.1 0.9 %coarse.1 = (f32[8,4,8,128]{3,2,1,0:T(8,128)}, bf16[2,96,512]{2,1,0:T(8,128)(2,1)S(1)}) custom-call(f32[136,128]{1,0:T(8,128)S(1)} %get-tuple-element.21.packed_ref, f32[32,512]{1,0:T(8,128)S(1)} %collective-permute-done.core_ref, f32[32,256]{1,0:T(8,128)S(1)} %get-tuple-element.23.rhs_ref, f32[32,256]{1,0:T(8,128)S(1)} %collective-permute-done.2.far_ref, ...), custom_call_target="tpu_custom_call" | custom-call | flops 8000000000 | tf_op jit(solution)/shard_map/coarse/pallas_call | solution.py:313
  11.1 4.0 %all-to-all-start = ((f32[32,8,128]{2,1,0:T(8,128)}), f32[32,8,128]{2,1,0:T(8,128)S(1)}, u32[]{:S(2)}, u32[]{:S(2)}) async-start(f32[32,8,128]{2,1,0:T(8,128)} %bitcast.4), calls=%async_computation | async-start | bytes 262144 | tf_op jit(solution)/shard_map/all_to_all | solution.py:327
  15.0 0.0 collective-permute-done.6.lists_ref
  15.1 0.0 collective-permute-done.5.both_ref
  15.1 0.0 collective-permute-done.4.y_ref
  15.1 0.3 %margins.1 = (f32[32,256]{1,0:T(8,128)S(1)}, bf16[2,96,512]{2,1,0:T(8,128)(2,1)S(1)}) custom-call(bf16[2,96,512]{2,1,0:T(8,128)(2,1)S(1)} %get-tuple-element.27.near_ref, f32[136,128]{1,0:T(8,128)S(1)} %collective-permute-done.4.y_ref, f32[136,128]{1,0:T(8,128)S(1)} %collective-permute-done.5.both_ref, s32[2,256]{1,0:T(2,128)S(1)} %collective-permute-done.6.lists_ref), custom_call_target="tpu_custom_call" | custom-call | flops 4000000000 | tf_op jit(solution)/shard_map/margins/pallas_call | solution.py:330
  15.4 3.7 %collective-permute-start.7 = (f32[32,256]{1,0:T(8,128)S(1)}, f32[32,256]{1,0:T(8,128)S(1)}, u32[]{:S(2)}, u32[]{:S(2)}) collective-permute-start(f32[32,256]{1,0:T(8,128)S(1)} %get-tuple-element.31), channel_id=1, source_target_pairs={{0,4},{2,6},{4,0},{5,9},{6,2},{7,11},{8,12},{9,5},{10,14},{11,7},{... | collective-permute-start | bytes 98312 | tf_op jit(solution)/shard_map/ppermute | solution.py:342
  19.1 2.7 %owned.1 = (f32[32,512]{1,0:T(8,128)S(1)}, bf16[2,256,512]{2,1,0:T(8,128)(2,1)S(1)}, bf16[2,256,512]{2,1,0:T(8,128)(2,1)S(1)}, bf16[256,512]{1,0:T(8,128)(2,1)S(1)}) custom-call(bf16[2,96,512]{2,1,0:T(8,128)(2,1)S(1)} %get-tuple-element.27.near_ref, bf16[2,96,512]{2,1,0:T(8,128)(2,1)S(1)} %get-tuple-element.29.far_ref, s32[1,512]{1,0:T(1,128)} %bitcast.11, ...), custom_call_target="tpu_custom_call" | custom-call | flops 40000000000 | tf_op jit(solution)/shard_map/owned/pallas_call | solution.py:344
  21.8 0.0 collective-permute-done.7.halo_ref
  21.8 0.2 mine.1
  22.0 0.0 collective-permute-start.8
  22.0 0.6 %all-to-all-done = f32[32,8,128]{2,1,0:T(8,128)S(1)} async-done(((f32[32,8,128]{2,1,0:T(8,128)}), f32[32,8,128]{2,1,0:T(8,128)S(1)}, u32[]{:S(2)}, u32[]{:S(2)}) %all-to-all-start) | async-done | bytes 131104 | tf_op jit(solution)/shard_map/all_to_all | solution.py:327
  22.6 0.7 %collective-permute-start.3 = (f32[4,8,128]{2,1,0:T(8,128)S(1)}, f32[4,8,128]{2,1,0:T(8,128)S(1)}, u32[]{:S(2)}, u32[]{:S(2)}) collective-permute-start(f32[4,8,128]{2,1,0:T(8,128)S(1)} %reduce.1.mine_ref), channel_id=1, source_target_pairs={{0,1},{1,0},{2,3},{3,2},{4,5},{5,4},{6,7},{7,6},{8,9},{9,8},{10,11... | collective-permute-start | bytes 49160 | tf_op jit(solution)/shard_map/ppermute | solution.py:396
  23.3 0.0 collective-permute-done.8.halo_ref
  23.3 0.2 other.1.total_ref
  23.5 0.6 %collective-permute-done.3.other_ref = f32[4,8,128]{2,1,0:T(8,128)S(1)} collective-permute-done((f32[4,8,128]{2,1,0:T(8,128)S(1)}, f32[4,8,128]{2,1,0:T(8,128)S(1)}, u32[]{:S(2)}, u32[]{:S(2)}) %collective-permute-start.3) | collective-permute-done | bytes 16416 | tf_op jit(solution)/shard_map/ppermute | solution.py:396
  24.1 0.9 %tail.1 = f32[32,512]{1,0:T(8,128)} custom-call(f32[4,8,128]{2,1,0:T(8,128)S(1)} %reduce.1.mine_ref, f32[4,8,128]{2,1,0:T(8,128)S(1)} %collective-permute-done.3.other_ref, bf16[256,512]{1,0:T(8,128)(2,1)S(1)} %get-tuple-element.30.hot_ref, f32[32,512]{1,0:T(8,128)S(1)} %other.1.total_ref), custom_call_target="tpu_custom_call" | custom-call | tf_op jit(solution)/shard_map/tail/pallas_call | solution.py:398
  (1 shorter events, 0.0 us)
Async XLA Ops:
  0.0 1.7 %collective-permute-start.1 = (s32[512]{0:T(512)}, s32[512]{0:T(512)S(1)}, u32[]{:S(2)}, u32[]{:S(2)}) collective-permute-start(s32[512]{0:T(512)} %param.11), channel_id=1, source_target_pairs={{0,1},{1,0},{2,3},{3,2},{4,5},{5,4},{6,7},{7,6},{8,9},{9,8},{10,11... | collective-permute-start | bytes 6152 | tf_op jit(solution)/shard_map/ppermute | solution.py:295
  0.5 1.5 %collective-permute-start = (f32[32,512]{1,0:T(8,128)}, f32[32,512]{1,0:T(8,128)S(1)}, u32[]{:S(2)}, u32[]{:S(2)}) collective-permute-start(f32[32,512]{1,0:T(8,128)} %residual_ref.1), channel_id=1, source_target_pairs={{0,1},{1,0},{2,3},{3,2},{4,5},{5,4},{6,7},{7,6},{8,9},{9,8},{10,11... | collective-permute-start | bytes 196616 | tf_op jit(solution)/shard_map/ppermute | solution.py:294
  2.3 7.8 %collective-permute-start.2 = (f32[32,256]{1,0:T(8,128)S(1)}, f32[32,256]{1,0:T(8,128)S(1)}, u32[]{:S(2)}, u32[]{:S(2)}) collective-permute-start(f32[32,256]{1,0:T(8,128)S(1)} %get-tuple-element.23.rhs_ref), channel_id=1, source_target_pairs={{0,2},{1,3},{2,0},{3,1},{4,6},{5,7},{6,4},{7,5},{8,10},{9,11},{10,... | collective-permute-start | bytes 98312 | tf_op jit(solution)/shard_map/ppermute | solution.py:310
  5.1 10.0 %collective-permute-start.5 = (f32[136,128]{1,0:T(8,128)S(1)}, f32[136,128]{1,0:T(8,128)S(1)}, u32[]{:S(2)}, u32[]{:S(2)}) collective-permute-start(f32[136,128]{1,0:T(8,128)S(1)} %get-tuple-element.21.packed_ref), channel_id=1, source_target_pairs={{0,3},{1,2},{2,1},{3,0},{4,7},{5,6},{6,5},{7,4},{8,11},{9,10},{10,... | collective-permute-start | bytes 208904 | tf_op jit(solution)/shard_map/ppermute | solution.py:312
  5.1 10.0 %collective-permute-start.4 = (f32[136,128]{1,0:T(8,128)S(1)}, f32[136,128]{1,0:T(8,128)S(1)}, u32[]{:S(2)}, u32[]{:S(2)}) collective-permute-start(f32[136,128]{1,0:T(8,128)S(1)} %get-tuple-element.21.packed_ref), channel_id=1, source_target_pairs={{0,2},{1,3},{2,0},{3,1},{4,6},{5,7},{6,4},{7,5},{8,10},{9,11},{10,... | collective-permute-start | bytes 208904 | tf_op jit(solution)/shard_map/ppermute | solution.py:311
  6.7 8.3 %collective-permute-start.6 = (s32[2,256]{1,0:T(2,128)S(1)}, s32[2,256]{1,0:T(2,128)S(1)}, u32[]{:S(2)}, u32[]{:S(2)}) collective-permute-start(s32[2,256]{1,0:T(2,128)S(1)} %get-tuple-element.28), channel_id=1, source_target_pairs={{0,4},{2,6},{4,0},{5,9},{6,2},{7,11},{8,12},{9,5},{10,14},{11,7},{... | collective-permute-start | bytes 6152 | tf_op jit(solution)/shard_map/ppermute | solution.py:293
  11.1 11.5 %all-to-all-start = ((f32[32,8,128]{2,1,0:T(8,128)}), f32[32,8,128]{2,1,0:T(8,128)S(1)}, u32[]{:S(2)}, u32[]{:S(2)}) async-start(f32[32,8,128]{2,1,0:T(8,128)} %bitcast.4), calls=%async_computation | async-start | bytes 262144 | tf_op jit(solution)/shard_map/all_to_all | solution.py:327
  15.4 6.4 %collective-permute-start.7 = (f32[32,256]{1,0:T(8,128)S(1)}, f32[32,256]{1,0:T(8,128)S(1)}, u32[]{:S(2)}, u32[]{:S(2)}) collective-permute-start(f32[32,256]{1,0:T(8,128)S(1)} %get-tuple-element.31), channel_id=1, source_target_pairs={{0,4},{2,6},{4,0},{5,9},{6,2},{7,11},{8,12},{9,5},{10,14},{11,7},{... | collective-permute-start | bytes 98312 | tf_op jit(solution)/shard_map/ppermute | solution.py:342
  22.0 1.3 %collective-permute-start.8 = (f32[32,256]{1,0:T(8,128)S(1)}, f32[32,256]{1,0:T(8,128)S(1)}, u32[]{:S(2)}, u32[]{:S(2)}) collective-permute-start(f32[32,256]{1,0:T(8,128)S(1)} %get-tuple-element.35), channel_id=1, source_target_pairs={{0,1},{1,0},{2,3},{3,2},{4,5},{5,4},{6,7},{7,6},{8,9},{9,8},{10,11... | collective-permute-start | bytes 98312 | tf_op jit(solution)/shard_map/ppermute | solution.py:376
  22.6 1.5 %collective-permute-start.3 = (f32[4,8,128]{2,1,0:T(8,128)S(1)}, f32[4,8,128]{2,1,0:T(8,128)S(1)}, u32[]{:S(2)}, u32[]{:S(2)}) collective-permute-start(f32[4,8,128]{2,1,0:T(8,128)S(1)} %reduce.1.mine_ref), channel_id=1, source_target_pairs={{0,1},{1,0},{2,3},{3,2},{4,5},{5,4},{6,7},{7,6},{8,9},{9,8},{10,11... | collective-permute-start | bytes 49160 | tf_op jit(solution)/shard_map/ppermute | solution.py:396
